TPU v7x, 256 devices: a whole 4x4x8 slice. The times are simulated.
256 devices in a mesh: fsdp: 32 (over z, x), tp: 8 (over y, core).
Axes of the slice: x: 4, y: 4, z: 8, core: 2. Of those that a mesh axis runs over, the one named last changes fastest.
Arguments:
- grads: bfloat16 [2, 16384, 3, 2048], P(None, 'fsdp', None, 'tp'), may hold values from -60 to 60
- accum: float32 [2, 16384, 3, 2048], P(None, 'fsdp', None, 'tp'), may hold values from 0.1 to 4
- roots: bfloat16 [2, 3, 2048, 2048], P(None, None, 'fsdp', 'tp'), may hold values from -3 to 3
Outputs:
- statistic: float32 [2, 3, 2048, 2048], P(None, None, 'fsdp', 'tp')
- step: float32 [2, 16384, 3, 2048], P(None, 'fsdp', None, 'tp')
All inputs are finite; a program needn't handle non-finite values.
Results may differ from a plain program's by a relative error of at most 0.00045.
Values may be sent and summed in bfloat16 or wider, within the bound.
No kernel may reach another device: no remote copies, remote signals or barrier semaphores. Data moves between devices by JAX's collectives and lax.ppermute only.
A program may use at most 128 MiB of HBM per device.

v0:
```python
import jax
import jax.numpy as jnp
from jax import lax
from jax.sharding import PartitionSpec as P

EPS = 1e-08


def on_device(grads, accum, roots):
    experts, local_rows, blocks, slab = grads.shape
    block_size = slab * lax.axis_size("tp")
    fsdp_count = lax.axis_size("fsdp")
    owned_rows = block_size // fsdp_count
    gradient = grads.astype(jnp.float32)
    adagrad = gradient / (jnp.sqrt(accum + gradient * gradient) + EPS)
    adagrad_sq = jnp.sum(adagrad * adagrad, axis=(1, 3))
    gathered = lax.all_gather(grads, "tp", axis=3, tiled=True)
    partial_value = jnp.einsum(
        "erjk,erjc->kejc", gathered, grads, preferred_element_type=jnp.float32
    )
    reduced = lax.psum_scatter(
        partial_value.reshape(owned_rows * lax.axis_size("fsdp"), experts * blocks * slab),
        "fsdp",
        scatter_dimension=0,
        tiled=True,
    )
    root_whole = lax.all_gather(roots, "fsdp", axis=2, tiled=True)
    direction = jnp.einsum(
        "erjk,ejkc->erjc", gathered, root_whole, preferred_element_type=jnp.float32
    )
    statistic = reduced.reshape(-1, experts, blocks, slab).transpose(1, 2, 0, 3) / (
        local_rows * fsdp_count
    )
    direction_sq = jnp.sum(direction * direction, axis=(1, 3))
    adagrad_total, direction_total = lax.psum((adagrad_sq, direction_sq), ("fsdp", "tp"))
    graft_scale = jnp.sqrt(adagrad_total) / jnp.sqrt(direction_total + 1e-06)
    step = direction * graft_scale[:, None, :, None]
    return (statistic, step)


def solution(mesh):
    placed = (P(None, "fsdp", None, "tp"), P(None, "fsdp", None, "tp"), P(None, None, "fsdp", "tp"))
    return jax.shard_map(
        on_device,
        mesh=mesh,
        in_specs=placed,
        out_specs=(P(None, None, "fsdp", "tp"), P(None, "fsdp", None, "tp")),
        check_vma=False,
    )
```

profile of v0, /device:TPU:32, one launch (start us, length us, event | category | flops | bytes accessed | tf_op | source)
XLA Modules:
  0.0 426.3 jit_solution(4376459949614296223)
XLA Ops:
  7.2 0.0 copy-start
  7.2 0.0 all-gather.3.cloned.1.call-start
  7.2 0.7 all-gather.3.cloned.1.call-update
  7.9 0.0 all-gather.5.cloned.1.call-start
  8.0 0.7 all-gather.5.cloned.1.call-update
  8.7 0.0 reduce-scatter.2.cloned.1.call-start
  8.7 78.4 %all-gather.3.cloned.1.call-done = bf16[2,512,3,2048]{3,1,2,0:T(8,128)(2,1)} async-done(((bf16[2,512,3,256]{3,1,2,0:T(8,128)(2,1)}), bf16[2,512,3,2048]{3,1,2,0:T(8,128)(2,1)}) %all-gather.3.cloned.1.call-update) | async-done | bytes 12582928 | tf_op jit(solution)/shard_map/all_gather | solution.py:17
  87.1 0.0 copy-done
  87.1 11.1 %fusion.5 = f32[2,3,256,2048]{3,2,1,0:T(8,128)} fusion(bf16[2,512,3,256]{3,1,2,0:T(8,128)(2,1)S(1)} %copy-done, bf16[2,512,3,2048]{3,1,2,0:T(8,128)(2,1)} %all-gather.3.cloned.1.call-done), kind=kOutput, calls=%fused_computation.11 | convolution fusion | flops 3221225472 | bytes 26738688 | tf_op jit(solution)/shard_map/erjk,erjc->kejc/dot_general | solution.py:18
  98.3 12.6 %copy.8 = f32[2048,1536]{1,0:T(8,128)} copy(f32[2048,1536]{0,1:T(8,128)} %bitcast.10) | data formatting | bytes 25165824 | tf_op jit(solution)/shard_map/reshape | solution.py:22
  110.9 0.0 reduce-scatter.2.cloned.1.call-update
  110.9 3.5 fusion.4
  114.5 64.3 %all-gather.5.cloned.1.call-done = bf16[2,3,2048,256]{3,2,1,0:T(8,128)(2,1)} async-done(((bf16[2,3,64,256]{3,2,1,0:T(8,128)(2,1)}), bf16[2,3,2048,256]{3,2,1,0:T(8,128)(2,1)}) %all-gather.5.cloned.1.call-update) | async-done | bytes 6291472 | tf_op jit(solution)/shard_map/all_gather | solution.py:27
  178.8 15.3 %multiply_reduce_fusion = (f32[2,3]{1,0:T(2,128)S(1)}, f32[2,3,256,512]{3,2,1,0:T(8,128)}) fusion(bf16[2,3,2048,256]{3,2,1,0:T(8,128)(2,1)} %all-gather.5.cloned.1.call-done, bf16[2,512,3,2048]{3,1,2,0:T(8,128)(2,1)} %all-gather.3.cloned.1.call-done), kind=kOutput, calls=%fused_computation.7 | convolution fusion | flops 3222798336 | bytes 22020120 | tf_op jit(solution)/shard_map/erjk,ejkc->erjc/dot_general | solution.py:28
  194.1 75.6 %all-reduce = (f32[2,3]{1,0:T(2,128)S(1)}, f32[2,3]{1,0:T(2,128)S(1)}) all-reduce(f32[2,3]{1,0:T(2,128)S(1)} %get-tuple-element.8, f32[2,3]{1,0:T(2,128)S(1)} %fusion.4), channel_id=1, replica_groups=mesh['fsdp'=32,'tp'=8] {'fsdp','tp'}, use_global_device_ids=true, to_apply=%region_4.0 | all-reduce | flops 12 | bytes 96 | tf_op jit(solution)/shard_map/psum | solution.py:35
  269.8 2.5 multiply_bitcast_fusion
  272.2 2.4 copy.10
  274.6 143.0 %reduce-scatter.2.cloned.1.call-done = f32[64,1536]{1,0:T(8,128)} async-done(((f32[2048,1536]{1,0:T(8,128)}), f32[64,1536]{1,0:T(8,128)}) %reduce-scatter.2.cloned.1.call-update) | async-done | bytes 393232 | tf_op jit(solution)/shard_map/reduce_scatter | solution.py:21
  417.6 1.0 broadcast_multiply_fusion
  418.6 0.3 div.18
  418.9 0.9 copy.9
  (1 shorter events, 0.0 us)
Async XLA Ops:
  7.2 80.0 %copy-start = (bf16[2,512,3,256]{3,1,2,0:T(8,128)(2,1)S(1)}, bf16[2,512,3,256]{3,1,2,0:T(8,128)(2,1)}, u32[]{:S(2)}) copy-start(bf16[2,512,3,256]{3,1,2,0:T(8,128)(2,1)} %param.3) | copy-start | bytes 4718596
  7.2 80.0 %all-gather.3.cloned.1.call-start = ((), (), s32[]{:S(2)}) async-start(), calls=%async_computation.1 | async-start | bytes 14155776 | tf_op jit(solution)/shard_map/all_gather | solution.py:17
  7.9 170.9 %all-gather.5.cloned.1.call-start = ((), (), s32[]{:S(2)}) async-start(), calls=%async_computation.3 | async-start | bytes 6488064 | tf_op jit(solution)/shard_map/all_gather | solution.py:27
  8.7 408.9 %reduce-scatter.2.cloned.1.call-start = ((), (), s32[]{:S(2)}) async-start(), calls=%async_computation.2 | async-start | bytes 12976128 | tf_op jit(solution)/shard_map/reduce_scatter | solution.py:21
Sparse Core Ops, SparseCore 0:
  9.8 77.2 all-gather.2
  89.7 89.0 all-gather.4
  183.0 234.5 reduce-scatter.1
where the time goes:
time: 428 us; the launch traced here: 426 us
  waiting for transfers between devices  287 us (67%)
  blocking collectives  75.6 us (18%)
  matrix products  26.5 us (6%)
  local copies, waits for them, and re-layouts  16.1 us (4%)
  between operations  13.8 us (3%)
  other arithmetic  7.02 us (2%)
    reduce_scatter x1, waiting for transfers between devices, on_device(): lax.psum_scatter(partial_value.reshape(owned_rows * lax.axis_size('fsdp')...  143 us
    all_gather x1, waiting for transfers between devices, on_device(): gathered = lax.all_gather(grads, 'tp', axis=3, tiled=True)  78.4 us
    psum x1, blocking collectives, on_device(): lax.psum((adagrad_sq, direction_sq), ('fsdp', 'tp'))  75.6 us
    all_gather x1, waiting for transfers between devices, on_device(): root_whole = lax.all_gather(roots, 'fsdp', axis=2, tiled=True)  64.3 us
    dot_general x1, matrix products, on_device(): jnp.einsum('erjk,ejkc->erjc', gathered, root_whole, preferred_element_typ...  15.3 us
    reshape x1, local copies, waits for them, and re-layouts, on_device(): partial_value.reshape(owned_rows * lax.axis_size('fsdp'), experts * block...  12.6 us
    dot_general x1, matrix products, on_device(): jnp.einsum('erjk,erjc->kejc', gathered, grads, preferred_element_type=jnp...  11.1 us
  transfers between devices with their start and end apart: 3, of which 3 were waited for; matrix products, arithmetic and copies ran while one was open for 11% of the time, Pallas kernels for 0%

commit v1 on v0

v1 whole, which is shorter than its diff:
```python
import functools
import jax
import jax.numpy as jnp
from jax import lax
from jax.experimental import pallas as pl
from jax.experimental.pallas import tpu as pltpu
from jax.sharding import PartitionSpec as P

EPS = 1e-08
NZ, NX, NY, NC = 8, 4, 4, 2
AXES = ("fsdp", "tp")
F32 = jnp.float32
F16 = jnp.float16
TAIL = 8
LARGEST = 14.0


def turn(c):
    return 1 - 2 * c


def device(z, x, y, c):
    return ((z * NX + x) * NY + y) * NC + c


EVERY = [(z, x, y, c) for z in range(NZ) for x in range(NX) for y in range(NY) for c in range(NC)]


def step_x(value, by):
    pairs = [(device(z, x, y, c), device(z, (x + by * turn(c)) % NX, y, c)) for z, x, y, c in EVERY]
    return lax.ppermute(value, AXES, pairs)


def step_y(value, by):
    pairs = [(y * NC + c, (y + by * turn(c)) % NY * NC + c) for y in range(NY) for c in range(NC)]
    return lax.ppermute(value, "tp", pairs)


def shift_x(value, by):
    pairs = [(z * NX + x, z * NX + (x + by) % NX) for z in range(NZ) for x in range(NX)]
    return lax.ppermute(value, "fsdp", pairs)


def swap_cores(value):
    return lax.ppermute(value, "tp", [(i, i ^ 1) for i in range(NY * NC)])


GROUPS_CZ = [
    [device(z, x, y, c) for c in range(NC) for z in range(NZ)] for x in range(NX) for y in range(NY)
]
GROUPS_Y = [[device(z, x, y, c) for y in range(NY) for c in range(NC)] for z in range(NZ) for x in range(NX)]
GROUPS_Z = [[device(z, x, y, c) for z in range(NZ)] for x in range(NX) for y in range(NY) for c in range(NC)]
RING_Z = [[z * NX + x for z in range(NZ)] for x in range(NX)]


def swap(value, dz, dx, dy, dc):
    pairs = [(device(z, x, y, c), device(z ^ dz, x ^ dx, y ^ dy, c ^ dc)) for z, x, y, c in EVERY]
    return lax.ppermute(value, AXES, pairs)


def spread(value, groups):
    copies = jnp.broadcast_to(value[None], (len(groups[0]),) + value.shape)
    return lax.all_to_all(copies, AXES, 0, 0, axis_index_groups=groups)


def after(value, *others):
    return lax.optimization_barrier((value,) + others)[0]


def contract_rows(a, b):
    return lax.dot_general(a, b, (((0,), (0,)), ((), ())), preferred_element_type=F32)


def gram_kernel(place, own, behind, beyond, ahead, cols, out):
    xi, yi, sense = place[0], place[1], 1 - 2 * place[2]
    rows = out.shape[3] - TAIL
    top = None
    for piece, dy in ((own, 0), (behind, -1), (beyond, -2), (ahead, 1)):
        part = lax.dot_general(
            piece[...], cols[...], (((0,), (0,)), ((), ())), preferred_element_type=F32
        )
        large = jnp.max(jnp.abs(part), axis=0, keepdims=True)
        top = large if top is None else jnp.maximum(top, large)
        y = lax.rem(yi + sense * dy + NY, NY)
        for i in range(2):
            for x in range(NX):
                first = (i * NX + x) * rows
                to = lax.rem((x - xi) * sense + NX, NX)
                out[to, 0, 2 * y + i, :rows] = part[first : first + rows]
    code = jnp.ceil(jnp.log2(jnp.clip(top, 2.0**-100, 2.0**100)))
    factor = jnp.exp2(LARGEST - code)
    tail = jnp.broadcast_to(code, (TAIL, code.shape[1]))
    for to in range(NX):
        for z in range(NZ):
            out[to, 0, z, :rows] = out[to, 0, z, :rows] * factor
            out[to, 0, z, rows:] = tail


def gram_parts(place, pieces):
    local_rows, wide = pieces[0].shape
    rows, cols = wide * NY // (NX * NZ), wide // NC
    whole = [pl.BlockSpec(piece.shape, lambda i, s: (0, 0)) for piece in pieces]
    return pl.pallas_call(
        gram_kernel,
        grid_spec=pltpu.PrefetchScalarGridSpec(
            num_scalar_prefetch=1,
            grid=(NC,),
            in_specs=whole + [pl.BlockSpec((local_rows, cols), lambda i, s: (0, i))],
            out_specs=pl.BlockSpec((NX, 1, NZ, rows + TAIL, cols), lambda i, s: (0, i, 0, 0, 0)),
        ),
        out_shape=jax.ShapeDtypeStruct((NX, NC, NZ, rows + TAIL, cols), F32),
        compiler_params=pltpu.CompilerParams(vmem_limit_bytes=32 << 20),
        cost_estimate=pl.CostEstimate(
            flops=2 * local_rows * wide * wide * NY,
            bytes_accessed=2 * local_rows * wide * NY + 4 * wide * wide * NY,
            transcendentals=0,
        ),
    )(place, *pieces, pieces[0])


def add_scaled(*terms):
    codes = [term[:, :1, -1:] for term in terms]
    code = functools.reduce(jnp.maximum, codes) + (len(terms) - 1)
    total = sum(term * jnp.exp2(own - code) for term, own in zip(terms, codes))
    in_tail = lax.broadcasted_iota(jnp.int32, total.shape, 2) >= total.shape[2] - TAIL
    return jnp.where(in_tail, code, total)


def direction_kernel(blocks, place, *refs):
    pieces, roots = refs[: NY * blocks], refs[NY * blocks]
    mine, theirs, squares, whole, root, sems = refs[NY * blocks + 1 :]
    xi, yi, ci = place[0], place[1], place[2]
    sense = 1 - 2 * ci
    wide, slab = root.shape[-1], mine.shape[-1]
    copies = []
    for j in range(blocks):
        group = [(roots.at[:, dx, j], root.at[j, :, lax.rem(xi + dx, NX)]) for dx in range(NX)]
        group += [(pieces[NY * j + k], whole.at[j, k]) for k in range(NY)]
        copies.append(
            [pltpu.make_async_copy(a, b, sems.at[j, i]) for i, (a, b) in enumerate(group)]
        )
    for group in copies:
        for copy in group:
            copy.start()
    for j in range(blocks):
        for copy in copies[j]:
            copy.wait()
        value = None
        for k, dy in enumerate((0, -1, -2, 1)):
            y = lax.rem(yi + sense * dy + NY, NY)
            b = root[j, pl.ds(2 * y, 2)].reshape(wide, wide)
            term = jnp.dot(whole[j, k], b, preferred_element_type=F32)
            value = term if value is None else value + term
        first, second = value[:, :slab], value[:, slab:]
        mine[j] = jnp.where(ci == 0, first, second)
        theirs[j] = jnp.where(ci == 0, second, first)
        squares[j] = jnp.full((8, 128), jnp.sum(value * value), F32)


def direction_of(place, pieces, roots):
    blocks = len(pieces)
    local_rows, wide = pieces[0][0].shape
    rows, slab = roots.shape[3], wide // NC
    result = jax.ShapeDtypeStruct((blocks, local_rows, slab), F32)
    vmem = pl.BlockSpec(memory_space=pltpu.VMEM)
    return pl.pallas_call(
        functools.partial(direction_kernel, blocks),
        in_specs=[pl.BlockSpec(memory_space=pltpu.SMEM)]
        + [pl.BlockSpec(memory_space=pltpu.HBM)] * (NY * blocks + 1),
        out_specs=[vmem, vmem, vmem],
        out_shape=[result, result, jax.ShapeDtypeStruct((blocks, 8, 128), F32)],
        scratch_shapes=[
            pltpu.VMEM((blocks, NY, local_rows, wide), jnp.bfloat16),
            pltpu.VMEM((blocks, NZ, NX, rows, wide), jnp.bfloat16),
            pltpu.SemaphoreType.DMA((blocks, NX + NY)),
        ],
        compiler_params=pltpu.CompilerParams(vmem_limit_bytes=60 << 20),
        cost_estimate=pl.CostEstimate(
            flops=2 * blocks * local_rows * wide * wide * NY,
            bytes_accessed=2 * blocks * (local_rows + wide) * wide * NY + 4 * blocks * local_rows * wide,
            transcendentals=0,
        ),
    )(place, *[piece for group in pieces for piece in group], roots)


def step_kernel(place, scale, kept, given, out):
    core, j = place[2], pl.program_id(0)
    out[core, 0] = kept[0] * scale[core, j]
    out[1 - core, 0] = given[0] * scale[1 - core, j]


def scaled_step(place, scale, kept, given):
    blocks, local_rows, slab = kept.shape
    return pl.pallas_call(
        step_kernel,
        grid=(blocks,),
        in_specs=[pl.BlockSpec(memory_space=pltpu.SMEM)] * 2
        + [pl.BlockSpec((1, local_rows, slab), lambda j: (j, 0, 0))] * 2,
        out_specs=pl.BlockSpec((NC, 1, local_rows, slab), lambda j: (0, j, 0, 0)),
        out_shape=jax.ShapeDtypeStruct((NC, blocks, local_rows, slab), F32),
        compiler_params=pltpu.CompilerParams(vmem_limit_bytes=32 << 20),
        cost_estimate=pl.CostEstimate(
            flops=2 * blocks * local_rows * slab,
            bytes_accessed=16 * blocks * local_rows * slab,
            transcendentals=0,
        ),
    )(place, scale, kept, given)


def on_device(grads, accum, roots):
    experts, local_rows, blocks, slab = grads.shape
    fsdp, tp = lax.axis_index("fsdp"), lax.axis_index("tp")
    core = lax.rem(tp, NC)
    first_core = core == 0
    place = jnp.stack([lax.rem(fsdp, NX), tp // NC, core]).astype(jnp.int32)
    rows_total = local_rows * lax.axis_size("fsdp")
    mine = grads.transpose(0, 2, 1, 3)

    def pick(pair):
        return jnp.where(first_core, pair[0], pair[1]), jnp.where(first_core, pair[1], pair[0])

    def by_core(kept, given):
        return jnp.concatenate(pick((kept, given)), axis=-1)

    (kept_grads, other_grads), (kept_roots, other_roots) = pick(mine), pick(roots)
    given = swap_cores(jnp.concatenate([other_grads, other_roots], axis=1))
    given_grads, given_roots = given[:, :local_rows], given[:, local_rows:]

    chip = [by_core(kept_grads[j], given_grads[j]) for j in range(blocks)]
    root = by_core(kept_roots, given_roots)
    chip[0], chip[1], chip[2], root = lax.optimization_barrier((*chip, root))

    def send_near(own):
        return step_y(own, 1), step_y(own, -1)

    near = [send_near(chip[0])]
    root = [root, shift_x(root, -1), shift_x(root, 2), shift_x(root, 1)]
    root = jnp.stack(lax.optimization_barrier((*root, *near[0]))[:NX])
    root_pieces = lax.all_gather(root, "fsdp", axis=0, axis_index_groups=RING_Z)

    near.append(send_near(after(chip[1], *near[0])))
    near.append(send_near(after(chip[2], *near[1])))
    gradient = mine.astype(F32)
    adagrad = gradient / (jnp.sqrt(accum.transpose(0, 2, 1, 3) + gradient * gradient) + EPS)
    adagrad_sq = jnp.sum(adagrad * adagrad, axis=(2, 3))

    def collect(j, *wait):
        behind = after(near[j][0], *wait) if wait else near[j][0]
        return chip[j], near[j][0], step_y(behind, 1), near[j][1]

    def send_first(part):
        return step_x(part[2].astype(F16), 1), step_x(part[3].astype(F16), -1)

    def onward(part, arrived):
        return add_scaled(part[1], arrived[0].astype(F32)).astype(F16)

    def send_second(value, arrived):
        return step_x(value, 1), arrived[1]

    def owned(part, arrived):
        return add_scaled(part[0], arrived[0].astype(F32), arrived[1].astype(F32)).astype(F16)

    def send_rows(summed):
        summed = summed.reshape(NC * NZ, -1, slab)
        return lax.all_to_all(summed, AXES, 0, 0, axis_index_groups=GROUPS_CZ)

    def add_rows(term):
        term = term.reshape(experts, NZ, -1, slab).astype(F32)
        factor = jnp.exp2(term[:, :, -1:] - LARGEST)
        return jnp.sum(term[:, :, :-TAIL] * factor, axis=1) / rows_total

    pieces = [collect(0), collect(1)]
    part0 = gram_parts(after(place, *near[1]), pieces[0])
    pieces.append(collect(2))
    got0 = send_first(part0)
    part1 = gram_parts(after(place, part0, *near[2]), pieces[1])
    got1 = send_first(part1)
    value0 = onward(part0, after(got0, part1))
    got0 = send_second(value0, got0)
    part2 = gram_parts(after(place, value0), pieces[2])
    got2 = send_first(part2)
    value1 = onward(part1, after(got1, part2))
    got1 = send_second(value1, got1)
    rows0 = owned(part0, after(got0, value1))
    terms = [send_rows(rows0)]
    kept_part, given_part, squares = direction_of(after(place, rows0), pieces, root_pieces)
    given_part = swap_cores(given_part)
    value2 = onward(part2, after(got2, squares))
    got2 = send_second(value2, got2)

    direction_sq = squares[:, 0, 0]
    none = jnp.zeros_like(direction_sq)
    direction_sq = jnp.where(
        first_core, jnp.stack([direction_sq, none]), jnp.stack([none, direction_sq])
    )
    sums = after(jnp.stack([adagrad_sq, direction_sq]), terms[0])
    sums = jnp.sum(spread(sums, GROUPS_Y), axis=0)
    rows1 = owned(part1, after(got1, value2, sums))
    terms.append(send_rows(rows1))
    sums = sums + swap(sums, 0, 1, 0, 0)
    sums = sums + swap(sums, 0, 2, 0, 0)
    rows2 = owned(part2, after(got2, rows1, sums))
    sums = jnp.sum(spread(after(sums, terms[1]), GROUPS_Z), axis=0)
    terms.append(send_rows(after(rows2, sums)))
    statistic = jnp.stack([add_rows(term) for term in terms], axis=1)
    graft_scale = jnp.sqrt(sums[0]) / jnp.sqrt(sums[1] + 1e-06)
    step = scaled_step(place, graft_scale, kept_part, given_part)
    return (statistic, step.transpose(0, 2, 1, 3))


def solution(mesh):
    placed = (P(None, "fsdp", None, "tp"), P(None, "fsdp", None, "tp"), P(None, None, "fsdp", "tp"))
    return jax.shard_map(
        on_device,
        mesh=mesh,
        in_specs=placed,
        out_specs=(P(None, None, "fsdp", "tp"), P(None, "fsdp", None, "tp")),
        check_vma=False,
    )
```

time: 428 us -> 208 us (0.49)
  waiting for transfers between devices: 287 us -> 71.6 us
  blocking collectives: 75.6 us -> 0 us
  starting transfers between devices: 0.11 us -> 60.1 us
  matrix products: 26.5 us -> 0 us
  Pallas kernels: 0 us -> 20.5 us
  other arithmetic: 7.02 us -> 26.1 us
    reduce_scatter x1 -> x0, waiting for transfers between devices: 143 us -> none  [on_device(): lax.psum_scatter(partial_value.reshape(owned_rows * lax.axis_size('fsdp')...]
    all_gather x2 -> x1, waiting for transfers between devices: 143 us -> 0.01 us  [on_device(): root_pieces = lax.all_gather(root, 'fsdp', axis=0, axis_index_groups=RING_Z)]
    psum x1 -> x0, blocking collectives: 75.6 us -> none  [on_device(): lax.psum((adagrad_sq, direction_sq), ('fsdp', 'tp'))]
    ppermute x0 -> x25, waiting for transfers between devices: none -> 47.2 us  [the longest x9 28.8 us: step_y(): return lax.ppermute(value, 'tp', pairs)]
    ppermute x0 -> x25, starting transfers between devices: none -> 32.9 us  [the longest x9 10.5 us: step_y(): return lax.ppermute(value, 'tp', pairs)]
    all_to_all x0 -> x5, starting transfers between devices: none -> 27.2 us  [the longest x3 18.6 us: send_rows(): return lax.all_to_all(summed, AXES, 0, 0, axis_index_groups=GROUPS_CZ)]
    dot_general x2 -> x0, matrix products: 26.5 us -> none  [the longest x1 15.3 us: on_device(): jnp.einsum('erjk,ejkc->erjc', gathered, root_whole, preferred_element_typ...]
    all_to_all x0 -> x5, waiting for transfers between devices: none -> 24.4 us  [the longest x3 17.8 us: send_rows(): return lax.all_to_all(summed, AXES, 0, 0, axis_index_groups=GROUPS_CZ)]
  transfers between devices with their start and end apart: 3 -> 31, of which waited for: 3 -> 17; matrix products, arithmetic and copies ran while one was open for 11% -> 13% of each run, Pallas kernels for 0% -> 10%
where the time goes in v1:
time: 208 us; the launch traced here: 205 us
  waiting for transfers between devices  71.6 us (34%)
  starting transfers between devices  60.1 us (29%)
  other arithmetic  26.1 us (13%)
  Pallas kernels  20.5 us (10%)
  between operations  14.9 us (7%)
  local copies, waits for them, and re-layouts  12.2 us (6%)
    ppermute x9, waiting for transfers between devices, step_y(): return lax.ppermute(value, 'tp', pairs)  28.8 us
    all_to_all x3, starting transfers between devices, send_rows(): return lax.all_to_all(summed, AXES, 0, 0, axis_index_groups=GROUPS_CZ)  18.6 us
    all_to_all x3, waiting for transfers between devices, send_rows(): return lax.all_to_all(summed, AXES, 0, 0, axis_index_groups=GROUPS_CZ)  17.8 us
    ppermute x9, starting transfers between devices, step_y(): return lax.ppermute(value, 'tp', pairs)  10.5 us
    ppermute x3, waiting for transfers between devices, shift_x(): return lax.ppermute(value, 'fsdp', pairs)  10.2 us
    ppermute x9, starting transfers between devices, step_x(): return lax.ppermute(value, AXES, pairs)  9.94 us
    pallas_call x1, Pallas kernels, direction_of(): pl.pallas_call(functools.partial(direction_kernel, blocks), in_specs=[pl....  8.98 us
    pallas_call x3, Pallas kernels, gram_parts(): pl.pallas_call(gram_kernel, grid_spec=pltpu.PrefetchScalarGridSpec(num_sc...  8.86 us
  transfers between devices with their start and end apart: 31, of which 17 were waited for; matrix products, arithmetic and copies ran while one was open for 13% of the time, Pallas kernels for 10%

profile of v1, /device:TPU:32, one launch (start us, length us, event | category | flops | bytes accessed | tf_op | source)
XLA Modules:
  0.0 205.5 jit_solution(12202904654603932595)
XLA Ops:
  7.2 1.5 select_bitcast_fusion
  8.9 2.4 %collective-permute-done = bf16[3,576,256]{2,1,0:T(8,128)(2,1)S(1)} collective-permute-done((bf16[3,576,256]{2,1,0:T(8,128)(2,1)S(1)}, bf16[3,576,256]{2,1,0:T(8,128)(2,1)S(1)}, u32[]{:S(2)}, u32[]{:S(2)}) %collective-permute-start) | collective-permute-done | bytes 884768 | tf_op jit(solution)/shard_map/ppermute | solution.py:45
  11.7 1.7 collective-permute-start.1
  13.3 1.7 collective-permute-start.2
  15.0 2.8 %collective-permute-start.18 = (bf16[3,64,512]{2,1,0:T(8,128)(2,1)S(1)}, bf16[3,64,512]{2,1,0:T(8,128)(2,1)S(1)}, u32[]{:S(2)}, u32[]{:S(2)}) collective-permute-start(bf16[3,64,512]{2,1,0:T(8,128)(2,1)S(1)} %pad_maximum_fusion.6), channel_id=1, source_target_pairs={{0,24},{8,0},{16,8},{24,16},{32,56},{40,32},{48,40},{56,48},{64,88... | collective-permute-start | bytes 589832 | tf_op jit(solution)/shard_map/ppermute | solution.py:41
  17.8 0.8 collective-permute-start.19
  18.6 0.9 collective-permute-start.20
  19.5 6.5 %collective-permute-done.18 = bf16[3,64,512]{2,1,0:T(8,128)(2,1)S(1)} collective-permute-done((bf16[3,64,512]{2,1,0:T(8,128)(2,1)S(1)}, bf16[3,64,512]{2,1,0:T(8,128)(2,1)S(1)}, u32[]{:S(2)}, u32[]{:S(2)}) %collective-permute-start.18) | collective-permute-done | bytes 196640 | tf_op jit(solution)/shard_map/ppermute | solution.py:41
  26.0 1.2 collective-permute-done.19
  27.2 2.5 %collective-permute-done.20 = bf16[3,64,512]{2,1,0:T(8,128)(2,1)S(1)} collective-permute-done((bf16[3,64,512]{2,1,0:T(8,128)(2,1)S(1)}, bf16[3,64,512]{2,1,0:T(8,128)(2,1)S(1)}, u32[]{:S(2)}, u32[]{:S(2)}) %collective-permute-start.20) | collective-permute-done | bytes 196640 | tf_op jit(solution)/shard_map/ppermute | solution.py:41
  29.7 1.1 pad_maximum_fusion.1
  31.2 2.9 %collective-permute-start.4 = (bf16[512,512]{1,0:T(8,128)(2,1)S(1)}, bf16[512,512]{1,0:T(8,128)(2,1)S(1)}, u32[]{:S(2)}, u32[]{:S(2)}) collective-permute-start(bf16[512,512]{1,0:T(8,128)(2,1)S(1)} %get-tuple-element.33.own.cols.refs_4_), channel_id=1, source_target_pairs={{0,6},{1,3},{2,0},{3,5},{4,2},{5,7},{6,4},{7,1},{8,14},{9,11},{10,... | collective-permute-start | bytes 1572872 | tf_op jit(solution)/shard_map/ppermute | solution.py:36
  34.2 4.0 %fusion.4 = f32[2,3]{1,0:T(2,128)S(1)} fusion(f32[2,512,3,256]{3,1,2,0:T(8,128)} %param.4, bf16[2,512,3,256]{3,1,2,0:T(8,128)(2,1)} %param.3), kind=kLoop, calls=%fused_computation.6 | loop fusion | flops 5505018 | bytes 4718616 | tf_op jit(solution)/shard_map/reduce_sum | solution.py:245
  38.1 7.0 %collective-permute-done.3.behind.refs_5_ = bf16[512,512]{1,0:T(8,128)(2,1)S(1)} collective-permute-done((bf16[512,512]{1,0:T(8,128)(2,1)S(1)}, bf16[512,512]{1,0:T(8,128)(2,1)S(1)}, u32[]{:S(2)}, u32[]{:S(2)}) %collective-permute-start.3) | collective-permute-done | bytes 524320 | tf_op jit(solution)/shard_map/ppermute | solution.py:36
  45.1 1.4 collective-permute-done.4.ahead.refs_7_
  46.5 1.6 collective-permute-start.8
  48.1 2.1 %collective-permute-start.9 = (bf16[512,512]{1,0:T(8,128)(2,1)S(1)}, bf16[512,512]{1,0:T(8,128)(2,1)S(1)}, u32[]{:S(2)}, u32[]{:S(2)}) collective-permute-start(bf16[512,512]{1,0:T(8,128)(2,1)S(1)} %pad_maximum_fusion.4.own.cols.refs_8_), channel_id=1, source_target_pairs={{0,6},{1,3},{2,0},{3,5},{4,2},{5,7},{6,4},{7,1},{8,14},{9,11},{10,... | collective-permute-start | bytes 1572872 | tf_op jit(solution)/shard_map/ppermute | solution.py:36
  50.2 2.4 %collective-permute-done.5.beyond.refs_2_ = bf16[512,512]{1,0:T(8,128)(2,1)S(1)} collective-permute-done((bf16[512,512]{1,0:T(8,128)(2,1)S(1)}, bf16[512,512]{1,0:T(8,128)(2,1)S(1)}, u32[]{:S(2)}, u32[]{:S(2)}) %collective-permute-start.5) | collective-permute-done | bytes 524320 | tf_op jit(solution)/shard_map/ppermute | solution.py:36
  52.6 3.0 %shard_map.50 = f32[4,2,8,72,256]{4,3,2,1,0:T(8,128)S(1)} custom-call(s32[3]{0:T(128)S(1)} %pad_add_fusion.place, bf16[512,512]{1,0:T(8,128)(2,1)S(1)} %get-tuple-element.32.own.cols.refs_0_, bf16[512,512]{1,0:T(8,128)(2,1)S(1)} %collective-permute-done.1.behind.refs_1_, bf16[512,512]{1,0:T(8,128)(2,1)S(1)} %collective-permute-done.5.beyond.refs_2_, ...), custom_call_target="tpu_custom_call" | custom-call | flops 1073741824 | bytes 6291456 | tf_op jit(solution)/shard_map/pallas_call | solution.py:103
  56.5 3.2 %collective-permute-start.7 = (f16[2,8,72,256]{3,2,1,0:T(8,128)(2,1)S(1)}, f16[2,8,72,256]{3,2,1,0:T(8,128)(2,1)S(1)}, u32[]{:S(2)}, u32[]{:S(2)}) collective-permute-start(f16[2,8,72,256]{3,2,1,0:T(8,128)(2,1)S(1)} %get-tuple-element.82), channel_id=1, source_target_pairs={{0,24},{1,9},{2,26},{3,11},{4,28},{5,13},{6,30},{7,15},{8,0},{9,17... | collective-permute-start | bytes 1769480 | tf_op jit(solution)/shard_map/ppermute | solution.py:31
  59.9 3.7 %collective-permute-done.8.behind.refs_9_ = bf16[512,512]{1,0:T(8,128)(2,1)S(1)} collective-permute-done((bf16[512,512]{1,0:T(8,128)(2,1)S(1)}, bf16[512,512]{1,0:T(8,128)(2,1)S(1)}, u32[]{:S(2)}, u32[]{:S(2)}) %collective-permute-start.8) | collective-permute-done | bytes 524320 | tf_op jit(solution)/shard_map/ppermute | solution.py:36
  63.6 5.8 %collective-permute-done.10.beyond.refs_6_ = bf16[512,512]{1,0:T(8,128)(2,1)S(1)} collective-permute-done((bf16[512,512]{1,0:T(8,128)(2,1)S(1)}, bf16[512,512]{1,0:T(8,128)(2,1)S(1)}, u32[]{:S(2)}, u32[]{:S(2)}) %collective-permute-start.10) | collective-permute-done | bytes 524320 | tf_op jit(solution)/shard_map/ppermute | solution.py:36
  69.4 3.0 %shard_map.51 = f32[4,2,8,72,256]{4,3,2,1,0:T(8,128)S(1)} custom-call(s32[3]{0:T(128)S(1)} %pad_add_fusion.place, bf16[512,512]{1,0:T(8,128)(2,1)S(1)} %get-tuple-element.33.own.cols.refs_4_, bf16[512,512]{1,0:T(8,128)(2,1)S(1)} %collective-permute-done.3.behind.refs_5_, bf16[512,512]{1,0:T(8,128)(2,1)S(1)} %collective-permute-done.10.beyond.refs_6_, ...), custom_call_target="tpu_custom_call" | custom-call | flops 1073741824 | bytes 6291456 | tf_op jit(solution)/shard_map/pallas_call | solution.py:103
  73.1 3.2 %collective-permute-start.13 = (f16[2,8,72,256]{3,2,1,0:T(8,128)(2,1)S(1)}, f16[2,8,72,256]{3,2,1,0:T(8,128)(2,1)S(1)}, u32[]{:S(2)}, u32[]{:S(2)}) collective-permute-start(f16[2,8,72,256]{3,2,1,0:T(8,128)(2,1)S(1)} %get-tuple-element.78), channel_id=1, source_target_pairs={{0,24},{1,9},{2,26},{3,11},{4,28},{5,13},{6,30},{7,15},{8,0},{9,17... | collective-permute-start | bytes 1769480 | tf_op jit(solution)/shard_map/ppermute | solution.py:31
  76.3 1.2 slice_bitcast_fusion.2
  78.1 8.6 %collective-permute-done.14.beyond.refs_10_ = bf16[512,512]{1,0:T(8,128)(2,1)S(1)} collective-permute-done((bf16[512,512]{1,0:T(8,128)(2,1)S(1)}, bf16[512,512]{1,0:T(8,128)(2,1)S(1)}, u32[]{:S(2)}, u32[]{:S(2)}) %collective-permute-start.14) | collective-permute-done | bytes 524320 | tf_op jit(solution)/shard_map/ppermute | solution.py:36
  86.7 3.0 %shard_map.52 = f32[4,2,8,72,256]{4,3,2,1,0:T(8,128)S(1)} custom-call(s32[3]{0:T(128)S(1)} %pad_add_fusion.place, bf16[512,512]{1,0:T(8,128)(2,1)S(1)} %pad_maximum_fusion.4.own.cols.refs_8_, bf16[512,512]{1,0:T(8,128)(2,1)S(1)} %collective-permute-done.8.behind.refs_9_, bf16[512,512]{1,0:T(8,128)(2,1)S(1)} %collective-permute-done.14.beyond.refs_10_, ...), custom_call_target="tpu_custom_call" | custom-call | flops 1073741824 | bytes 6291456 | tf_op jit(solution)/shard_map/pallas_call | solution.py:103
  90.0 1.9 copy-done
  91.9 1.3 slice_bitcast_fusion.6
  93.2 3.2 %collective-permute-start.17 = (f16[2,8,72,256]{3,2,1,0:T(8,128)(2,1)}, f16[2,8,72,256]{3,2,1,0:T(8,128)(2,1)S(1)}, u32[]{:S(2)}, u32[]{:S(2)}) collective-permute-start(f16[2,8,72,256]{3,2,1,0:T(8,128)(2,1)} %get-tuple-element.80), channel_id=1, source_target_pairs={{0,24},{1,9},{2,26},{3,11},{4,28},{5,13},{6,30},{7,15},{8,0},{9,17... | collective-permute-start | bytes 1769480 | tf_op jit(solution)/shard_map/ppermute | solution.py:31
  96.6 1.1 select_convert_fusion.4
  98.1 1.2 select_convert_fusion.3
  99.3 8.6 %all-to-all-start = ((f16[16,72,256]{2,1,0:T(8,128)(2,1)}), f16[16,72,256]{2,1,0:T(8,128)(2,1)S(1)}, u32[]{:S(2)}, u32[]{:S(2)}) async-start(f16[16,72,256]{2,1,0:T(8,128)(2,1)} %bitcast.23), calls=%async_computation | async-start | bytes 1179648 | tf_op jit(solution)/shard_map/all_to_all | solution.py:265
  107.9 3.3 %slice_bitcast_fusion.1 = (f32[2,8,72,256]{3,2,1,0:T(8,128)}, f32[2,8,72,256]{3,2,1,0:T(8,128)}) fusion(f32[4,2,8,72,256]{4,3,2,1,0:T(8,128)} %copy-done), kind=kLoop, calls=%fused_computation.8 | loop fusion | bytes 4718592 | tf_op jit(solution)/shard_map/squeeze | solution.py:255
  111.2 9.0 %shard_map.53 = (f32[3,512,256]{2,1,0:T(8,128)}, f32[3,512,256]{2,1,0:T(8,128)}, f32[3,8,128]{2,1,0:T(8,128)}) custom-call(s32[3]{0:T(128)} %copy-done.15, bf16[512,512]{1,0:T(8,128)(2,1)} %copy-done.3, bf16[512,512]{1,0:T(8,128)(2,1)} %copy-done.5, bf16[512,512]{1,0:T(8,128)(2,1)} %copy-done.9, bf16[512,512]{1,0:T(8,128)(2,1)} %copy-done.6, ...), custom_call_target="tpu_custom_call" | custom-call | flops 3221225472 | bytes 15728640 | tf_op jit(solution)/shard_map/pallas_call | solution.py:166
  120.2 1.2 convert_element_type.105
  121.3 0.7 multiply_exponential_fusion.7
  122.1 0.8 slice_reduce_fusion
  123.0 2.6 %all-to-all-done = f16[16,72,256]{2,1,0:T(8,128)(2,1)S(1)} async-done(((f16[16,72,256]{2,1,0:T(8,128)(2,1)}), f16[16,72,256]{2,1,0:T(8,128)(2,1)S(1)}, u32[]{:S(2)}, u32[]{:S(2)}) %all-to-all-start) | async-done | bytes 589856 | tf_op jit(solution)/shard_map/all_to_all | solution.py:265
  125.6 0.6 broadcast_in_dim.65
  126.2 3.3 %all-to-all-start.1 = ((f32[8,2,2,3]{3,2,1,0:T(2,128)}), f32[8,2,2,3]{3,2,1,0:T(2,128)S(1)}, u32[]{:S(2)}, u32[]{:S(2)}) async-start(f32[8,2,2,3]{3,2,1,0:T(2,128)} %broadcast_in_dim.65), calls=%async_computation.1 | async-start | bytes 32768 | tf_op jit(solution)/shard_map/all_to_all | solution.py:63
  129.6 2.6 %select_convert_fusion.2 = f16[2,8,72,256]{3,2,1,0:T(8,128)(2,1)} fusion(f32[2,256]{1,0:T(2,128)S(1)} %bitcast.201, f32[2,256]{1,0:T(2,128)S(1)} %bitcast.203, f32[2,256]{1,0:T(2,128)S(1)} %bitcast.200, pred[72]{0:T(512)(128)(4,1)S(1)} %iota_compare_fusion, f16[2,8,72,256]{3,2,1,0:T(8,128)(2,1)} %collective-permute-done.16, f32[4,2,8,72,256]{4,3,2,1,0:T(8,128)} %copy-done), kind=kLoop, calls=%fused_computation.15 | loop fusion | flops 1769472 | bytes 2365512 | tf_op jit(solution)/shard_map/convert_element_type | solution.py:255
  132.1 2.7 %all-to-all-done.1 = f32[8,2,2,3]{3,2,1,0:T(2,128)S(1)} async-done(((f32[8,2,2,3]{3,2,1,0:T(2,128)}), f32[8,2,2,3]{3,2,1,0:T(2,128)S(1)}, u32[]{:S(2)}, u32[]{:S(2)}) %all-to-all-start.1) | async-done | bytes 416 | tf_op jit(solution)/shard_map/all_to_all | solution.py:63
  135.2 0.7 multiply_exponential_fusion.5
  136.0 2.5 %select_convert_fusion.1 = f16[2,8,72,256]{3,2,1,0:T(8,128)(2,1)} fusion(f32[2,256]{1,0:T(2,128)S(1)} %bitcast.209, f32[2,256]{1,0:T(2,128)S(1)} %bitcast.213, f32[2,256]{1,0:T(2,128)S(1)} %bitcast.215, f32[2,256]{1,0:T(2,128)S(1)} %bitcast.207, pred[72]{0:T(512)(128)(4,1)S(1)} %iota_compare_fusion, f16[2,8,72,256]{3,2,1,0:T(8,128)(2,1)S(1)} %collective-permute-done.13, ...), kind=kLoop, calls=%fused_computation.14 | loop fusion | flops 2654208 | bytes 2957384 | tf_op jit(solution)/shard_map/convert_element_type | solution.py:261
  138.4 4.6 %all-to-all-start.2 = ((f16[16,72,256]{2,1,0:T(8,128)(2,1)}), f16[16,72,256]{2,1,0:T(8,128)(2,1)}, u32[]{:S(2)}, u32[]{:S(2)}) async-start(f16[16,72,256]{2,1,0:T(8,128)(2,1)} %bitcast.191), calls=%async_computation.2 | async-start | bytes 1179648 | tf_op jit(solution)/shard_map/all_to_all | solution.py:265
  143.1 1.0 copy-done.18
  144.3 3.2 %collective-permute-start.24 = (f32[3,512,256]{2,1,0:T(8,128)}, f32[3,512,256]{2,1,0:T(8,128)S(1)}, u32[]{:S(2)}, u32[]{:S(2)}) collective-permute-start(f32[3,512,256]{2,1,0:T(8,128)} %get-tuple-element.59), channel_id=1, source_target_pairs={{0,1},{1,0},{2,3},{3,2},{4,5},{5,4},{6,7},{7,6},{8,9},{9,8},{10,11... | collective-permute-start | bytes 4718600 | tf_op jit(solution)/shard_map/ppermute | solution.py:45
  147.4 4.1 %collective-permute-done.22 = f32[2,2,3]{1,2,0:T(4,128)S(1)} collective-permute-done((f32[2,2,3]{1,2,0:T(4,128)S(1)}, f32[2,2,3]{1,2,0:T(4,128)S(1)}, u32[]{:S(2)}, u32[]{:S(2)}) %collective-permute-start.22) | collective-permute-done | bytes 80 | tf_op jit(solution)/shard_map/ppermute | solution.py:58
  151.6 4.7 %collective-permute-start.23 = (f32[2,2,3]{1,2,0:T(4,128)S(1)}, f32[2,2,3]{1,2,0:T(4,128)S(1)}, u32[]{:S(2)}, u32[]{:S(2)}) collective-permute-start(f32[2,2,3]{1,2,0:T(4,128)S(1)} %add.87), channel_id=1, source_target_pairs={{0,16},{1,17},{2,18},{3,19},{4,20},{5,21},{6,22},{7,23},{8,24},{9,... | collective-permute-start | bytes 152 | tf_op jit(solution)/shard_map/ppermute | solution.py:58
  156.3 1.6 collective-permute-done.23
  158.1 0.7 multiply_exponential_fusion.2
  158.9 2.0 all-to-all-done.2
  160.9 0.6 broadcast_in_dim.70
  161.5 5.3 %all-to-all-start.3 = ((f32[8,2,2,3]{3,2,1,0:T(2,128)}), f32[8,2,2,3]{3,2,1,0:T(2,128)S(1)}, u32[]{:S(2)}, u32[]{:S(2)}) async-start(f32[8,2,2,3]{3,2,1,0:T(2,128)} %broadcast_in_dim.70), calls=%async_computation.3 | async-start | bytes 32768 | tf_op jit(solution)/shard_map/all_to_all | solution.py:63
  166.8 2.5 %select_convert_fusion = f16[2,8,72,256]{3,2,1,0:T(8,128)(2,1)} fusion(f32[2,256]{1,0:T(2,128)S(1)} %bitcast.202, f32[2,256]{1,0:T(2,128)S(1)} %bitcast.204, f32[2,256]{1,0:T(2,128)S(1)} %bitcast.205, f32[2,256]{1,0:T(2,128)S(1)} %bitcast.199, pred[72]{0:T(512)(128)(4,1)S(1)} %iota_compare_fusion, f16[2,8,72,256]{3,2,1,0:T(8,128)(2,1)S(1)} %collective-permute-done.17, ...), kind=kLoop, calls=%fused_computation.13 | loop fusion | flops 2654208 | bytes 2957384 | tf_op jit(solution)/shard_map/convert_element_type | solution.py:261
  169.3 3.9 %all-to-all-done.3 = f32[8,2,2,3]{3,2,1,0:T(2,128)S(1)} async-done(((f32[8,2,2,3]{3,2,1,0:T(2,128)}), f32[8,2,2,3]{3,2,1,0:T(2,128)S(1)}, u32[]{:S(2)}, u32[]{:S(2)}) %all-to-all-start.3) | async-done | bytes 416 | tf_op jit(solution)/shard_map/all_to_all | solution.py:63
  173.3 5.4 %all-to-all-start.4 = ((f16[16,72,256]{2,1,0:T(8,128)(2,1)}), f16[16,72,256]{2,1,0:T(8,128)(2,1)}, u32[]{:S(2)}, u32[]{:S(2)}) async-start(f16[16,72,256]{2,1,0:T(8,128)(2,1)} %bitcast.46), calls=%async_computation.4 | async-start | bytes 1179648 | tf_op jit(solution)/shard_map/all_to_all | solution.py:265
  178.7 1.3 bitcast_convert_fusion.1
  180.3 0.4 copy-done.16
  180.7 2.7 %shard_map.54 = f32[2,3,512,256]{3,2,1,0:T(8,128)} custom-call(s32[3]{0:T(128)S(1)} %copy-done.16, f32[2,3]{1,0:T(2,128)S(1)} %bitcast.187, f32[3,512,256]{2,1,0:T(8,128)S(1)} %copy-done.14, f32[3,512,256]{2,1,0:T(8,128)S(1)} %collective-permute-done.24.given), custom_call_target="tpu_custom_call" | custom-call | flops 786432 | bytes 6291456 | tf_op jit(solution)/shard_map/pallas_call | solution.py:194
  183.4 13.2 %all-to-all-done.4 = f16[16,72,256]{2,1,0:T(8,128)(2,1)} async-done(((f16[16,72,256]{2,1,0:T(8,128)(2,1)}), f16[16,72,256]{2,1,0:T(8,128)(2,1)}, u32[]{:S(2)}, u32[]{:S(2)}) %all-to-all-start.4) | async-done | bytes 589856 | tf_op jit(solution)/shard_map/all_to_all | solution.py:265
  196.5 1.2 bitcast_convert_fusion
  197.8 0.8 pad_maximum_fusion.5
  (141 shorter events, 5.4 us)
Async XLA Ops:
  7.2 104.0 %all-gather.3.cloned.1.call-start = ((), (), s32[]{:S(2)}) async-start(), calls=%async_computation.5 | async-start | bytes 7077888 | tf_op jit(solution)/shard_map/all_gather | solution.py:239
  7.2 1.5 copy-start.17
  8.8 2.5 %collective-permute-start = (bf16[3,576,256]{2,1,0:T(8,128)(2,1)S(1)}, bf16[3,576,256]{2,1,0:T(8,128)(2,1)S(1)}, u32[]{:S(2)}, u32[]{:S(2)}) collective-permute-start(bf16[3,576,256]{2,1,0:T(8,128)(2,1)S(1)} %pad_maximum_fusion), channel_id=1, source_target_pairs={{0,1},{1,0},{2,3},{3,2},{4,5},{5,4},{6,7},{7,6},{8,9},{9,8},{10,11... | collective-permute-start | bytes 2654216 | tf_op jit(solution)/shard_map/ppermute | solution.py:45
  11.5 75.2 %copy-start.2 = (bf16[512,512]{1,0:T(8,128)(2,1)}, bf16[512,512]{1,0:T(8,128)(2,1)S(1)}, u32[]{:S(2)}) copy-start(bf16[512,512]{1,0:T(8,128)(2,1)S(1)} %pad_maximum_fusion.4.own.cols.refs_8_) | copy-start | bytes 1572868
  11.7 40.9 %copy-start.3 = (bf16[512,512]{1,0:T(8,128)(2,1)}, bf16[512,512]{1,0:T(8,128)(2,1)S(1)}, u32[]{:S(2)}) copy-start(bf16[512,512]{1,0:T(8,128)(2,1)S(1)} %get-tuple-element.32.own.cols.refs_0_) | copy-start | bytes 1572868
  11.7 57.7 %copy-start.4 = (bf16[512,512]{1,0:T(8,128)(2,1)}, bf16[512,512]{1,0:T(8,128)(2,1)S(1)}, u32[]{:S(2)}) copy-start(bf16[512,512]{1,0:T(8,128)(2,1)S(1)} %get-tuple-element.33.own.cols.refs_4_) | copy-start | bytes 1572868
  11.7 18.0 %collective-permute-start.1 = (bf16[512,512]{1,0:T(8,128)(2,1)S(1)}, bf16[512,512]{1,0:T(8,128)(2,1)S(1)}, u32[]{:S(2)}, u32[]{:S(2)}) collective-permute-start(bf16[512,512]{1,0:T(8,128)(2,1)S(1)} %get-tuple-element.32.own.cols.refs_0_), channel_id=1, source_target_pairs={{0,2},{1,7},{2,4},{3,1},{4,6},{5,3},{6,0},{7,5},{8,10},{9,15},{10,... | collective-permute-start | bytes 1572872 | tf_op jit(solution)/shard_map/ppermute | solution.py:36
  13.3 16.3 %collective-permute-start.2 = (bf16[512,512]{1,0:T(8,128)(2,1)S(1)}, bf16[512,512]{1,0:T(8,128)(2,1)S(1)}, u32[]{:S(2)}, u32[]{:S(2)}) collective-permute-start(bf16[512,512]{1,0:T(8,128)(2,1)S(1)} %get-tuple-element.32.own.cols.refs_0_), channel_id=1, source_target_pairs={{0,6},{1,3},{2,0},{3,5},{4,2},{5,7},{6,4},{7,1},{8,14},{9,11},{10,... | collective-permute-start | bytes 1572872 | tf_op jit(solution)/shard_map/ppermute | solution.py:36
  15.0 11.0 %collective-permute-start.18 = (bf16[3,64,512]{2,1,0:T(8,128)(2,1)S(1)}, bf16[3,64,512]{2,1,0:T(8,128)(2,1)S(1)}, u32[]{:S(2)}, u32[]{:S(2)}) collective-permute-start(bf16[3,64,512]{2,1,0:T(8,128)(2,1)S(1)} %pad_maximum_fusion.6), channel_id=1, source_target_pairs={{0,24},{8,0},{16,8},{24,16},{32,56},{40,32},{48,40},{56,48},{64,88... | collective-permute-start | bytes 589832 | tf_op jit(solution)/shard_map/ppermute | solution.py:41
  17.8 9.4 %collective-permute-start.19 = (bf16[3,64,512]{2,1,0:T(8,128)(2,1)S(1)}, bf16[3,64,512]{2,1,0:T(8,128)(2,1)S(1)}, u32[]{:S(2)}, u32[]{:S(2)}) collective-permute-start(bf16[3,64,512]{2,1,0:T(8,128)(2,1)S(1)} %pad_maximum_fusion.6), channel_id=1, source_target_pairs={{0,16},{8,24},{16,0},{24,8},{32,48},{40,56},{48,32},{56,40},{64,80... | collective-permute-start | bytes 589832 | tf_op jit(solution)/shard_map/ppermute | solution.py:41
  18.6 11.1 %collective-permute-start.20 = (bf16[3,64,512]{2,1,0:T(8,128)(2,1)S(1)}, bf16[3,64,512]{2,1,0:T(8,128)(2,1)S(1)}, u32[]{:S(2)}, u32[]{:S(2)}) collective-permute-start(bf16[3,64,512]{2,1,0:T(8,128)(2,1)S(1)} %pad_maximum_fusion.6), channel_id=1, source_target_pairs={{0,8},{8,16},{16,24},{24,0},{32,40},{40,48},{48,56},{56,32},{64,72... | collective-permute-start | bytes 589832 | tf_op jit(solution)/shard_map/ppermute | solution.py:41
  29.7 22.9 %copy-start.5 = (bf16[512,512]{1,0:T(8,128)(2,1)}, bf16[512,512]{1,0:T(8,128)(2,1)S(1)}, u32[]{:S(2)}) copy-start(bf16[512,512]{1,0:T(8,128)(2,1)S(1)} %collective-permute-done.1.behind.refs_1_) | copy-start | bytes 1572868
  29.7 22.9 %copy-start.6 = (bf16[512,512]{1,0:T(8,128)(2,1)}, bf16[512,512]{1,0:T(8,128)(2,1)S(1)}, u32[]{:S(2)}) copy-start(bf16[512,512]{1,0:T(8,128)(2,1)S(1)} %collective-permute-done.2.ahead.refs_3_) | copy-start | bytes 1572868
  30.9 55.8 %copy-start.15 = (s32[3]{0:T(128)}, s32[3]{0:T(128)S(1)}, u32[]{:S(2)}) copy-start(s32[3]{0:T(128)S(1)} %pad_add_fusion.place) | copy-start | bytes 40
  30.9 14.2 %collective-permute-start.3 = (bf16[512,512]{1,0:T(8,128)(2,1)S(1)}, bf16[512,512]{1,0:T(8,128)(2,1)S(1)}, u32[]{:S(2)}, u32[]{:S(2)}) collective-permute-start(bf16[512,512]{1,0:T(8,128)(2,1)S(1)} %get-tuple-element.33.own.cols.refs_4_), channel_id=1, source_target_pairs={{0,2},{1,7},{2,4},{3,1},{4,6},{5,3},{6,0},{7,5},{8,10},{9,15},{10,... | collective-permute-start | bytes 1572872 | tf_op jit(solution)/shard_map/ppermute | solution.py:36
  31.2 15.3 %collective-permute-start.4 = (bf16[512,512]{1,0:T(8,128)(2,1)S(1)}, bf16[512,512]{1,0:T(8,128)(2,1)S(1)}, u32[]{:S(2)}, u32[]{:S(2)}) collective-permute-start(bf16[512,512]{1,0:T(8,128)(2,1)S(1)} %get-tuple-element.33.own.cols.refs_4_), channel_id=1, source_target_pairs={{0,6},{1,3},{2,0},{3,5},{4,2},{5,7},{6,4},{7,1},{8,14},{9,11},{10,... | collective-permute-start | bytes 1572872 | tf_op jit(solution)/shard_map/ppermute | solution.py:36
  34.2 18.4 %collective-permute-start.5 = (bf16[512,512]{1,0:T(8,128)(2,1)S(1)}, bf16[512,512]{1,0:T(8,128)(2,1)S(1)}, u32[]{:S(2)}, u32[]{:S(2)}) collective-permute-start(bf16[512,512]{1,0:T(8,128)(2,1)S(1)} %collective-permute-done.1.behind.refs_1_), channel_id=1, source_target_pairs={{0,2},{1,7},{2,4},{3,1},{4,6},{5,3},{6,0},{7,5},{8,10},{9,15},{10,... | collective-permute-start | bytes 1572872 | tf_op jit(solution)/shard_map/ppermute | solution.py:36
  45.1 24.3 %copy-start.7 = (bf16[512,512]{1,0:T(8,128)(2,1)}, bf16[512,512]{1,0:T(8,128)(2,1)S(1)}, u32[]{:S(2)}) copy-start(bf16[512,512]{1,0:T(8,128)(2,1)S(1)} %collective-permute-done.3.behind.refs_5_) | copy-start | bytes 1572868
  46.5 22.9 %copy-start.8 = (bf16[512,512]{1,0:T(8,128)(2,1)}, bf16[512,512]{1,0:T(8,128)(2,1)S(1)}, u32[]{:S(2)}) copy-start(bf16[512,512]{1,0:T(8,128)(2,1)S(1)} %collective-permute-done.4.ahead.refs_7_) | copy-start | bytes 1572868
  46.5 17.1 %collective-permute-start.8 = (bf16[512,512]{1,0:T(8,128)(2,1)S(1)}, bf16[512,512]{1,0:T(8,128)(2,1)S(1)}, u32[]{:S(2)}, u32[]{:S(2)}) collective-permute-start(bf16[512,512]{1,0:T(8,128)(2,1)S(1)} %pad_maximum_fusion.4.own.cols.refs_8_), channel_id=1, source_target_pairs={{0,2},{1,7},{2,4},{3,1},{4,6},{5,3},{6,0},{7,5},{8,10},{9,15},{10,... | collective-permute-start | bytes 1572872 | tf_op jit(solution)/shard_map/ppermute | solution.py:36
  48.1 15.5 %collective-permute-start.9 = (bf16[512,512]{1,0:T(8,128)(2,1)S(1)}, bf16[512,512]{1,0:T(8,128)(2,1)S(1)}, u32[]{:S(2)}, u32[]{:S(2)}) collective-permute-start(bf16[512,512]{1,0:T(8,128)(2,1)S(1)} %pad_maximum_fusion.4.own.cols.refs_8_), channel_id=1, source_target_pairs={{0,6},{1,3},{2,0},{3,5},{4,2},{5,7},{6,4},{7,1},{8,14},{9,11},{10,... | collective-permute-start | bytes 1572872 | tf_op jit(solution)/shard_map/ppermute | solution.py:36
  52.6 3.0 %copy-start.9 = (bf16[512,512]{1,0:T(8,128)(2,1)}, bf16[512,512]{1,0:T(8,128)(2,1)S(1)}, u32[]{:S(2)}) copy-start(bf16[512,512]{1,0:T(8,128)(2,1)S(1)} %collective-permute-done.5.beyond.refs_2_) | copy-start | bytes 1572868
  55.8 13.5 %collective-permute-start.10 = (bf16[512,512]{1,0:T(8,128)(2,1)S(1)}, bf16[512,512]{1,0:T(8,128)(2,1)S(1)}, u32[]{:S(2)}, u32[]{:S(2)}) collective-permute-start(bf16[512,512]{1,0:T(8,128)(2,1)S(1)} %collective-permute-done.3.behind.refs_5_), channel_id=1, source_target_pairs={{0,2},{1,7},{2,4},{3,1},{4,6},{5,3},{6,0},{7,5},{8,10},{9,15},{10,... | collective-permute-start | bytes 1572872 | tf_op jit(solution)/shard_map/ppermute | solution.py:36
  56.4 21.1 %collective-permute-start.6 = (f16[2,8,72,256]{3,2,1,0:T(8,128)(2,1)S(1)}, f16[2,8,72,256]{3,2,1,0:T(8,128)(2,1)S(1)}, u32[]{:S(2)}, u32[]{:S(2)}) collective-permute-start(f16[2,8,72,256]{3,2,1,0:T(8,128)(2,1)S(1)} %get-tuple-element.83), channel_id=1, source_target_pairs={{0,8},{1,25},{2,10},{3,27},{4,12},{5,29},{6,14},{7,31},{8,16},{9,1... | collective-permute-start | bytes 1769480 | tf_op jit(solution)/shard_map/ppermute | solution.py:31
  56.5 21.0 %collective-permute-start.7 = (f16[2,8,72,256]{3,2,1,0:T(8,128)(2,1)S(1)}, f16[2,8,72,256]{3,2,1,0:T(8,128)(2,1)S(1)}, u32[]{:S(2)}, u32[]{:S(2)}) collective-permute-start(f16[2,8,72,256]{3,2,1,0:T(8,128)(2,1)S(1)} %get-tuple-element.82), channel_id=1, source_target_pairs={{0,24},{1,9},{2,26},{3,11},{4,28},{5,13},{6,30},{7,15},{8,0},{9,17... | collective-permute-start | bytes 1769480 | tf_op jit(solution)/shard_map/ppermute | solution.py:31
  63.6 23.1 %copy-start.10 = (bf16[512,512]{1,0:T(8,128)(2,1)}, bf16[512,512]{1,0:T(8,128)(2,1)S(1)}, u32[]{:S(2)}) copy-start(bf16[512,512]{1,0:T(8,128)(2,1)S(1)} %collective-permute-done.8.behind.refs_9_) | copy-start | bytes 1572868
  63.6 23.1 %copy-start.11 = (bf16[512,512]{1,0:T(8,128)(2,1)}, bf16[512,512]{1,0:T(8,128)(2,1)S(1)}, u32[]{:S(2)}) copy-start(bf16[512,512]{1,0:T(8,128)(2,1)S(1)} %collective-permute-done.9.ahead.refs_11_) | copy-start | bytes 1572868
  69.4 3.0 %copy-start.12 = (bf16[512,512]{1,0:T(8,128)(2,1)}, bf16[512,512]{1,0:T(8,128)(2,1)S(1)}, u32[]{:S(2)}) copy-start(bf16[512,512]{1,0:T(8,128)(2,1)S(1)} %collective-permute-done.10.beyond.refs_6_) | copy-start | bytes 1572868
  72.4 24.2 %copy-start.1 = (f32[4,2,8,72,256]{4,3,2,1,0:T(8,128)}, f32[4,2,8,72,256]{4,3,2,1,0:T(8,128)S(1)}, u32[]{:S(2)}) copy-start(f32[4,2,8,72,256]{4,3,2,1,0:T(8,128)S(1)} %shard_map.51) | copy-start | bytes 14155780
  73.0 23.5 %collective-permute-start.12 = (f16[2,8,72,256]{3,2,1,0:T(8,128)(2,1)S(1)}, f16[2,8,72,256]{3,2,1,0:T(8,128)(2,1)S(1)}, u32[]{:S(2)}, u32[]{:S(2)}) collective-permute-start(f16[2,8,72,256]{3,2,1,0:T(8,128)(2,1)S(1)} %get-tuple-element.79), channel_id=1, source_target_pairs={{0,8},{1,25},{2,10},{3,27},{4,12},{5,29},{6,14},{7,31},{8,16},{9,1... | collective-permute-start | bytes 1769480 | tf_op jit(solution)/shard_map/ppermute | solution.py:31
  73.1 23.4 %collective-permute-start.13 = (f16[2,8,72,256]{3,2,1,0:T(8,128)(2,1)S(1)}, f16[2,8,72,256]{3,2,1,0:T(8,128)(2,1)S(1)}, u32[]{:S(2)}, u32[]{:S(2)}) collective-permute-start(f16[2,8,72,256]{3,2,1,0:T(8,128)(2,1)S(1)} %get-tuple-element.78), channel_id=1, source_target_pairs={{0,24},{1,9},{2,26},{3,11},{4,28},{5,13},{6,30},{7,15},{8,0},{9,17... | collective-permute-start | bytes 1769480 | tf_op jit(solution)/shard_map/ppermute | solution.py:31
  76.3 10.4 %collective-permute-start.14 = (bf16[512,512]{1,0:T(8,128)(2,1)S(1)}, bf16[512,512]{1,0:T(8,128)(2,1)S(1)}, u32[]{:S(2)}, u32[]{:S(2)}) collective-permute-start(bf16[512,512]{1,0:T(8,128)(2,1)S(1)} %collective-permute-done.8.behind.refs_9_), channel_id=1, source_target_pairs={{0,2},{1,7},{2,4},{3,1},{4,6},{5,3},{6,0},{7,5},{8,10},{9,15},{10,... | collective-permute-start | bytes 1572872 | tf_op jit(solution)/shard_map/ppermute | solution.py:36
  78.0 19.8 %collective-permute-start.11 = (f16[2,8,72,256]{3,2,1,0:T(8,128)(2,1)S(1)}, f16[2,8,72,256]{3,2,1,0:T(8,128)(2,1)S(1)}, u32[]{:S(2)}, u32[]{:S(2)}) collective-permute-start(f16[2,8,72,256]{3,2,1,0:T(8,128)(2,1)S(1)} %select_convert_fusion.5), channel_id=1, source_target_pairs={{0,8},{1,25},{2,10},{3,27},{4,12},{5,29},{6,14},{7,31},{8,16},{9,1... | collective-permute-start | bytes 1769480 | tf_op jit(solution)/shard_map/ppermute | solution.py:31
  86.7 3.0 %copy-start.13 = (bf16[512,512]{1,0:T(8,128)(2,1)}, bf16[512,512]{1,0:T(8,128)(2,1)S(1)}, u32[]{:S(2)}) copy-start(bf16[512,512]{1,0:T(8,128)(2,1)S(1)} %collective-permute-done.14.beyond.refs_10_) | copy-start | bytes 1572868
  89.7 2.2 %copy-start = (f32[4,2,8,72,256]{4,3,2,1,0:T(8,128)}, f32[4,2,8,72,256]{4,3,2,1,0:T(8,128)S(1)}, u32[]{:S(2)}) copy-start(f32[4,2,8,72,256]{4,3,2,1,0:T(8,128)S(1)} %shard_map.52) | copy-start | bytes 14155780
  93.2 27.0 %collective-permute-start.16 = (f16[2,8,72,256]{3,2,1,0:T(8,128)(2,1)}, f16[2,8,72,256]{3,2,1,0:T(8,128)(2,1)}, u32[]{:S(2)}, u32[]{:S(2)}) collective-permute-start(f16[2,8,72,256]{3,2,1,0:T(8,128)(2,1)} %get-tuple-element.81), channel_id=1, source_target_pairs={{0,8},{1,25},{2,10},{3,27},{4,12},{5,29},{6,14},{7,31},{8,16},{9,1... | collective-permute-start | bytes 1769480 | tf_op jit(solution)/shard_map/ppermute | solution.py:31
  93.2 27.0 %collective-permute-start.17 = (f16[2,8,72,256]{3,2,1,0:T(8,128)(2,1)}, f16[2,8,72,256]{3,2,1,0:T(8,128)(2,1)S(1)}, u32[]{:S(2)}, u32[]{:S(2)}) collective-permute-start(f16[2,8,72,256]{3,2,1,0:T(8,128)(2,1)} %get-tuple-element.80), channel_id=1, source_target_pairs={{0,24},{1,9},{2,26},{3,11},{4,28},{5,13},{6,30},{7,15},{8,0},{9,17... | collective-permute-start | bytes 1769480 | tf_op jit(solution)/shard_map/ppermute | solution.py:31
  99.3 26.3 %all-to-all-start = ((f16[16,72,256]{2,1,0:T(8,128)(2,1)}), f16[16,72,256]{2,1,0:T(8,128)(2,1)S(1)}, u32[]{:S(2)}, u32[]{:S(2)}) async-start(f16[16,72,256]{2,1,0:T(8,128)(2,1)} %bitcast.23), calls=%async_computation | async-start | bytes 1179648 | tf_op jit(solution)/shard_map/all_to_all | solution.py:265
  111.2 23.8 %collective-permute-start.15 = (f16[2,8,72,256]{3,2,1,0:T(8,128)(2,1)}, f16[2,8,72,256]{3,2,1,0:T(8,128)(2,1)S(1)}, u32[]{:S(2)}, u32[]{:S(2)}) collective-permute-start(f16[2,8,72,256]{3,2,1,0:T(8,128)(2,1)} %select_convert_fusion.4), channel_id=1, source_target_pairs={{0,8},{1,25},{2,10},{3,27},{4,12},{5,29},{6,14},{7,31},{8,16},{9,1... | collective-permute-start | bytes 1769480 | tf_op jit(solution)/shard_map/ppermute | solution.py:31
  126.2 8.6 %all-to-all-start.1 = ((f32[8,2,2,3]{3,2,1,0:T(2,128)}), f32[8,2,2,3]{3,2,1,0:T(2,128)S(1)}, u32[]{:S(2)}, u32[]{:S(2)}) async-start(f32[8,2,2,3]{3,2,1,0:T(2,128)} %broadcast_in_dim.65), calls=%async_computation.1 | async-start | bytes 32768 | tf_op jit(solution)/shard_map/all_to_all | solution.py:63
  138.4 22.4 %all-to-all-start.2 = ((f16[16,72,256]{2,1,0:T(8,128)(2,1)}), f16[16,72,256]{2,1,0:T(8,128)(2,1)}, u32[]{:S(2)}, u32[]{:S(2)}) async-start(f16[16,72,256]{2,1,0:T(8,128)(2,1)} %bitcast.191), calls=%async_computation.2 | async-start | bytes 1179648 | tf_op jit(solution)/shard_map/all_to_all | solution.py:265
  143.0 1.1 copy-start.18
  144.1 13.8 %collective-permute-start.21 = (f16[2,8,72,256]{3,2,1,0:T(8,128)(2,1)S(1)}, f16[2,8,72,256]{3,2,1,0:T(8,128)(2,1)S(1)}, u32[]{:S(2)}, u32[]{:S(2)}) collective-permute-start(f16[2,8,72,256]{3,2,1,0:T(8,128)(2,1)S(1)} %copy-done.18), channel_id=1, source_target_pairs={{0,8},{1,25},{2,10},{3,27},{4,12},{5,29},{6,14},{7,31},{8,16},{9,1... | collective-permute-start | bytes 1769480 | tf_op jit(solution)/shard_map/ppermute | solution.py:31
  144.3 36.0 %collective-permute-start.24 = (f32[3,512,256]{2,1,0:T(8,128)}, f32[3,512,256]{2,1,0:T(8,128)S(1)}, u32[]{:S(2)}, u32[]{:S(2)}) collective-permute-start(f32[3,512,256]{2,1,0:T(8,128)} %get-tuple-element.59), channel_id=1, source_target_pairs={{0,1},{1,0},{2,3},{3,2},{4,5},{5,4},{6,7},{7,6},{8,9},{9,8},{10,11... | collective-permute-start | bytes 4718600 | tf_op jit(solution)/shard_map/ppermute | solution.py:45
  147.4 4.1 %collective-permute-start.22 = (f32[2,2,3]{1,2,0:T(4,128)S(1)}, f32[2,2,3]{1,2,0:T(4,128)S(1)}, u32[]{:S(2)}, u32[]{:S(2)}) collective-permute-start(f32[2,2,3]{1,2,0:T(4,128)S(1)} %copy.51), channel_id=1, source_target_pairs={{0,8},{1,9},{2,10},{3,11},{4,12},{5,13},{6,14},{7,15},{8,0},{9,1},... | collective-permute-start | bytes 152 | tf_op jit(solution)/shard_map/ppermute | solution.py:58
  151.6 6.3 %collective-permute-start.23 = (f32[2,2,3]{1,2,0:T(4,128)S(1)}, f32[2,2,3]{1,2,0:T(4,128)S(1)}, u32[]{:S(2)}, u32[]{:S(2)}) collective-permute-start(f32[2,2,3]{1,2,0:T(4,128)S(1)} %add.87), channel_id=1, source_target_pairs={{0,16},{1,17},{2,18},{3,19},{4,20},{5,21},{6,22},{7,23},{8,24},{9,... | collective-permute-start | bytes 152 | tf_op jit(solution)/shard_map/ppermute | solution.py:58
  161.5 11.6 %all-to-all-start.3 = ((f32[8,2,2,3]{3,2,1,0:T(2,128)}), f32[8,2,2,3]{3,2,1,0:T(2,128)S(1)}, u32[]{:S(2)}, u32[]{:S(2)}) async-start(f32[8,2,2,3]{3,2,1,0:T(2,128)} %broadcast_in_dim.70), calls=%async_computation.3 | async-start | bytes 32768 | tf_op jit(solution)/shard_map/all_to_all | solution.py:63
  173.3 23.2 %all-to-all-start.4 = ((f16[16,72,256]{2,1,0:T(8,128)(2,1)}), f16[16,72,256]{2,1,0:T(8,128)(2,1)}, u32[]{:S(2)}, u32[]{:S(2)}) async-start(f16[16,72,256]{2,1,0:T(8,128)(2,1)} %bitcast.46), calls=%async_computation.4 | async-start | bytes 1179648 | tf_op jit(solution)/shard_map/all_to_all | solution.py:265
  178.7 1.6 copy-start.14
  180.0 0.7 copy-start.16
Sparse Core Ops, SparseCore 0:
  30.9 72.8 all-gather.2

commit v2 on v1

--- a/solution.py
+++ b/solution.py
@@ -13,6 +13,7 @@
 F16 = jnp.float16
 TAIL = 8
 LARGEST = 14.0
+LOW = 256.0
 
 
 def turn(c):
@@ -53,6 +54,26 @@
 RING_Z = [[z * NX + x for z in range(NZ)] for x in range(NX)]
 
 
+def swap_cores(value):
+    return lax.ppermute(value, "tp", [(i, i ^ 1) for i in range(NY * NC)])
+
+
+GROUPS_CZ = [
+    [device(z, x, y, c) for c in range(NC) for z in range(NZ)] for x in range(NX) for y in range(NY)
+]
+GROUPS_Y = [[device(z, x, y, c) for y in range(NY) for c in range(NC)] for z in range(NZ) for x in range(NX)]
+GROUPS_Z = [[device(z, x, y, c) for z in range(NZ)] for x in range(NX) for y in range(NY) for c in range(NC)]
+RING_Z = [[z * NX + x for z in range(NZ)] for x in range(NX)]
+
+
+SWAPS = (
+    (0, 2, 0, 0),
+    (0, 1, 0, 0),
+    (0, 0, 2, 0),
+    (0, 0, 1, 0),
+)
+
+
 def swap(value, dz, dx, dy, dc):
     pairs = [(device(z, x, y, c), device(z ^ dz, x ^ dx, y ^ dy, c ^ dc)) for z, x, y, c in EVERY]
     return lax.ppermute(value, AXES, pairs)
@@ -71,9 +92,10 @@
     return lax.dot_general(a, b, (((0,), (0,)), ((), ())), preferred_element_type=F32)
 
 
-def gram_kernel(place, own, behind, beyond, ahead, cols, out):
+def gram_kernel(place, own, behind, beyond, ahead, cols, *refs):
+    outs, terms = refs[:NX], refs[NX]
     xi, yi, sense = place[0], place[1], 1 - 2 * place[2]
-    rows = out.shape[3] - TAIL
+    rows = terms.shape[2]
     top = None
     for piece, dy in ((own, 0), (behind, -1), (beyond, -2), (ahead, 1)):
         part = lax.dot_general(
@@ -86,29 +108,31 @@
             for x in range(NX):
                 first = (i * NX + x) * rows
                 to = lax.rem((x - xi) * sense + NX, NX)
-                out[to, 0, 2 * y + i, :rows] = part[first : first + rows]
+                terms[to, 2 * y + i] = part[first : first + rows]
     code = jnp.ceil(jnp.log2(jnp.clip(top, 2.0**-100, 2.0**100)))
     factor = jnp.exp2(LARGEST - code)
     tail = jnp.broadcast_to(code, (TAIL, code.shape[1]))
-    for to in range(NX):
+    for to, out in enumerate(outs):
         for z in range(NZ):
-            out[to, 0, z, :rows] = out[to, 0, z, :rows] * factor
-            out[to, 0, z, rows:] = tail
+            out[0, z, :rows] = terms[to, z] * factor
+            out[0, z, rows:] = tail
 
 
 def gram_parts(place, pieces):
     local_rows, wide = pieces[0].shape
     rows, cols = wide * NY // (NX * NZ), wide // NC
     whole = [pl.BlockSpec(piece.shape, lambda i, s: (0, 0)) for piece in pieces]
+    shape = (NC, NZ, rows + TAIL, cols)
     return pl.pallas_call(
         gram_kernel,
         grid_spec=pltpu.PrefetchScalarGridSpec(
             num_scalar_prefetch=1,
             grid=(NC,),
             in_specs=whole + [pl.BlockSpec((local_rows, cols), lambda i, s: (0, i))],
-            out_specs=pl.BlockSpec((NX, 1, NZ, rows + TAIL, cols), lambda i, s: (0, i, 0, 0, 0)),
+            out_specs=[pl.BlockSpec((1,) + shape[1:], lambda i, s: (i, 0, 0, 0))] * NX,
+            scratch_shapes=[pltpu.VMEM((NX, NZ, rows, cols), F32)],
         ),
-        out_shape=jax.ShapeDtypeStruct((NX, NC, NZ, rows + TAIL, cols), F32),
+        out_shape=[jax.ShapeDtypeStruct(shape, F32)] * NX,
         compiler_params=pltpu.CompilerParams(vmem_limit_bytes=32 << 20),
         cost_estimate=pl.CostEstimate(
             flops=2 * local_rows * wide * wide * NY,
@@ -118,46 +142,64 @@
     )(place, *pieces, pieces[0])
 
 
-def add_scaled(*terms):
-    codes = [term[:, :1, -1:] for term in terms]
+def power(code):
+    return jnp.left_shift(1, 30 + jnp.maximum(code, -30.0).astype(jnp.int32)).astype(F32) * 2.0**-30
+
+
+def add_scaled(*terms, note=None):
+    codes = [term[:, :1, -1:].astype(F32) for term in terms]
     code = functools.reduce(jnp.maximum, codes) + (len(terms) - 1)
-    total = sum(term * jnp.exp2(own - code) for term, own in zip(terms, codes))
-    in_tail = lax.broadcasted_iota(jnp.int32, total.shape, 2) >= total.shape[2] - TAIL
-    return jnp.where(in_tail, code, total)
-
-
-def direction_kernel(blocks, place, *refs):
+    total = sum(term.astype(F32) * power(own - code) for term, own in zip(terms, codes))
+    row = lax.broadcasted_iota(jnp.int32, total.shape, 2)
+    rest = code if note is None else jnp.where(row == total.shape[2] - 1, code, note)
+    return jnp.where(row >= total.shape[2] - TAIL, rest, total).astype(F16)
+
+
+def direction_kernel(blocks, place, adagrad, *refs):
     pieces, roots = refs[: NY * blocks], refs[NY * blocks]
-    mine, theirs, squares, whole, root, sems = refs[NY * blocks + 1 :]
+    mine, theirs, note, whole, root, sems = refs[NY * blocks + 1 :]
     xi, yi, ci = place[0], place[1], place[2]
     sense = 1 - 2 * ci
     wide, slab = root.shape[-1], mine.shape[-1]
     copies = []
     for j in range(blocks):
         group = [(roots.at[:, dx, j], root.at[j, :, lax.rem(xi + dx, NX)]) for dx in range(NX)]
-        group += [(pieces[NY * j + k], whole.at[j, k]) for k in range(NY)]
+        for k, dy in enumerate((0, -1, -2, 1)):
+            start = pl.multiple_of(lax.rem(yi + sense * dy + NY, NY) * wide, wide)
+            group.append((pieces[NY * j + k], whole.at[j, :, pl.ds(start, wide)]))
         copies.append(
             [pltpu.make_async_copy(a, b, sems.at[j, i]) for i, (a, b) in enumerate(group)]
         )
-    for group in copies:
-        for copy in group:
-            copy.start()
+    for copy in copies[0]:
+        copy.start()
+    sums = [adagrad[e, j] for e in range(NC) for j in range(blocks)]
     for j in range(blocks):
+        if j + 1 < blocks:
+            for copy in copies[j + 1]:
+                copy.start()
         for copy in copies[j]:
             copy.wait()
-        value = None
-        for k, dy in enumerate((0, -1, -2, 1)):
-            y = lax.rem(yi + sense * dy + NY, NY)
-            b = root[j, pl.ds(2 * y, 2)].reshape(wide, wide)
-            term = jnp.dot(whole[j, k], b, preferred_element_type=F32)
-            value = term if value is None else value + term
+        value = jnp.dot(
+            whole[j], root[j].reshape(NY * wide, wide), preferred_element_type=F32
+        )
         first, second = value[:, :slab], value[:, slab:]
         mine[j] = jnp.where(ci == 0, first, second)
         theirs[j] = jnp.where(ci == 0, second, first)
-        squares[j] = jnp.full((8, 128), jnp.sum(value * value), F32)
-
-
-def direction_of(place, pieces, roots):
+        sums.append(jnp.sum(value * value))
+    lane = lax.broadcasted_iota(jnp.int32, (1, note.shape[1]), 1)
+    line = jnp.zeros(lane.shape, F32)
+    for i, value in enumerate(sums):
+        line = jnp.where(lane == i, value, line)
+    code = jnp.ceil(jnp.log2(jnp.clip(line, 2.0**-100, 2.0**100)))
+    line = line * jnp.exp2(-code)
+    high = line.astype(jnp.bfloat16).astype(F32)
+    rows = note.shape[0] - TAIL
+    note[...] = jnp.zeros(note.shape, F32)
+    for i, value in enumerate((code, high, (line - high) * LOW)):
+        note[rows + i : rows + i + 1] = value
+
+
+def direction_of(place, adagrad_sq, pieces, roots):
     blocks = len(pieces)
     local_rows, wide = pieces[0][0].shape
     rows, slab = roots.shape[3], wide // NC
@@ -165,12 +207,12 @@
     vmem = pl.BlockSpec(memory_space=pltpu.VMEM)
     return pl.pallas_call(
         functools.partial(direction_kernel, blocks),
-        in_specs=[pl.BlockSpec(memory_space=pltpu.SMEM)]
+        in_specs=[pl.BlockSpec(memory_space=pltpu.SMEM)] * 2
         + [pl.BlockSpec(memory_space=pltpu.HBM)] * (NY * blocks + 1),
         out_specs=[vmem, vmem, vmem],
-        out_shape=[result, result, jax.ShapeDtypeStruct((blocks, 8, 128), F32)],
+        out_shape=[result, result, jax.ShapeDtypeStruct((rows + TAIL, slab), F32)],
         scratch_shapes=[
-            pltpu.VMEM((blocks, NY, local_rows, wide), jnp.bfloat16),
+            pltpu.VMEM((blocks, local_rows, NY * wide), jnp.bfloat16),
             pltpu.VMEM((blocks, NZ, NX, rows, wide), jnp.bfloat16),
             pltpu.SemaphoreType.DMA((blocks, NX + NY)),
         ],
@@ -180,7 +222,7 @@
             bytes_accessed=2 * blocks * (local_rows + wide) * wide * NY + 4 * blocks * local_rows * wide,
             transcendentals=0,
         ),
-    )(place, *[piece for group in pieces for piece in group], roots)
+    )(place, adagrad_sq, *[piece for group in pieces for piece in group], roots)
 
 
 def step_kernel(place, scale, kept, given, out):
@@ -239,7 +281,6 @@
     root_pieces = lax.all_gather(root, "fsdp", axis=0, axis_index_groups=RING_Z)
 
     near.append(send_near(after(chip[1], *near[0])))
-    near.append(send_near(after(chip[2], *near[1])))
     gradient = mine.astype(F32)
     adagrad = gradient / (jnp.sqrt(accum.transpose(0, 2, 1, 3) + gradient * gradient) + EPS)
     adagrad_sq = jnp.sum(adagrad * adagrad, axis=(2, 3))
@@ -252,56 +293,54 @@
         return step_x(part[2].astype(F16), 1), step_x(part[3].astype(F16), -1)
 
     def onward(part, arrived):
-        return add_scaled(part[1], arrived[0].astype(F32)).astype(F16)
+        return add_scaled(part[1], arrived[0])
 
     def send_second(value, arrived):
         return step_x(value, 1), arrived[1]
 
-    def owned(part, arrived):
-        return add_scaled(part[0], arrived[0].astype(F32), arrived[1].astype(F32)).astype(F16)
+    def owned(part, arrived, note=None):
+        return add_scaled(part[0], *arrived, note=note)
 
     def send_rows(summed):
-        summed = summed.reshape(NC * NZ, -1, slab)
+        summed = summed.reshape((NC * NZ,) + summed.shape[2:])
         return lax.all_to_all(summed, AXES, 0, 0, axis_index_groups=GROUPS_CZ)
 
     def add_rows(term):
-        term = term.reshape(experts, NZ, -1, slab).astype(F32)
-        factor = jnp.exp2(term[:, :, -1:] - LARGEST)
-        return jnp.sum(term[:, :, :-TAIL] * factor, axis=1) / rows_total
+        term = term.reshape((experts, NZ) + term.shape[1:])
+        factor = jnp.exp2(term[..., -1:, :].astype(F32) - LARGEST)
+        return jnp.sum(term[..., :-TAIL, :].astype(F32) * factor, axis=1) / rows_total
 
     pieces = [collect(0), collect(1)]
-    part0 = gram_parts(after(place, *near[1]), pieces[0])
+    near.append(send_near(after(chip[2], pieces[1][2])))
     pieces.append(collect(2))
+    part0 = gram_parts(after(place, adagrad_sq, *near[1]), pieces[0])
     got0 = send_first(part0)
-    part1 = gram_parts(after(place, part0, *near[2]), pieces[1])
+    part1 = gram_parts(after(place, part0[0]), pieces[1])
     got1 = send_first(part1)
-    value0 = onward(part0, after(got0, part1))
+    value0 = onward(part0, after(got0, part1[0], *near[2]))
     got0 = send_second(value0, got0)
     part2 = gram_parts(after(place, value0), pieces[2])
     got2 = send_first(part2)
-    value1 = onward(part1, after(got1, part2))
+    value1 = onward(part1, after(got1, part2[0]))
     got1 = send_second(value1, got1)
     rows0 = owned(part0, after(got0, value1))
     terms = [send_rows(rows0)]
-    kept_part, given_part, squares = direction_of(after(place, rows0), pieces, root_pieces)
+    kept_part, given_part, note = direction_of(after(place, rows0, *got2), adagrad_sq, pieces, root_pieces)
     given_part = swap_cores(given_part)
-    value2 = onward(part2, after(got2, squares))
+    value2 = onward(part2, after(got2, note))
     got2 = send_second(value2, got2)
-
-    direction_sq = squares[:, 0, 0]
-    none = jnp.zeros_like(direction_sq)
-    direction_sq = jnp.where(
-        first_core, jnp.stack([direction_sq, none]), jnp.stack([none, direction_sq])
-    )
-    sums = after(jnp.stack([adagrad_sq, direction_sq]), terms[0])
-    sums = jnp.sum(spread(sums, GROUPS_Y), axis=0)
-    rows1 = owned(part1, after(got1, value2, sums))
+    rows1 = owned(part1, after(got1, value2), note)
     terms.append(send_rows(rows1))
-    sums = sums + swap(sums, 0, 1, 0, 0)
-    sums = sums + swap(sums, 0, 2, 0, 0)
-    rows2 = owned(part2, after(got2, rows1, sums))
-    sums = jnp.sum(spread(after(sums, terms[1]), GROUPS_Z), axis=0)
-    terms.append(send_rows(after(rows2, sums)))
+    terms[0] = after(terms[0], rows1)
+    sums = terms[1][:, -TAIL : 3 - TAIL].astype(F32)
+    sums = (sums[:, 1] + sums[:, 2] / LOW) * jnp.exp2(sums[:, 0])
+    sums = jnp.sum(sums.reshape(experts, NZ, slab), axis=1)
+    rows2 = owned(part2, after(got2, terms[1]))
+    terms.append(send_rows(rows2))
+    sums = sums + step_x(sums, 1) + step_x(sums, -1) + step_x(sums, 2)
+    sums = sums + step_y(sums, 1) + step_y(sums, -1) + step_y(sums, 2)
+    count = experts * blocks
+    sums = jnp.sum(sums[:, :count], axis=0).reshape(experts, blocks), sums[:, count : count + blocks]
     statistic = jnp.stack([add_rows(term) for term in terms], axis=1)
     graft_scale = jnp.sqrt(sums[0]) / jnp.sqrt(sums[1] + 1e-06)
     step = scaled_step(place, graft_scale, kept_part, given_part)

time: 208 us -> 192 us (0.923)
  local copies, waits for them, and re-layouts: 12.2 us -> 4.48 us
  waiting for transfers between devices: 71.6 us -> 66.7 us
  starting transfers between devices: 60.1 us -> 55.7 us
    ppermute x9 -> x12, waiting for transfers between devices: 0.02 us -> 14.2 us  [step_x(): return lax.ppermute(value, AXES, pairs)]
    all_to_all x2 -> x0, starting transfers between devices: 8.59 us -> none  [spread(): return lax.all_to_all(copies, AXES, 0, 0, axis_index_groups=groups)]
    all_to_all x2 -> x0, waiting for transfers between devices: 6.62 us -> none  [spread(): return lax.all_to_all(copies, AXES, 0, 0, axis_index_groups=groups)]
    all_to_all x3, waiting for transfers between devices: 17.8 us -> 11.9 us  [send_rows(): return lax.all_to_all(summed, AXES, 0, 0, axis_index_groups=GROUPS_CZ)]
    ppermute x2 -> x0, waiting for transfers between devices: 5.73 us -> none  [swap(): return lax.ppermute(value, AXES, pairs)]
    ppermute x2 -> x0, starting transfers between devices: 4.7 us -> none  [swap(): return lax.ppermute(value, AXES, pairs)]
    squeeze x3 -> x0, local copies, waits for them, and re-layouts: 4.61 us -> none  [the longest x1 3.27 us: onward(): return add_scaled(part[1], arrived[0].astype(F32)).astype(F16)]
    convert_element_type x18 -> x13, other arithmetic: 14.6 us -> 11.1 us  [the longest x6 8.68 us: add_scaled(): return jnp.where(row >= total.shape[2] - TAIL, rest, total).astype(F16)]
  transfers between devices with their start and end apart: 31 -> 33, of which waited for: 17 -> 17; matrix products, arithmetic and copies ran while one was open for 13% -> 12% of each run, Pallas kernels for 10% -> 12%
where the time goes in v2:
time: 192 us; the launch traced here: 190 us
  waiting for transfers between devices  66.7 us (35%)
  starting transfers between devices  55.7 us (29%)
  other arithmetic  26.5 us (14%)
  Pallas kernels  22.1 us (12%)
  between operations  14.7 us (8%)
  local copies, waits for them, and re-layouts  4.48 us (2%)
    ppermute x12, waiting for transfers between devices, step_y(): return lax.ppermute(value, 'tp', pairs)  28 us
    all_to_all x3, starting transfers between devices, send_rows(): return lax.all_to_all(summed, AXES, 0, 0, axis_index_groups=GROUPS_CZ)  22 us
    ppermute x12, waiting for transfers between devices, step_x(): return lax.ppermute(value, AXES, pairs)  14.2 us
    ppermute x12, starting transfers between devices, step_y(): return lax.ppermute(value, 'tp', pairs)  13.7 us
    all_to_all x3, waiting for transfers between devices, send_rows(): return lax.all_to_all(summed, AXES, 0, 0, axis_index_groups=GROUPS_CZ)  11.9 us
    ppermute x12, starting transfers between devices, step_x(): return lax.ppermute(value, AXES, pairs)  11.8 us
    ppermute x3, waiting for transfers between devices, shift_x(): return lax.ppermute(value, 'fsdp', pairs)  10.2 us
    pallas_call x3, Pallas kernels, gram_parts(): pl.pallas_call(gram_kernel, grid_spec=pltpu.PrefetchScalarGridSpec(num_sc...  10.1 us
  transfers between devices with their start and end apart: 33, of which 17 were waited for; matrix products, arithmetic and copies ran while one was open for 12% of the time, Pallas kernels for 12%

profile of v2, /device:TPU:32, one launch (start us, length us, event | category | flops | bytes accessed | tf_op | source)
XLA Modules:
  0.0 190.2 jit_solution(4291517122719719318)
XLA Ops:
  7.2 1.5 select_bitcast_fusion
  8.9 2.4 %collective-permute-done = bf16[3,576,256]{2,1,0:T(8,128)(2,1)S(1)} collective-permute-done((bf16[3,576,256]{2,1,0:T(8,128)(2,1)S(1)}, bf16[3,576,256]{2,1,0:T(8,128)(2,1)S(1)}, u32[]{:S(2)}, u32[]{:S(2)}) %collective-permute-start) | collective-permute-done | bytes 884768 | tf_op jit(solution)/shard_map/ppermute | solution.py:58
  11.7 1.7 collective-permute-start.1
  13.4 1.7 collective-permute-start.2
  15.0 2.8 %collective-permute-start.18 = (bf16[3,64,512]{2,1,0:T(8,128)(2,1)S(1)}, bf16[3,64,512]{2,1,0:T(8,128)(2,1)S(1)}, u32[]{:S(2)}, u32[]{:S(2)}) collective-permute-start(bf16[3,64,512]{2,1,0:T(8,128)(2,1)S(1)} %pad_maximum_fusion.6), channel_id=1, source_target_pairs={{0,24},{8,0},{16,8},{24,16},{32,56},{40,32},{48,40},{56,48},{64,88... | collective-permute-start | bytes 589832 | tf_op jit(solution)/shard_map/ppermute | solution.py:42
  17.8 0.8 collective-permute-start.19
  18.6 0.9 collective-permute-start.20
  19.5 6.5 %collective-permute-done.18 = bf16[3,64,512]{2,1,0:T(8,128)(2,1)S(1)} collective-permute-done((bf16[3,64,512]{2,1,0:T(8,128)(2,1)S(1)}, bf16[3,64,512]{2,1,0:T(8,128)(2,1)S(1)}, u32[]{:S(2)}, u32[]{:S(2)}) %collective-permute-start.18) | collective-permute-done | bytes 196640 | tf_op jit(solution)/shard_map/ppermute | solution.py:42
  26.0 1.2 collective-permute-done.19
  27.2 2.5 %collective-permute-done.20 = bf16[3,64,512]{2,1,0:T(8,128)(2,1)S(1)} collective-permute-done((bf16[3,64,512]{2,1,0:T(8,128)(2,1)S(1)}, bf16[3,64,512]{2,1,0:T(8,128)(2,1)S(1)}, u32[]{:S(2)}, u32[]{:S(2)}) %collective-permute-start.20) | collective-permute-done | bytes 196640 | tf_op jit(solution)/shard_map/ppermute | solution.py:42
  29.7 1.1 pad_maximum_fusion.1
  30.8 0.4 collective-permute-start.3
  31.2 2.9 %collective-permute-start.4 = (bf16[512,512]{1,0:T(8,128)(2,1)S(1)}, bf16[512,512]{1,0:T(8,128)(2,1)}, u32[]{:S(2)}, u32[]{:S(2)}) collective-permute-start(bf16[512,512]{1,0:T(8,128)(2,1)S(1)} %get-tuple-element.43.own.cols.refs_4_), channel_id=1, source_target_pairs={{0,6},{1,3},{2,0},{3,5},{4,2},{5,7},{6,4},{7,1},{8,14},{9,11},{10,... | collective-permute-start | bytes 1572872 | tf_op jit(solution)/shard_map/ppermute | solution.py:37
  34.1 11.0 %collective-permute-done.3.behind.refs_5_ = bf16[512,512]{1,0:T(8,128)(2,1)S(1)} collective-permute-done((bf16[512,512]{1,0:T(8,128)(2,1)S(1)}, bf16[512,512]{1,0:T(8,128)(2,1)S(1)}, u32[]{:S(2)}, u32[]{:S(2)}) %collective-permute-start.3) | collective-permute-done | bytes 524320 | tf_op jit(solution)/shard_map/ppermute | solution.py:37
  45.1 4.7 %fusion.4.adagrad = f32[2,3]{1,0:T(2,128)} fusion(f32[2,512,3,256]{3,1,2,0:T(8,128)} %param.4, bf16[2,512,3,256]{3,1,2,0:T(8,128)(2,1)} %param.3), kind=kLoop, calls=%fused_computation.6 | loop fusion | flops 5505018 | bytes 4718616 | tf_op jit(solution)/shard_map/reduce_sum | solution.py:286
  49.9 2.7 %collective-permute-done.5.beyond.refs_2_ = bf16[512,512]{1,0:T(8,128)(2,1)} collective-permute-done((bf16[512,512]{1,0:T(8,128)(2,1)S(1)}, bf16[512,512]{1,0:T(8,128)(2,1)}, u32[]{:S(2)}, u32[]{:S(2)}) %collective-permute-start.5) | collective-permute-done | bytes 524320 | tf_op jit(solution)/shard_map/ppermute | solution.py:37
  52.6 3.7 %shard_map.50 = (f32[2,8,72,256]{3,2,1,0:T(8,128)S(1)}, f32[2,8,72,256]{3,2,1,0:T(8,128)S(1)}, f32[2,8,72,256]{3,2,1,0:T(8,128)S(1)}, f32[2,8,72,256]{3,2,1,0:T(8,128)S(1)}) custom-call(s32[3]{0:T(128)S(1)} %pad_add_fusion.place, bf16[512,512]{1,0:T(8,128)(2,1)S(1)} %get-tuple-element.42.own.cols.refs_0_, ...), custom_call_target="tpu_custom_call" | custom-call | flops 1073741824 | bytes 6291456 | tf_op jit(solution)/shard_map/pallas_call | solution.py:126
  56.6 3.5 %collective-permute-start.7 = (f16[2,8,72,256]{3,2,1,0:T(8,128)(2,1)S(1)}, f16[2,8,72,256]{3,2,1,0:T(8,128)(2,1)S(1)}, u32[]{:S(2)}, u32[]{:S(2)}) collective-permute-start(f16[2,8,72,256]{3,2,1,0:T(8,128)(2,1)S(1)} %convert_element_type.206), channel_id=1, source_target_pairs={{0,24},{1,9},{2,26},{3,11},{4,28},{5,13},{6,30},{7,15},{8,0},{9,17... | collective-permute-start | bytes 1769480 | tf_op jit(solution)/shard_map/ppermute | solution.py:32
  60.1 3.2 %collective-permute-start.10 = (bf16[512,512]{1,0:T(8,128)(2,1)S(1)}, bf16[512,512]{1,0:T(8,128)(2,1)S(1)}, u32[]{:S(2)}, u32[]{:S(2)}) collective-permute-start(bf16[512,512]{1,0:T(8,128)(2,1)S(1)} %pad_maximum_fusion.4.own.cols.refs_8_), channel_id=1, source_target_pairs={{0,6},{1,3},{2,0},{3,5},{4,2},{5,7},{6,4},{7,1},{8,14},{9,11},{10,... | collective-permute-start | bytes 1572872 | tf_op jit(solution)/shard_map/ppermute | solution.py:37
  63.4 3.8 %shard_map.51 = (f32[2,8,72,256]{3,2,1,0:T(8,128)S(1)}, f32[2,8,72,256]{3,2,1,0:T(8,128)S(1)}, f32[2,8,72,256]{3,2,1,0:T(8,128)S(1)}, f32[2,8,72,256]{3,2,1,0:T(8,128)S(1)}) custom-call(s32[3]{0:T(128)S(1)} %pad_add_fusion.place, bf16[512,512]{1,0:T(8,128)(2,1)S(1)} %get-tuple-element.43.own.cols.refs_4_, bf16[512,512]{1,0:T(8,128)(2,1)S(1)} %copy-done.11, ...), custom_call_target="tpu_custom_call" | custom-call | flops 1073741824 | bytes 6291456 | tf_op jit(solution)/shard_map/pallas_call | solution.py:126
  67.5 5.5 %collective-permute-done.6 = f16[2,8,72,256]{3,2,1,0:T(8,128)(2,1)S(1)} collective-permute-done((f16[2,8,72,256]{3,2,1,0:T(8,128)(2,1)S(1)}, f16[2,8,72,256]{3,2,1,0:T(8,128)(2,1)S(1)}, u32[]{:S(2)}, u32[]{:S(2)}) %collective-permute-start.6) | collective-permute-done | bytes 589856 | tf_op jit(solution)/shard_map/ppermute | solution.py:32
  73.2 1.7 collective-permute-done.9.behind.refs_9_
  75.1 0.3 select_convert_fusion.5
  75.6 9.8 %collective-permute-done.14.beyond.refs_10_ = bf16[512,512]{1,0:T(8,128)(2,1)S(1)} collective-permute-done((bf16[512,512]{1,0:T(8,128)(2,1)S(1)}, bf16[512,512]{1,0:T(8,128)(2,1)S(1)}, u32[]{:S(2)}, u32[]{:S(2)}) %collective-permute-start.14) | collective-permute-done | bytes 524320 | tf_op jit(solution)/shard_map/ppermute | solution.py:37
  85.4 2.6 %shard_map.52 = (f32[2,8,72,256]{3,2,1,0:T(8,128)S(1)}, f32[2,8,72,256]{3,2,1,0:T(8,128)S(1)}, f32[2,8,72,256]{3,2,1,0:T(8,128)S(1)}, f32[2,8,72,256]{3,2,1,0:T(8,128)S(1)}) custom-call(s32[3]{0:T(128)S(1)} %pad_add_fusion.place, bf16[512,512]{1,0:T(8,128)(2,1)S(1)} %pad_maximum_fusion.4.own.cols.refs_8_, ...), custom_call_target="tpu_custom_call" | custom-call | flops 1073741824 | bytes 6291456 | tf_op jit(solution)/shard_map/pallas_call | solution.py:126
  88.1 1.1 convert_element_type.234
  89.2 0.9 convert_element_type.235
  90.2 3.1 %collective-permute-start.17 = (f16[2,8,72,256]{3,2,1,0:T(8,128)(2,1)}, f16[2,8,72,256]{3,2,1,0:T(8,128)(2,1)S(1)}, u32[]{:S(2)}, u32[]{:S(2)}) collective-permute-start(f16[2,8,72,256]{3,2,1,0:T(8,128)(2,1)} %convert_element_type.235), channel_id=1, source_target_pairs={{0,24},{1,9},{2,26},{3,11},{4,28},{5,13},{6,30},{7,15},{8,0},{9,17... | collective-permute-start | bytes 1769480 | tf_op jit(solution)/shard_map/ppermute | solution.py:32
  93.4 1.1 select_convert_fusion.4
  94.6 1.3 select_convert_fusion.3
  95.9 8.9 %all-to-all-start = ((f16[16,72,256]{2,1,0:T(8,128)(2,1)}), f16[16,72,256]{2,1,0:T(8,128)(2,1)S(1)}, u32[]{:S(2)}, u32[]{:S(2)}) async-start(f16[16,72,256]{2,1,0:T(8,128)(2,1)} %bitcast.17), calls=%async_computation | async-start | bytes 1179648 | tf_op jit(solution)/shard_map/all_to_all | solution.py:306
  104.8 1.0 collective-permute-done.16
  105.8 1.6 collective-permute-done.17
  107.4 0.8 copy-done.20
  108.2 9.3 %shard_map.53 = (f32[3,512,256]{2,1,0:T(8,128)}, f32[3,512,256]{2,1,0:T(8,128)}, f32[72,256]{1,0:T(8,128)}) custom-call(s32[3]{0:T(128)} %copy-done.15, f32[2,3]{1,0:T(2,128)} %fusion.4.adagrad, bf16[512,512]{1,0:T(8,128)(2,1)} %copy-done.1, bf16[512,512]{1,0:T(8,128)(2,1)} %copy-done.8, bf16[512,512]{1,0:T(8,128)(2,1)} %collective-permute-done.5.beyond.refs_2_, ...), custom_call_target="tpu_custom_call" | custom-call | flops 3221225472 | bytes 15728640 | tf_op jit(solution)/shard_map/pallas_call | solution.py:208
  117.6 1.1 select_convert_fusion.2
  118.7 0.7 convert_multiply_fusion.6
  119.5 0.7 convert_multiply_fusion.5
  120.2 2.3 %select_convert_fusion.1 = f16[2,8,72,256]{3,2,1,0:T(8,128)(2,1)} fusion(f16[2,8,72,256]{3,2,1,0:T(8,128)(2,1)S(1)} %copy-done.22, f16[2,8,72,256]{3,2,1,0:T(8,128)(2,1)} %collective-permute-done.15, f32[2,8,72,256]{3,2,1,0:T(8,128)S(1)} %get-tuple-element.50, f32[2,256]{1,0:T(2,128)S(1)} %bitcast.169, f32[2,256]{1,0:T(2,128)S(1)} %bitcast.170, ...), kind=kLoop, calls=%fused_computation.8 | loop fusion | flops 2949120 | bytes 3031184 | tf_op jit(solution)/shard_map/convert_element_type | solution.py:155
  122.6 0.8 copy-done.18
  123.4 8.9 %all-to-all-start.1 = ((f16[16,72,256]{2,1,0:T(8,128)(2,1)}), f16[16,72,256]{2,1,0:T(8,128)(2,1)S(1)}, u32[]{:S(2)}, u32[]{:S(2)}) async-start(f16[16,72,256]{2,1,0:T(8,128)(2,1)} %bitcast.27), calls=%async_computation.1 | async-start | bytes 1179648 | tf_op jit(solution)/shard_map/all_to_all | solution.py:306
  132.3 0.9 slice.182
  133.1 3.5 %collective-permute-start.28 = (f32[3,512,256]{2,1,0:T(8,128)}, f32[3,512,256]{2,1,0:T(8,128)S(1)}, u32[]{:S(2)}, u32[]{:S(2)}) collective-permute-start(f32[3,512,256]{2,1,0:T(8,128)} %get-tuple-element.79), channel_id=1, source_target_pairs={{0,1},{1,0},{2,3},{3,2},{4,5},{5,4},{6,7},{7,6},{8,9},{9,8},{10,11... | collective-permute-start | bytes 4718600 | tf_op jit(solution)/shard_map/ppermute | solution.py:58
  136.7 1.2 multiply_reduce_fusion.2
  137.9 6.1 %collective-permute-done.21 = f16[2,8,72,256]{3,2,1,0:T(8,128)(2,1)} collective-permute-done((f16[2,8,72,256]{3,2,1,0:T(8,128)(2,1)}, f16[2,8,72,256]{3,2,1,0:T(8,128)(2,1)}, u32[]{:S(2)}, u32[]{:S(2)}) %collective-permute-start.21) | collective-permute-done | bytes 589856 | tf_op jit(solution)/shard_map/ppermute | solution.py:32
  144.0 5.9 %all-to-all-done.1 = f16[16,72,256]{2,1,0:T(8,128)(2,1)S(1)} async-done(((f16[16,72,256]{2,1,0:T(8,128)(2,1)}), f16[16,72,256]{2,1,0:T(8,128)(2,1)S(1)}, u32[]{:S(2)}, u32[]{:S(2)}) %all-to-all-start.1) | async-done | bytes 589856 | tf_op jit(solution)/shard_map/all_to_all | solution.py:306
  150.0 0.8 convert_multiply_fusion.3
  150.8 0.7 convert_multiply_fusion.2
  151.6 1.9 %collective-permute-start.24 = (f32[2,256]{1,0:T(2,128)S(1)}, f32[2,256]{1,0:T(2,128)S(1)}, u32[]{:S(2)}, u32[]{:S(2)}) collective-permute-start(f32[2,256]{1,0:T(2,128)S(1)} %bitcast_reduce_fusion), channel_id=1, source_target_pairs={{0,16},{1,17},{2,18},{3,19},{4,20},{5,21},{6,22},{7,23},{8,24},{9,... | collective-permute-start | bytes 6152 | tf_op jit(solution)/shard_map/ppermute | solution.py:32
  153.5 1.9 collective-permute-start.23
  155.4 0.8 collective-permute-start.22
  156.1 2.5 %select_convert_fusion = f16[2,8,72,256]{3,2,1,0:T(8,128)(2,1)} fusion(f16[2,8,72,256]{3,2,1,0:T(8,128)(2,1)} %copy-done.20, f16[2,8,72,256]{3,2,1,0:T(8,128)(2,1)} %collective-permute-done.21, f32[2,8,72,256]{3,2,1,0:T(8,128)S(1)} %copy-done.5, f32[2,256]{1,0:T(2,128)S(1)} %bitcast.153, f32[2,256]{1,0:T(2,128)S(1)} %bitcast.155, f32[2,256]{1,0:T(2,128)S(1)} %bitcast.160, ...), kind=kLoop, calls=%fused_computation.7 | loop fusion | flops 2654208 | bytes 2957384 | tf_op jit(solution)/shard_map/convert_element_type | solution.py:155
  158.7 4.3 %all-to-all-start.2 = ((f16[16,72,256]{2,1,0:T(8,128)(2,1)}), f16[16,72,256]{2,1,0:T(8,128)(2,1)}, u32[]{:S(2)}, u32[]{:S(2)}) async-start(f16[16,72,256]{2,1,0:T(8,128)(2,1)} %bitcast.142), calls=%async_computation.2 | async-start | bytes 1179648 | tf_op jit(solution)/shard_map/all_to_all | solution.py:306
  163.0 0.9 slice.184
  163.9 1.2 multiply_reduce_fusion.1
  165.1 1.7 collective-permute-start.27
  166.8 2.0 %collective-permute-start.25 = (f32[2,256]{1,0:T(2,128)S(1)}, f32[2,256]{1,0:T(2,128)S(1)}, u32[]{:S(2)}, u32[]{:S(2)}) collective-permute-start(f32[2,256]{1,0:T(2,128)S(1)} %add_add_fusion.1), channel_id=1, source_target_pairs={{0,2},{1,7},{2,4},{3,1},{4,6},{5,3},{6,0},{7,5},{8,10},{9,15},{10,... | collective-permute-start | bytes 6152 | tf_op jit(solution)/shard_map/ppermute | solution.py:37
  168.8 1.4 collective-permute-done.27
  170.4 1.3 collective-permute-done.25
  171.9 2.7 %shard_map.54 = f32[2,3,512,256]{3,2,1,0:T(8,128)} custom-call(s32[3]{0:T(128)S(1)} %copy-done.16, f32[2,3]{1,0:T(2,128)S(1)} %fusion.9.scale, f32[3,512,256]{2,1,0:T(8,128)S(1)} %copy-done.3, f32[3,512,256]{2,1,0:T(8,128)S(1)} %collective-permute-done.28.given), custom_call_target="tpu_custom_call" | custom-call | flops 786432 | bytes 6291456 | tf_op jit(solution)/shard_map/pallas_call | solution.py:236
  174.5 6.0 %all-to-all-done.2 = f16[16,72,256]{2,1,0:T(8,128)(2,1)} async-done(((f16[16,72,256]{2,1,0:T(8,128)(2,1)}), f16[16,72,256]{2,1,0:T(8,128)(2,1)}, u32[]{:S(2)}, u32[]{:S(2)}) %all-to-all-start.2) | async-done | bytes 589856 | tf_op jit(solution)/shard_map/all_to_all | solution.py:306
  180.5 0.9 slice.186
  181.4 1.2 multiply_reduce_fusion
  182.6 0.8 pad_maximum_fusion.5
  (140 shorter events, 2.7 us)
Async XLA Ops:
  7.2 100.2 %all-gather.3.cloned.1.call-start = ((), (), s32[]{:S(2)}) async-start(), calls=%async_computation.3 | async-start | bytes 7077888 | tf_op jit(solution)/shard_map/all_gather | solution.py:281
  7.2 1.5 copy-start.19
  8.8 2.5 %collective-permute-start = (bf16[3,576,256]{2,1,0:T(8,128)(2,1)S(1)}, bf16[3,576,256]{2,1,0:T(8,128)(2,1)S(1)}, u32[]{:S(2)}, u32[]{:S(2)}) collective-permute-start(bf16[3,576,256]{2,1,0:T(8,128)(2,1)S(1)} %pad_maximum_fusion), channel_id=1, source_target_pairs={{0,1},{1,0},{2,3},{3,2},{4,5},{5,4},{6,7},{7,6},{8,9},{9,8},{10,11... | collective-permute-start | bytes 2654216 | tf_op jit(solution)/shard_map/ppermute | solution.py:58
  11.5 73.9 %copy-start = (bf16[512,512]{1,0:T(8,128)(2,1)}, bf16[512,512]{1,0:T(8,128)(2,1)S(1)}, u32[]{:S(2)}) copy-start(bf16[512,512]{1,0:T(8,128)(2,1)S(1)} %pad_maximum_fusion.4.own.cols.refs_8_) | copy-start | bytes 1572868
  11.7 40.9 %copy-start.1 = (bf16[512,512]{1,0:T(8,128)(2,1)}, bf16[512,512]{1,0:T(8,128)(2,1)S(1)}, u32[]{:S(2)}) copy-start(bf16[512,512]{1,0:T(8,128)(2,1)S(1)} %get-tuple-element.42.own.cols.refs_0_) | copy-start | bytes 1572868
  11.7 51.6 %copy-start.2 = (bf16[512,512]{1,0:T(8,128)(2,1)}, bf16[512,512]{1,0:T(8,128)(2,1)S(1)}, u32[]{:S(2)}) copy-start(bf16[512,512]{1,0:T(8,128)(2,1)S(1)} %get-tuple-element.43.own.cols.refs_4_) | copy-start | bytes 1572868
  11.7 18.0 %collective-permute-start.1 = (bf16[512,512]{1,0:T(8,128)(2,1)S(1)}, bf16[512,512]{1,0:T(8,128)(2,1)S(1)}, u32[]{:S(2)}, u32[]{:S(2)}) collective-permute-start(bf16[512,512]{1,0:T(8,128)(2,1)S(1)} %get-tuple-element.42.own.cols.refs_0_), channel_id=1, source_target_pairs={{0,2},{1,7},{2,4},{3,1},{4,6},{5,3},{6,0},{7,5},{8,10},{9,15},{10,... | collective-permute-start | bytes 1572872 | tf_op jit(solution)/shard_map/ppermute | solution.py:37
  13.4 16.3 %collective-permute-start.2 = (bf16[512,512]{1,0:T(8,128)(2,1)S(1)}, bf16[512,512]{1,0:T(8,128)(2,1)S(1)}, u32[]{:S(2)}, u32[]{:S(2)}) collective-permute-start(bf16[512,512]{1,0:T(8,128)(2,1)S(1)} %get-tuple-element.42.own.cols.refs_0_), channel_id=1, source_target_pairs={{0,6},{1,3},{2,0},{3,5},{4,2},{5,7},{6,4},{7,1},{8,14},{9,11},{10,... | collective-permute-start | bytes 1572872 | tf_op jit(solution)/shard_map/ppermute | solution.py:37
  15.0 11.0 %collective-permute-start.18 = (bf16[3,64,512]{2,1,0:T(8,128)(2,1)S(1)}, bf16[3,64,512]{2,1,0:T(8,128)(2,1)S(1)}, u32[]{:S(2)}, u32[]{:S(2)}) collective-permute-start(bf16[3,64,512]{2,1,0:T(8,128)(2,1)S(1)} %pad_maximum_fusion.6), channel_id=1, source_target_pairs={{0,24},{8,0},{16,8},{24,16},{32,56},{40,32},{48,40},{56,48},{64,88... | collective-permute-start | bytes 589832 | tf_op jit(solution)/shard_map/ppermute | solution.py:42
  17.8 9.4 %collective-permute-start.19 = (bf16[3,64,512]{2,1,0:T(8,128)(2,1)S(1)}, bf16[3,64,512]{2,1,0:T(8,128)(2,1)S(1)}, u32[]{:S(2)}, u32[]{:S(2)}) collective-permute-start(bf16[3,64,512]{2,1,0:T(8,128)(2,1)S(1)} %pad_maximum_fusion.6), channel_id=1, source_target_pairs={{0,16},{8,24},{16,0},{24,8},{32,48},{40,56},{48,32},{56,40},{64,80... | collective-permute-start | bytes 589832 | tf_op jit(solution)/shard_map/ppermute | solution.py:42
  18.6 11.1 %collective-permute-start.20 = (bf16[3,64,512]{2,1,0:T(8,128)(2,1)S(1)}, bf16[3,64,512]{2,1,0:T(8,128)(2,1)S(1)}, u32[]{:S(2)}, u32[]{:S(2)}) collective-permute-start(bf16[3,64,512]{2,1,0:T(8,128)(2,1)S(1)} %pad_maximum_fusion.6), channel_id=1, source_target_pairs={{0,8},{8,16},{16,24},{24,0},{32,40},{40,48},{48,56},{56,32},{64,72... | collective-permute-start | bytes 589832 | tf_op jit(solution)/shard_map/ppermute | solution.py:42
  29.7 22.9 %copy-start.8 = (bf16[512,512]{1,0:T(8,128)(2,1)}, bf16[512,512]{1,0:T(8,128)(2,1)S(1)}, u32[]{:S(2)}) copy-start(bf16[512,512]{1,0:T(8,128)(2,1)S(1)} %collective-permute-done.1.behind.refs_1_) | copy-start | bytes 1572868
  29.7 22.9 %copy-start.9 = (bf16[512,512]{1,0:T(8,128)(2,1)}, bf16[512,512]{1,0:T(8,128)(2,1)S(1)}, u32[]{:S(2)}) copy-start(bf16[512,512]{1,0:T(8,128)(2,1)S(1)} %collective-permute-done.2.ahead.refs_3_) | copy-start | bytes 1572868
  30.8 14.3 %collective-permute-start.3 = (bf16[512,512]{1,0:T(8,128)(2,1)S(1)}, bf16[512,512]{1,0:T(8,128)(2,1)S(1)}, u32[]{:S(2)}, u32[]{:S(2)}) collective-permute-start(bf16[512,512]{1,0:T(8,128)(2,1)S(1)} %get-tuple-element.43.own.cols.refs_4_), channel_id=1, source_target_pairs={{0,2},{1,7},{2,4},{3,1},{4,6},{5,3},{6,0},{7,5},{8,10},{9,15},{10,... | collective-permute-start | bytes 1572872 | tf_op jit(solution)/shard_map/ppermute | solution.py:37
  31.2 18.7 %collective-permute-start.4 = (bf16[512,512]{1,0:T(8,128)(2,1)S(1)}, bf16[512,512]{1,0:T(8,128)(2,1)}, u32[]{:S(2)}, u32[]{:S(2)}) collective-permute-start(bf16[512,512]{1,0:T(8,128)(2,1)S(1)} %get-tuple-element.43.own.cols.refs_4_), channel_id=1, source_target_pairs={{0,6},{1,3},{2,0},{3,5},{4,2},{5,7},{6,4},{7,1},{8,14},{9,11},{10,... | collective-permute-start | bytes 1572872 | tf_op jit(solution)/shard_map/ppermute | solution.py:37
  34.1 18.5 %collective-permute-start.5 = (bf16[512,512]{1,0:T(8,128)(2,1)S(1)}, bf16[512,512]{1,0:T(8,128)(2,1)}, u32[]{:S(2)}, u32[]{:S(2)}) collective-permute-start(bf16[512,512]{1,0:T(8,128)(2,1)S(1)} %collective-permute-done.1.behind.refs_1_), channel_id=1, source_target_pairs={{0,2},{1,7},{2,4},{3,1},{4,6},{5,3},{6,0},{7,5},{8,10},{9,15},{10,... | collective-permute-start | bytes 1572872 | tf_op jit(solution)/shard_map/ppermute | solution.py:37
  45.1 4.8 %copy-start.10 = (bf16[512,512]{1,0:T(8,128)(2,1)}, bf16[512,512]{1,0:T(8,128)(2,1)S(1)}, u32[]{:S(2)}) copy-start(bf16[512,512]{1,0:T(8,128)(2,1)S(1)} %collective-permute-done.3.behind.refs_5_) | copy-start | bytes 1572868
  45.1 15.0 %collective-permute-start.8 = (bf16[512,512]{1,0:T(8,128)(2,1)S(1)}, bf16[512,512]{1,0:T(8,128)(2,1)}, u32[]{:S(2)}, u32[]{:S(2)}) collective-permute-start(bf16[512,512]{1,0:T(8,128)(2,1)S(1)} %collective-permute-done.3.behind.refs_5_), channel_id=1, source_target_pairs={{0,2},{1,7},{2,4},{3,1},{4,6},{5,3},{6,0},{7,5},{8,10},{9,15},{10,... | collective-permute-start | bytes 1572872 | tf_op jit(solution)/shard_map/ppermute | solution.py:37
  49.9 35.5 %copy-start.15 = (s32[3]{0:T(128)}, s32[3]{0:T(128)S(1)}, u32[]{:S(2)}) copy-start(s32[3]{0:T(128)S(1)} %pad_add_fusion.place) | copy-start | bytes 40
  56.4 6.9 %copy-start.11 = (bf16[512,512]{1,0:T(8,128)(2,1)S(1)}, bf16[512,512]{1,0:T(8,128)(2,1)}, u32[]{:S(2)}) copy-start(bf16[512,512]{1,0:T(8,128)(2,1)} %copy-done.10) | copy-start | bytes 1572868
  56.4 16.6 %collective-permute-start.6 = (f16[2,8,72,256]{3,2,1,0:T(8,128)(2,1)S(1)}, f16[2,8,72,256]{3,2,1,0:T(8,128)(2,1)S(1)}, u32[]{:S(2)}, u32[]{:S(2)}) collective-permute-start(f16[2,8,72,256]{3,2,1,0:T(8,128)(2,1)S(1)} %convert_element_type.205), channel_id=1, source_target_pairs={{0,8},{1,25},{2,10},{3,27},{4,12},{5,29},{6,14},{7,31},{8,16},{9,1... | collective-permute-start | bytes 1769480 | tf_op jit(solution)/shard_map/ppermute | solution.py:32
  56.6 16.6 %collective-permute-start.7 = (f16[2,8,72,256]{3,2,1,0:T(8,128)(2,1)S(1)}, f16[2,8,72,256]{3,2,1,0:T(8,128)(2,1)S(1)}, u32[]{:S(2)}, u32[]{:S(2)}) collective-permute-start(f16[2,8,72,256]{3,2,1,0:T(8,128)(2,1)S(1)} %convert_element_type.206), channel_id=1, source_target_pairs={{0,24},{1,9},{2,26},{3,11},{4,28},{5,13},{6,30},{7,15},{8,0},{9,17... | collective-permute-start | bytes 1769480 | tf_op jit(solution)/shard_map/ppermute | solution.py:32
  60.1 14.8 %collective-permute-start.9 = (bf16[512,512]{1,0:T(8,128)(2,1)S(1)}, bf16[512,512]{1,0:T(8,128)(2,1)S(1)}, u32[]{:S(2)}, u32[]{:S(2)}) collective-permute-start(bf16[512,512]{1,0:T(8,128)(2,1)S(1)} %pad_maximum_fusion.4.own.cols.refs_8_), channel_id=1, source_target_pairs={{0,2},{1,7},{2,4},{3,1},{4,6},{5,3},{6,0},{7,5},{8,10},{9,15},{10,... | collective-permute-start | bytes 1572872 | tf_op jit(solution)/shard_map/ppermute | solution.py:37
  60.1 14.8 %collective-permute-start.10 = (bf16[512,512]{1,0:T(8,128)(2,1)S(1)}, bf16[512,512]{1,0:T(8,128)(2,1)S(1)}, u32[]{:S(2)}, u32[]{:S(2)}) collective-permute-start(bf16[512,512]{1,0:T(8,128)(2,1)S(1)} %pad_maximum_fusion.4.own.cols.refs_8_), channel_id=1, source_target_pairs={{0,6},{1,3},{2,0},{3,5},{4,2},{5,7},{6,4},{7,1},{8,14},{9,11},{10,... | collective-permute-start | bytes 1572872 | tf_op jit(solution)/shard_map/ppermute | solution.py:37
  67.3 26.0 %collective-permute-start.12 = (f16[2,8,72,256]{3,2,1,0:T(8,128)(2,1)S(1)}, f16[2,8,72,256]{3,2,1,0:T(8,128)(2,1)S(1)}, u32[]{:S(2)}, u32[]{:S(2)}) collective-permute-start(f16[2,8,72,256]{3,2,1,0:T(8,128)(2,1)S(1)} %convert_element_type.214), channel_id=1, source_target_pairs={{0,8},{1,25},{2,10},{3,27},{4,12},{5,29},{6,14},{7,31},{8,16},{9,1... | collective-permute-start | bytes 1769480 | tf_op jit(solution)/shard_map/ppermute | solution.py:32
  73.0 20.3 %collective-permute-start.13 = (f16[2,8,72,256]{3,2,1,0:T(8,128)(2,1)S(1)}, f16[2,8,72,256]{3,2,1,0:T(8,128)(2,1)S(1)}, u32[]{:S(2)}, u32[]{:S(2)}) collective-permute-start(f16[2,8,72,256]{3,2,1,0:T(8,128)(2,1)S(1)} %convert_element_type.215), channel_id=1, source_target_pairs={{0,24},{1,9},{2,26},{3,11},{4,28},{5,13},{6,30},{7,15},{8,0},{9,17... | collective-permute-start | bytes 1769480 | tf_op jit(solution)/shard_map/ppermute | solution.py:32
  74.9 10.5 %copy-start.12 = (bf16[512,512]{1,0:T(8,128)(2,1)}, bf16[512,512]{1,0:T(8,128)(2,1)S(1)}, u32[]{:S(2)}) copy-start(bf16[512,512]{1,0:T(8,128)(2,1)S(1)} %collective-permute-done.9.behind.refs_9_) | copy-start | bytes 1572868
  74.9 10.5 %copy-start.13 = (bf16[512,512]{1,0:T(8,128)(2,1)}, bf16[512,512]{1,0:T(8,128)(2,1)S(1)}, u32[]{:S(2)}) copy-start(bf16[512,512]{1,0:T(8,128)(2,1)S(1)} %collective-permute-done.10.ahead.refs_11_) | copy-start | bytes 1572868
  74.9 10.5 %collective-permute-start.14 = (bf16[512,512]{1,0:T(8,128)(2,1)S(1)}, bf16[512,512]{1,0:T(8,128)(2,1)S(1)}, u32[]{:S(2)}, u32[]{:S(2)}) collective-permute-start(bf16[512,512]{1,0:T(8,128)(2,1)S(1)} %collective-permute-done.9.behind.refs_9_), channel_id=1, source_target_pairs={{0,2},{1,7},{2,4},{3,1},{4,6},{5,3},{6,0},{7,5},{8,10},{9,15},{10,... | collective-permute-start | bytes 1572872 | tf_op jit(solution)/shard_map/ppermute | solution.py:37
  75.4 19.1 %collective-permute-start.11 = (f16[2,8,72,256]{3,2,1,0:T(8,128)(2,1)S(1)}, f16[2,8,72,256]{3,2,1,0:T(8,128)(2,1)S(1)}, u32[]{:S(2)}, u32[]{:S(2)}) collective-permute-start(f16[2,8,72,256]{3,2,1,0:T(8,128)(2,1)S(1)} %select_convert_fusion.5), channel_id=1, source_target_pairs={{0,8},{1,25},{2,10},{3,27},{4,12},{5,29},{6,14},{7,31},{8,16},{9,1... | collective-permute-start | bytes 1769480 | tf_op jit(solution)/shard_map/ppermute | solution.py:32
  85.4 2.6 %copy-start.14 = (bf16[512,512]{1,0:T(8,128)(2,1)}, bf16[512,512]{1,0:T(8,128)(2,1)S(1)}, u32[]{:S(2)}) copy-start(bf16[512,512]{1,0:T(8,128)(2,1)S(1)} %collective-permute-done.14.beyond.refs_10_) | copy-start | bytes 1572868
  88.0 2.1 %copy-start.4 = (f32[2,8,72,256]{3,2,1,0:T(8,128)}, f32[2,8,72,256]{3,2,1,0:T(8,128)S(1)}, u32[]{:S(2)}) copy-start(f32[2,8,72,256]{3,2,1,0:T(8,128)S(1)} %get-tuple-element.58) | copy-start | bytes 3538948
  88.1 2.1 %copy-start.6 = (f32[2,8,72,256]{3,2,1,0:T(8,128)}, f32[2,8,72,256]{3,2,1,0:T(8,128)S(1)}, u32[]{:S(2)}) copy-start(f32[2,8,72,256]{3,2,1,0:T(8,128)S(1)} %get-tuple-element.62) | copy-start | bytes 3538948
  89.1 16.7 %collective-permute-start.16 = (f16[2,8,72,256]{3,2,1,0:T(8,128)(2,1)}, f16[2,8,72,256]{3,2,1,0:T(8,128)(2,1)S(1)}, u32[]{:S(2)}, u32[]{:S(2)}) collective-permute-start(f16[2,8,72,256]{3,2,1,0:T(8,128)(2,1)} %convert_element_type.234), channel_id=1, source_target_pairs={{0,8},{1,25},{2,10},{3,27},{4,12},{5,29},{6,14},{7,31},{8,16},{9,1... | collective-permute-start | bytes 1769480 | tf_op jit(solution)/shard_map/ppermute | solution.py:32
  90.2 17.2 %collective-permute-start.17 = (f16[2,8,72,256]{3,2,1,0:T(8,128)(2,1)}, f16[2,8,72,256]{3,2,1,0:T(8,128)(2,1)S(1)}, u32[]{:S(2)}, u32[]{:S(2)}) collective-permute-start(f16[2,8,72,256]{3,2,1,0:T(8,128)(2,1)} %convert_element_type.235), channel_id=1, source_target_pairs={{0,24},{1,9},{2,26},{3,11},{4,28},{5,13},{6,30},{7,15},{8,0},{9,17... | collective-permute-start | bytes 1769480 | tf_op jit(solution)/shard_map/ppermute | solution.py:32
  93.3 1.2 copy-start.21
  94.5 24.2 %collective-permute-start.15 = (f16[2,8,72,256]{3,2,1,0:T(8,128)(2,1)}, f16[2,8,72,256]{3,2,1,0:T(8,128)(2,1)}, u32[]{:S(2)}, u32[]{:S(2)}) collective-permute-start(f16[2,8,72,256]{3,2,1,0:T(8,128)(2,1)} %select_convert_fusion.4), channel_id=1, source_target_pairs={{0,8},{1,25},{2,10},{3,27},{4,12},{5,29},{6,14},{7,31},{8,16},{9,1... | collective-permute-start | bytes 1769480 | tf_op jit(solution)/shard_map/ppermute | solution.py:32
  95.9 26.6 %all-to-all-start = ((f16[16,72,256]{2,1,0:T(8,128)(2,1)}), f16[16,72,256]{2,1,0:T(8,128)(2,1)S(1)}, u32[]{:S(2)}, u32[]{:S(2)}) async-start(f16[16,72,256]{2,1,0:T(8,128)(2,1)} %bitcast.17), calls=%async_computation | async-start | bytes 1179648 | tf_op jit(solution)/shard_map/all_to_all | solution.py:306
  105.8 1.6 copy-start.23
  107.4 0.8 copy-start.20
  108.2 9.3 %copy-start.7 = (f32[2,8,72,256]{3,2,1,0:T(8,128)S(1)}, f32[2,8,72,256]{3,2,1,0:T(8,128)}, u32[]{:S(2)}) copy-start(f32[2,8,72,256]{3,2,1,0:T(8,128)} %copy-done.6) | copy-start | bytes 3538948
  108.2 9.3 %copy-start.24 = (f16[2,8,72,256]{3,2,1,0:T(8,128)(2,1)S(1)}, f16[2,8,72,256]{3,2,1,0:T(8,128)(2,1)}, u32[]{:S(2)}) copy-start(f16[2,8,72,256]{3,2,1,0:T(8,128)(2,1)} %copy-done.23) | copy-start | bytes 1769476
  117.6 1.1 copy-start.22
  117.6 2.6 %copy-start.25 = (f32[72,256]{1,0:T(8,128)S(1)}, f32[72,256]{1,0:T(8,128)}, u32[]{:S(2)}) copy-start(f32[72,256]{1,0:T(8,128)} %get-tuple-element.71) | copy-start | bytes 221188
  122.5 27.4 %copy-start.5 = (f32[2,8,72,256]{3,2,1,0:T(8,128)S(1)}, f32[2,8,72,256]{3,2,1,0:T(8,128)}, u32[]{:S(2)}) copy-start(f32[2,8,72,256]{3,2,1,0:T(8,128)} %copy-done.4) | copy-start | bytes 3538948
  122.6 0.8 copy-start.18
  123.4 26.6 %all-to-all-start.1 = ((f16[16,72,256]{2,1,0:T(8,128)(2,1)}), f16[16,72,256]{2,1,0:T(8,128)(2,1)S(1)}, u32[]{:S(2)}, u32[]{:S(2)}) async-start(f16[16,72,256]{2,1,0:T(8,128)(2,1)} %bitcast.27), calls=%async_computation.1 | async-start | bytes 1179648 | tf_op jit(solution)/shard_map/all_to_all | solution.py:306
  132.3 11.8 %collective-permute-start.21 = (f16[2,8,72,256]{3,2,1,0:T(8,128)(2,1)}, f16[2,8,72,256]{3,2,1,0:T(8,128)(2,1)}, u32[]{:S(2)}, u32[]{:S(2)}) collective-permute-start(f16[2,8,72,256]{3,2,1,0:T(8,128)(2,1)} %select_convert_fusion.2), channel_id=1, source_target_pairs={{0,8},{1,25},{2,10},{3,27},{4,12},{5,29},{6,14},{7,31},{8,16},{9,1... | collective-permute-start | bytes 1769480 | tf_op jit(solution)/shard_map/ppermute | solution.py:32
  133.1 38.7 %collective-permute-start.28 = (f32[3,512,256]{2,1,0:T(8,128)}, f32[3,512,256]{2,1,0:T(8,128)S(1)}, u32[]{:S(2)}, u32[]{:S(2)}) collective-permute-start(f32[3,512,256]{2,1,0:T(8,128)} %get-tuple-element.79), channel_id=1, source_target_pairs={{0,1},{1,0},{2,3},{3,2},{4,5},{5,4},{6,7},{7,6},{8,9},{9,8},{10,11... | collective-permute-start | bytes 4718600 | tf_op jit(solution)/shard_map/ppermute | solution.py:58
  150.0 6.2 %copy-start.17 = (f16[16,72,256]{2,1,0:T(8,128)(2,1)}, f16[16,72,256]{2,1,0:T(8,128)(2,1)S(1)}, u32[]{:S(2)}) copy-start(f16[16,72,256]{2,1,0:T(8,128)(2,1)S(1)} %all-to-all-done.1) | copy-start | bytes 1769476
  151.6 13.4 %collective-permute-start.24 = (f32[2,256]{1,0:T(2,128)S(1)}, f32[2,256]{1,0:T(2,128)S(1)}, u32[]{:S(2)}, u32[]{:S(2)}) collective-permute-start(f32[2,256]{1,0:T(2,128)S(1)} %bitcast_reduce_fusion), channel_id=1, source_target_pairs={{0,16},{1,17},{2,18},{3,19},{4,20},{5,21},{6,22},{7,23},{8,24},{9,... | collective-permute-start | bytes 6152 | tf_op jit(solution)/shard_map/ppermute | solution.py:32
  153.5 11.5 %collective-permute-start.23 = (f32[2,256]{1,0:T(2,128)S(1)}, f32[2,256]{1,0:T(2,128)S(1)}, u32[]{:S(2)}, u32[]{:S(2)}) collective-permute-start(f32[2,256]{1,0:T(2,128)S(1)} %bitcast_reduce_fusion), channel_id=1, source_target_pairs={{0,24},{1,9},{2,26},{3,11},{4,28},{5,13},{6,30},{7,15},{8,0},{9,17... | collective-permute-start | bytes 6152 | tf_op jit(solution)/shard_map/ppermute | solution.py:32
  155.4 9.7 %collective-permute-start.22 = (f32[2,256]{1,0:T(2,128)S(1)}, f32[2,256]{1,0:T(2,128)S(1)}, u32[]{:S(2)}, u32[]{:S(2)}) collective-permute-start(f32[2,256]{1,0:T(2,128)S(1)} %bitcast_reduce_fusion), channel_id=1, source_target_pairs={{0,8},{1,25},{2,10},{3,27},{4,12},{5,29},{6,14},{7,31},{8,16},{9,1... | collective-permute-start | bytes 6152 | tf_op jit(solution)/shard_map/ppermute | solution.py:32
  158.7 13.2 %copy-start.3 = (f32[3,512,256]{2,1,0:T(8,128)S(1)}, f32[3,512,256]{2,1,0:T(8,128)}, u32[]{:S(2)}) copy-start(f32[3,512,256]{2,1,0:T(8,128)} %get-tuple-element.78.kept) | copy-start | bytes 4718596
  158.7 13.2 %copy-start.16 = (s32[3]{0:T(128)S(1)}, s32[3]{0:T(128)}, u32[]{:S(2)}) copy-start(s32[3]{0:T(128)} %copy-done.15) | copy-start | bytes 40
  158.7 21.9 %all-to-all-start.2 = ((f16[16,72,256]{2,1,0:T(8,128)(2,1)}), f16[16,72,256]{2,1,0:T(8,128)(2,1)}, u32[]{:S(2)}, u32[]{:S(2)}) async-start(f16[16,72,256]{2,1,0:T(8,128)(2,1)} %bitcast.142), calls=%async_computation.2 | async-start | bytes 1179648 | tf_op jit(solution)/shard_map/all_to_all | solution.py:306
  165.1 5.2 %collective-permute-start.27 = (f32[2,256]{1,0:T(2,128)S(1)}, f32[2,256]{1,0:T(2,128)S(1)}, u32[]{:S(2)}, u32[]{:S(2)}) collective-permute-start(f32[2,256]{1,0:T(2,128)S(1)} %add_add_fusion.1), channel_id=1, source_target_pairs={{0,4},{1,5},{2,6},{3,7},{4,0},{5,1},{6,2},{7,3},{8,12},{9,13},{10,... | collective-permute-start | bytes 6152 | tf_op jit(solution)/shard_map/ppermute | solution.py:37
  166.8 3.6 %collective-permute-start.26 = (f32[2,256]{1,0:T(2,128)S(1)}, f32[2,256]{1,0:T(2,128)S(1)}, u32[]{:S(2)}, u32[]{:S(2)}) collective-permute-start(f32[2,256]{1,0:T(2,128)S(1)} %add_add_fusion.1), channel_id=1, source_target_pairs={{0,6},{1,3},{2,0},{3,5},{4,2},{5,7},{6,4},{7,1},{8,14},{9,11},{10,... | collective-permute-start | bytes 6152 | tf_op jit(solution)/shard_map/ppermute | solution.py:37
  166.8 4.8 %collective-permute-start.25 = (f32[2,256]{1,0:T(2,128)S(1)}, f32[2,256]{1,0:T(2,128)S(1)}, u32[]{:S(2)}, u32[]{:S(2)}) collective-permute-start(f32[2,256]{1,0:T(2,128)S(1)} %add_add_fusion.1), channel_id=1, source_target_pairs={{0,2},{1,7},{2,4},{3,1},{4,6},{5,3},{6,0},{7,5},{8,10},{9,15},{10,... | collective-permute-start | bytes 6152 | tf_op jit(solution)/shard_map/ppermute | solution.py:37
Sparse Core Ops, SparseCore 0:
  30.9 72.8 all-gather.2

commit v3 on v2

--- a/solution.py
+++ b/solution.py
@@ -308,7 +308,7 @@
     def add_rows(term):
         term = term.reshape((experts, NZ) + term.shape[1:])
         factor = jnp.exp2(term[..., -1:, :].astype(F32) - LARGEST)
-        return jnp.sum(term[..., :-TAIL, :].astype(F32) * factor, axis=1) / rows_total
+        return (jnp.sum(term.astype(F32) * factor, axis=1) / rows_total)[..., :-TAIL, :]
 
     pieces = [collect(0), collect(1)]
     near.append(send_near(after(chip[2], pieces[1][2])))
@@ -335,8 +335,8 @@
     sums = terms[1][:, -TAIL : 3 - TAIL].astype(F32)
     sums = (sums[:, 1] + sums[:, 2] / LOW) * jnp.exp2(sums[:, 0])
     sums = jnp.sum(sums.reshape(experts, NZ, slab), axis=1)
-    rows2 = owned(part2, after(got2, terms[1]))
-    terms.append(send_rows(rows2))
+    rows2 = owned(part2, after(got2, rows1))
+    terms.append(send_rows(after(rows2, terms[1])))
     sums = sums + step_x(sums, 1) + step_x(sums, -1) + step_x(sums, 2)
     sums = sums + step_y(sums, 1) + step_y(sums, -1) + step_y(sums, 2)
     count = experts * blocks

time: 192 us -> 191 us (level)
  starting transfers between devices: 55.7 us -> 53.3 us
    ppermute x12, waiting for transfers between devices: 14.2 us -> 8.11 us  [step_x(): return lax.ppermute(value, AXES, pairs)]
    all_to_all x3, waiting for transfers between devices: 11.9 us -> 16.9 us  [send_rows(): return lax.all_to_all(summed, AXES, 0, 0, axis_index_groups=GROUPS_CZ)]
    ppermute x2, starting transfers between devices: 3.62 us -> 0.33 us  [swap_cores(): return lax.ppermute(value, 'tp', [(i, i ^ 1) for i in range(NY * NC)])]
    ppermute x12, starting transfers between devices: 11.8 us -> 14.6 us  [step_x(): return lax.ppermute(value, AXES, pairs)]
  transfers between devices with their start and end apart: 33 -> 33, of which waited for: 17 -> 15; matrix products, arithmetic and copies ran while one was open for 12% -> 13% of each run, Pallas kernels for 12% -> 12%
where the time goes in v3:
time: 191 us; the launch traced here: 190 us
  waiting for transfers between devices  66.9 us (35%)
  starting transfers between devices  53.3 us (28%)
  other arithmetic  27.2 us (14%)
  Pallas kernels  22.1 us (12%)
  between operations  14.8 us (8%)
  local copies, waits for them, and re-layouts  5.28 us (3%)
    ppermute x12, waiting for transfers between devices, step_y(): return lax.ppermute(value, 'tp', pairs)  29.3 us
    all_to_all x3, starting transfers between devices, send_rows(): return lax.all_to_all(summed, AXES, 0, 0, axis_index_groups=GROUPS_CZ)  21.8 us
    all_to_all x3, waiting for transfers between devices, send_rows(): return lax.all_to_all(summed, AXES, 0, 0, axis_index_groups=GROUPS_CZ)  16.9 us
    ppermute x12, starting transfers between devices, step_x(): return lax.ppermute(value, AXES, pairs)  14.6 us
    ppermute x12, starting transfers between devices, step_y(): return lax.ppermute(value, 'tp', pairs)  12.1 us
    ppermute x3, waiting for transfers between devices, shift_x(): return lax.ppermute(value, 'fsdp', pairs)  10.2 us
    pallas_call x3, Pallas kernels, gram_parts(): pl.pallas_call(gram_kernel, grid_spec=pltpu.PrefetchScalarGridSpec(num_sc...  10.1 us
    pallas_call x1, Pallas kernels, direction_of(): pl.pallas_call(functools.partial(direction_kernel, blocks), in_specs=[pl....  9.28 us
  transfers between devices with their start and end apart: 33, of which 15 were waited for; matrix products, arithmetic and copies ran while one was open for 13% of the time, Pallas kernels for 12%

profile of v3, /device:TPU:32, one launch (start us, length us, event | category | flops | bytes accessed | tf_op | source)
XLA Modules:
  0.0 189.6 jit_solution(12687782255407607296)
XLA Ops:
  7.2 1.5 select_bitcast_fusion
  8.9 2.4 %collective-permute-done = bf16[3,576,256]{2,1,0:T(8,128)(2,1)S(1)} collective-permute-done((bf16[3,576,256]{2,1,0:T(8,128)(2,1)S(1)}, bf16[3,576,256]{2,1,0:T(8,128)(2,1)S(1)}, u32[]{:S(2)}, u32[]{:S(2)}) %collective-permute-start) | collective-permute-done | bytes 884768 | tf_op jit(solution)/shard_map/ppermute | solution.py:58
  11.7 1.7 collective-permute-start.1
  13.4 1.7 collective-permute-start.2
  15.0 2.8 %collective-permute-start.18 = (bf16[3,64,512]{2,1,0:T(8,128)(2,1)S(1)}, bf16[3,64,512]{2,1,0:T(8,128)(2,1)S(1)}, u32[]{:S(2)}, u32[]{:S(2)}) collective-permute-start(bf16[3,64,512]{2,1,0:T(8,128)(2,1)S(1)} %pad_maximum_fusion.6), channel_id=1, source_target_pairs={{0,24},{8,0},{16,8},{24,16},{32,56},{40,32},{48,40},{56,48},{64,88... | collective-permute-start | bytes 589832 | tf_op jit(solution)/shard_map/ppermute | solution.py:42
  17.8 0.8 collective-permute-start.19
  18.6 0.9 collective-permute-start.20
  19.5 6.5 %collective-permute-done.18 = bf16[3,64,512]{2,1,0:T(8,128)(2,1)S(1)} collective-permute-done((bf16[3,64,512]{2,1,0:T(8,128)(2,1)S(1)}, bf16[3,64,512]{2,1,0:T(8,128)(2,1)S(1)}, u32[]{:S(2)}, u32[]{:S(2)}) %collective-permute-start.18) | collective-permute-done | bytes 196640 | tf_op jit(solution)/shard_map/ppermute | solution.py:42
  26.0 1.2 collective-permute-done.19
  27.2 2.5 %collective-permute-done.20 = bf16[3,64,512]{2,1,0:T(8,128)(2,1)S(1)} collective-permute-done((bf16[3,64,512]{2,1,0:T(8,128)(2,1)S(1)}, bf16[3,64,512]{2,1,0:T(8,128)(2,1)S(1)}, u32[]{:S(2)}, u32[]{:S(2)}) %collective-permute-start.20) | collective-permute-done | bytes 196640 | tf_op jit(solution)/shard_map/ppermute | solution.py:42
  29.7 1.1 pad_maximum_fusion.1
  30.8 0.4 collective-permute-start.3
  31.2 2.9 %collective-permute-start.4 = (bf16[512,512]{1,0:T(8,128)(2,1)S(1)}, bf16[512,512]{1,0:T(8,128)(2,1)}, u32[]{:S(2)}, u32[]{:S(2)}) collective-permute-start(bf16[512,512]{1,0:T(8,128)(2,1)S(1)} %get-tuple-element.44.own.cols.refs_4_), channel_id=1, source_target_pairs={{0,6},{1,3},{2,0},{3,5},{4,2},{5,7},{6,4},{7,1},{8,14},{9,11},{10,... | collective-permute-start | bytes 1572872 | tf_op jit(solution)/shard_map/ppermute | solution.py:37
  34.1 11.0 %collective-permute-done.3.behind.refs_5_ = bf16[512,512]{1,0:T(8,128)(2,1)S(1)} collective-permute-done((bf16[512,512]{1,0:T(8,128)(2,1)S(1)}, bf16[512,512]{1,0:T(8,128)(2,1)S(1)}, u32[]{:S(2)}, u32[]{:S(2)}) %collective-permute-start.3) | collective-permute-done | bytes 524320 | tf_op jit(solution)/shard_map/ppermute | solution.py:37
  45.1 4.8 %fusion.4.adagrad = f32[2,3]{1,0:T(2,128)} fusion(f32[2,512,3,256]{3,1,2,0:T(8,128)} %param.4, bf16[2,512,3,256]{3,1,2,0:T(8,128)(2,1)} %param.3), kind=kLoop, calls=%fused_computation.6 | loop fusion | flops 5505018 | bytes 4718616 | tf_op jit(solution)/shard_map/reduce_sum | solution.py:286
  49.9 2.7 %collective-permute-done.5.beyond.refs_2_ = bf16[512,512]{1,0:T(8,128)(2,1)} collective-permute-done((bf16[512,512]{1,0:T(8,128)(2,1)S(1)}, bf16[512,512]{1,0:T(8,128)(2,1)}, u32[]{:S(2)}, u32[]{:S(2)}) %collective-permute-start.5) | collective-permute-done | bytes 524320 | tf_op jit(solution)/shard_map/ppermute | solution.py:37
  52.6 3.7 %shard_map.50 = (f32[2,8,72,256]{3,2,1,0:T(8,128)S(1)}, f32[2,8,72,256]{3,2,1,0:T(8,128)S(1)}, f32[2,8,72,256]{3,2,1,0:T(8,128)S(1)}, f32[2,8,72,256]{3,2,1,0:T(8,128)S(1)}) custom-call(s32[3]{0:T(128)S(1)} %pad_add_fusion.place, bf16[512,512]{1,0:T(8,128)(2,1)S(1)} %get-tuple-element.43.own.cols.refs_0_, ...), custom_call_target="tpu_custom_call" | custom-call | flops 1073741824 | bytes 6291456 | tf_op jit(solution)/shard_map/pallas_call | solution.py:126
  56.6 3.5 %collective-permute-start.7 = (f16[2,8,72,256]{3,2,1,0:T(8,128)(2,1)S(1)}, f16[2,8,72,256]{3,2,1,0:T(8,128)(2,1)S(1)}, u32[]{:S(2)}, u32[]{:S(2)}) collective-permute-start(f16[2,8,72,256]{3,2,1,0:T(8,128)(2,1)S(1)} %convert_element_type.206), channel_id=1, source_target_pairs={{0,24},{1,9},{2,26},{3,11},{4,28},{5,13},{6,30},{7,15},{8,0},{9,17... | collective-permute-start | bytes 1769480 | tf_op jit(solution)/shard_map/ppermute | solution.py:32
  60.1 3.2 %collective-permute-start.10 = (bf16[512,512]{1,0:T(8,128)(2,1)S(1)}, bf16[512,512]{1,0:T(8,128)(2,1)S(1)}, u32[]{:S(2)}, u32[]{:S(2)}) collective-permute-start(bf16[512,512]{1,0:T(8,128)(2,1)S(1)} %pad_maximum_fusion.4.own.cols.refs_8_), channel_id=1, source_target_pairs={{0,6},{1,3},{2,0},{3,5},{4,2},{5,7},{6,4},{7,1},{8,14},{9,11},{10,... | collective-permute-start | bytes 1572872 | tf_op jit(solution)/shard_map/ppermute | solution.py:37
  63.3 3.8 %shard_map.51 = (f32[2,8,72,256]{3,2,1,0:T(8,128)S(1)}, f32[2,8,72,256]{3,2,1,0:T(8,128)S(1)}, f32[2,8,72,256]{3,2,1,0:T(8,128)S(1)}, f32[2,8,72,256]{3,2,1,0:T(8,128)S(1)}) custom-call(s32[3]{0:T(128)S(1)} %pad_add_fusion.place, bf16[512,512]{1,0:T(8,128)(2,1)S(1)} %get-tuple-element.44.own.cols.refs_4_, bf16[512,512]{1,0:T(8,128)(2,1)S(1)} %copy-done.11, ...), custom_call_target="tpu_custom_call" | custom-call | flops 1073741824 | bytes 6291456 | tf_op jit(solution)/shard_map/pallas_call | solution.py:126
  67.5 5.5 %collective-permute-done.6 = f16[2,8,72,256]{3,2,1,0:T(8,128)(2,1)S(1)} collective-permute-done((f16[2,8,72,256]{3,2,1,0:T(8,128)(2,1)S(1)}, f16[2,8,72,256]{3,2,1,0:T(8,128)(2,1)S(1)}, u32[]{:S(2)}, u32[]{:S(2)}) %collective-permute-start.6) | collective-permute-done | bytes 589856 | tf_op jit(solution)/shard_map/ppermute | solution.py:32
  73.2 1.7 collective-permute-done.9.behind.refs_9_
  75.1 0.3 select_convert_fusion.5
  75.6 9.8 %collective-permute-done.14.beyond.refs_10_ = bf16[512,512]{1,0:T(8,128)(2,1)S(1)} collective-permute-done((bf16[512,512]{1,0:T(8,128)(2,1)S(1)}, bf16[512,512]{1,0:T(8,128)(2,1)S(1)}, u32[]{:S(2)}, u32[]{:S(2)}) %collective-permute-start.14) | collective-permute-done | bytes 524320 | tf_op jit(solution)/shard_map/ppermute | solution.py:37
  85.4 2.6 %shard_map.52 = (f32[2,8,72,256]{3,2,1,0:T(8,128)S(1)}, f32[2,8,72,256]{3,2,1,0:T(8,128)S(1)}, f32[2,8,72,256]{3,2,1,0:T(8,128)S(1)}, f32[2,8,72,256]{3,2,1,0:T(8,128)S(1)}) custom-call(s32[3]{0:T(128)S(1)} %pad_add_fusion.place, bf16[512,512]{1,0:T(8,128)(2,1)S(1)} %pad_maximum_fusion.4.own.cols.refs_8_, ...), custom_call_target="tpu_custom_call" | custom-call | flops 1073741824 | bytes 6291456 | tf_op jit(solution)/shard_map/pallas_call | solution.py:126
  88.1 1.1 convert_element_type.234
  89.3 0.9 convert_element_type.235
  90.2 3.1 %collective-permute-start.17 = (f16[2,8,72,256]{3,2,1,0:T(8,128)(2,1)}, f16[2,8,72,256]{3,2,1,0:T(8,128)(2,1)S(1)}, u32[]{:S(2)}, u32[]{:S(2)}) collective-permute-start(f16[2,8,72,256]{3,2,1,0:T(8,128)(2,1)} %convert_element_type.235), channel_id=1, source_target_pairs={{0,24},{1,9},{2,26},{3,11},{4,28},{5,13},{6,30},{7,15},{8,0},{9,17... | collective-permute-start | bytes 1769480 | tf_op jit(solution)/shard_map/ppermute | solution.py:32
  93.4 1.1 select_convert_fusion.4
  94.6 1.3 select_convert_fusion.3
  95.9 8.9 %all-to-all-start = ((f16[16,72,256]{2,1,0:T(8,128)(2,1)}), f16[16,72,256]{2,1,0:T(8,128)(2,1)S(1)}, u32[]{:S(2)}, u32[]{:S(2)}) async-start(f16[16,72,256]{2,1,0:T(8,128)(2,1)} %bitcast.17), calls=%async_computation | async-start | bytes 1179648 | tf_op jit(solution)/shard_map/all_to_all | solution.py:306
  104.8 1.0 collective-permute-done.16
  105.8 1.6 collective-permute-done.17
  107.4 0.8 copy-done.20
  108.2 9.3 %shard_map.53 = (f32[3,512,256]{2,1,0:T(8,128)}, f32[3,512,256]{2,1,0:T(8,128)}, f32[72,256]{1,0:T(8,128)}) custom-call(s32[3]{0:T(128)} %copy-done.15, f32[2,3]{1,0:T(2,128)} %fusion.4.adagrad, bf16[512,512]{1,0:T(8,128)(2,1)} %copy-done.1, bf16[512,512]{1,0:T(8,128)(2,1)} %copy-done.8, bf16[512,512]{1,0:T(8,128)(2,1)} %collective-permute-done.5.beyond.refs_2_, ...), custom_call_target="tpu_custom_call" | custom-call | flops 3221225472 | bytes 15728640 | tf_op jit(solution)/shard_map/pallas_call | solution.py:208
  117.6 1.1 select_convert_fusion.2
  118.9 0.7 convert_multiply_fusion.6
  119.6 0.7 convert_multiply_fusion.5
  120.4 2.3 %select_convert_fusion.1 = f16[2,8,72,256]{3,2,1,0:T(8,128)(2,1)} fusion(f16[2,8,72,256]{3,2,1,0:T(8,128)(2,1)S(1)} %copy-done.22, f16[2,8,72,256]{3,2,1,0:T(8,128)(2,1)} %collective-permute-done.15, f32[2,8,72,256]{3,2,1,0:T(8,128)S(1)} %get-tuple-element.51, f32[2,256]{1,0:T(2,128)S(1)} %bitcast.171, f32[2,256]{1,0:T(2,128)S(1)} %bitcast.172, ...), kind=kLoop, calls=%fused_computation.11 | loop fusion | flops 2949120 | bytes 3031184 | tf_op jit(solution)/shard_map/convert_element_type | solution.py:155
  122.7 0.8 copy-done.18
  123.5 8.7 %all-to-all-start.1 = ((f16[16,72,256]{2,1,0:T(8,128)(2,1)}), f16[16,72,256]{2,1,0:T(8,128)(2,1)S(1)}, u32[]{:S(2)}, u32[]{:S(2)}) async-start(f16[16,72,256]{2,1,0:T(8,128)(2,1)} %bitcast.148), calls=%async_computation.1 | async-start | bytes 1179648 | tf_op jit(solution)/shard_map/all_to_all | solution.py:306
  132.3 0.9 slice.181
  133.1 0.2 collective-permute-start.28
  133.4 1.2 multiply_reduce_fusion.2
  134.6 0.7 fusion.7
  135.3 0.7 convert_multiply_fusion.3
  136.0 0.7 convert_multiply_fusion.2
  136.8 2.5 %select_convert_fusion = f16[2,8,72,256]{3,2,1,0:T(8,128)(2,1)} fusion(f16[2,8,72,256]{3,2,1,0:T(8,128)(2,1)} %copy-done.20, f16[2,8,72,256]{3,2,1,0:T(8,128)(2,1)} %collective-permute-done.21, f32[2,8,72,256]{3,2,1,0:T(8,128)S(1)} %copy-done.5, f32[2,256]{1,0:T(2,128)S(1)} %bitcast.155, f32[2,256]{1,0:T(2,128)S(1)} %bitcast.157, f32[2,256]{1,0:T(2,128)S(1)} %bitcast.162, ...), kind=kLoop, calls=%fused_computation.8 | loop fusion | flops 2654208 | bytes 2957384 | tf_op jit(solution)/shard_map/convert_element_type | solution.py:155
  139.3 10.7 %all-to-all-done.1 = f16[16,72,256]{2,1,0:T(8,128)(2,1)S(1)} async-done(((f16[16,72,256]{2,1,0:T(8,128)(2,1)}), f16[16,72,256]{2,1,0:T(8,128)(2,1)S(1)}, u32[]{:S(2)}, u32[]{:S(2)}) %all-to-all-start.1) | async-done | bytes 589856 | tf_op jit(solution)/shard_map/all_to_all | solution.py:306
  150.0 0.8 copy-done.17
  150.9 5.1 %collective-permute-start.24 = (f32[2,256]{1,0:T(2,128)S(1)}, f32[2,256]{1,0:T(2,128)S(1)}, u32[]{:S(2)}, u32[]{:S(2)}) collective-permute-start(f32[2,256]{1,0:T(2,128)S(1)} %bitcast_reduce_fusion), channel_id=1, source_target_pairs={{0,16},{1,17},{2,18},{3,19},{4,20},{5,21},{6,22},{7,23},{8,24},{9,... | collective-permute-start | bytes 6152 | tf_op jit(solution)/shard_map/ppermute | solution.py:32
  156.0 2.0 %collective-permute-start.22 = (f32[2,256]{1,0:T(2,128)S(1)}, f32[2,256]{1,0:T(2,128)S(1)}, u32[]{:S(2)}, u32[]{:S(2)}) collective-permute-start(f32[2,256]{1,0:T(2,128)S(1)} %bitcast_reduce_fusion), channel_id=1, source_target_pairs={{0,8},{1,25},{2,10},{3,27},{4,12},{5,29},{6,14},{7,31},{8,16},{9,1... | collective-permute-start | bytes 6152 | tf_op jit(solution)/shard_map/ppermute | solution.py:32
  158.1 4.2 %all-to-all-start.2 = ((f16[16,72,256]{2,1,0:T(8,128)(2,1)}), f16[16,72,256]{2,1,0:T(8,128)(2,1)}, u32[]{:S(2)}, u32[]{:S(2)}) async-start(f16[16,72,256]{2,1,0:T(8,128)(2,1)} %bitcast.147), calls=%async_computation.2 | async-start | bytes 1179648 | tf_op jit(solution)/shard_map/all_to_all | solution.py:306
  162.2 0.9 slice.183
  163.1 1.2 multiply_reduce_fusion.1
  164.5 1.4 collective-permute-start.26
  165.9 0.7 collective-permute-start.25
  166.6 3.0 %collective-permute-done.27 = f32[2,256]{1,0:T(2,128)S(1)} collective-permute-done((f32[2,256]{1,0:T(2,128)S(1)}, f32[2,256]{1,0:T(2,128)S(1)}, u32[]{:S(2)}, u32[]{:S(2)}) %collective-permute-start.27) | collective-permute-done | bytes 2080 | tf_op jit(solution)/shard_map/ppermute | solution.py:37
  169.5 1.2 collective-permute-done.25
  170.9 2.7 %shard_map.54 = f32[2,3,512,256]{3,2,1,0:T(8,128)} custom-call(s32[3]{0:T(128)S(1)} %copy-done.16, f32[2,3]{1,0:T(2,128)S(1)} %fusion.12.scale, f32[3,512,256]{2,1,0:T(8,128)S(1)} %copy-done.3, f32[3,512,256]{2,1,0:T(8,128)S(1)} %collective-permute-done.28.given), custom_call_target="tpu_custom_call" | custom-call | flops 786432 | bytes 6291456 | tf_op jit(solution)/shard_map/pallas_call | solution.py:236
  173.6 6.2 %all-to-all-done.2 = f16[16,72,256]{2,1,0:T(8,128)(2,1)} async-done(((f16[16,72,256]{2,1,0:T(8,128)(2,1)}), f16[16,72,256]{2,1,0:T(8,128)(2,1)}, u32[]{:S(2)}, u32[]{:S(2)}) %all-to-all-start.2) | async-done | bytes 589856 | tf_op jit(solution)/shard_map/all_to_all | solution.py:306
  179.8 0.9 slice.185
  180.7 1.2 multiply_reduce_fusion
  181.9 0.8 pad_maximum_fusion.5
  (142 shorter events, 2.8 us)
Async XLA Ops:
  7.2 100.2 %all-gather.3.cloned.1.call-start = ((), (), s32[]{:S(2)}) async-start(), calls=%async_computation.3 | async-start | bytes 7077888 | tf_op jit(solution)/shard_map/all_gather | solution.py:281
  7.2 1.5 copy-start.19
  8.8 2.5 %collective-permute-start = (bf16[3,576,256]{2,1,0:T(8,128)(2,1)S(1)}, bf16[3,576,256]{2,1,0:T(8,128)(2,1)S(1)}, u32[]{:S(2)}, u32[]{:S(2)}) collective-permute-start(bf16[3,576,256]{2,1,0:T(8,128)(2,1)S(1)} %pad_maximum_fusion), channel_id=1, source_target_pairs={{0,1},{1,0},{2,3},{3,2},{4,5},{5,4},{6,7},{7,6},{8,9},{9,8},{10,11... | collective-permute-start | bytes 2654216 | tf_op jit(solution)/shard_map/ppermute | solution.py:58
  11.5 73.9 %copy-start = (bf16[512,512]{1,0:T(8,128)(2,1)}, bf16[512,512]{1,0:T(8,128)(2,1)S(1)}, u32[]{:S(2)}) copy-start(bf16[512,512]{1,0:T(8,128)(2,1)S(1)} %pad_maximum_fusion.4.own.cols.refs_8_) | copy-start | bytes 1572868
  11.7 40.9 %copy-start.1 = (bf16[512,512]{1,0:T(8,128)(2,1)}, bf16[512,512]{1,0:T(8,128)(2,1)S(1)}, u32[]{:S(2)}) copy-start(bf16[512,512]{1,0:T(8,128)(2,1)S(1)} %get-tuple-element.43.own.cols.refs_0_) | copy-start | bytes 1572868
  11.7 51.6 %copy-start.2 = (bf16[512,512]{1,0:T(8,128)(2,1)}, bf16[512,512]{1,0:T(8,128)(2,1)S(1)}, u32[]{:S(2)}) copy-start(bf16[512,512]{1,0:T(8,128)(2,1)S(1)} %get-tuple-element.44.own.cols.refs_4_) | copy-start | bytes 1572868
  11.7 18.0 %collective-permute-start.1 = (bf16[512,512]{1,0:T(8,128)(2,1)S(1)}, bf16[512,512]{1,0:T(8,128)(2,1)S(1)}, u32[]{:S(2)}, u32[]{:S(2)}) collective-permute-start(bf16[512,512]{1,0:T(8,128)(2,1)S(1)} %get-tuple-element.43.own.cols.refs_0_), channel_id=1, source_target_pairs={{0,2},{1,7},{2,4},{3,1},{4,6},{5,3},{6,0},{7,5},{8,10},{9,15},{10,... | collective-permute-start | bytes 1572872 | tf_op jit(solution)/shard_map/ppermute | solution.py:37
  13.4 16.3 %collective-permute-start.2 = (bf16[512,512]{1,0:T(8,128)(2,1)S(1)}, bf16[512,512]{1,0:T(8,128)(2,1)S(1)}, u32[]{:S(2)}, u32[]{:S(2)}) collective-permute-start(bf16[512,512]{1,0:T(8,128)(2,1)S(1)} %get-tuple-element.43.own.cols.refs_0_), channel_id=1, source_target_pairs={{0,6},{1,3},{2,0},{3,5},{4,2},{5,7},{6,4},{7,1},{8,14},{9,11},{10,... | collective-permute-start | bytes 1572872 | tf_op jit(solution)/shard_map/ppermute | solution.py:37
  15.0 11.0 %collective-permute-start.18 = (bf16[3,64,512]{2,1,0:T(8,128)(2,1)S(1)}, bf16[3,64,512]{2,1,0:T(8,128)(2,1)S(1)}, u32[]{:S(2)}, u32[]{:S(2)}) collective-permute-start(bf16[3,64,512]{2,1,0:T(8,128)(2,1)S(1)} %pad_maximum_fusion.6), channel_id=1, source_target_pairs={{0,24},{8,0},{16,8},{24,16},{32,56},{40,32},{48,40},{56,48},{64,88... | collective-permute-start | bytes 589832 | tf_op jit(solution)/shard_map/ppermute | solution.py:42
  17.8 9.4 %collective-permute-start.19 = (bf16[3,64,512]{2,1,0:T(8,128)(2,1)S(1)}, bf16[3,64,512]{2,1,0:T(8,128)(2,1)S(1)}, u32[]{:S(2)}, u32[]{:S(2)}) collective-permute-start(bf16[3,64,512]{2,1,0:T(8,128)(2,1)S(1)} %pad_maximum_fusion.6), channel_id=1, source_target_pairs={{0,16},{8,24},{16,0},{24,8},{32,48},{40,56},{48,32},{56,40},{64,80... | collective-permute-start | bytes 589832 | tf_op jit(solution)/shard_map/ppermute | solution.py:42
  18.6 11.1 %collective-permute-start.20 = (bf16[3,64,512]{2,1,0:T(8,128)(2,1)S(1)}, bf16[3,64,512]{2,1,0:T(8,128)(2,1)S(1)}, u32[]{:S(2)}, u32[]{:S(2)}) collective-permute-start(bf16[3,64,512]{2,1,0:T(8,128)(2,1)S(1)} %pad_maximum_fusion.6), channel_id=1, source_target_pairs={{0,8},{8,16},{16,24},{24,0},{32,40},{40,48},{48,56},{56,32},{64,72... | collective-permute-start | bytes 589832 | tf_op jit(solution)/shard_map/ppermute | solution.py:42
  29.7 22.9 %copy-start.8 = (bf16[512,512]{1,0:T(8,128)(2,1)}, bf16[512,512]{1,0:T(8,128)(2,1)S(1)}, u32[]{:S(2)}) copy-start(bf16[512,512]{1,0:T(8,128)(2,1)S(1)} %collective-permute-done.1.behind.refs_1_) | copy-start | bytes 1572868
  29.7 22.9 %copy-start.9 = (bf16[512,512]{1,0:T(8,128)(2,1)}, bf16[512,512]{1,0:T(8,128)(2,1)S(1)}, u32[]{:S(2)}) copy-start(bf16[512,512]{1,0:T(8,128)(2,1)S(1)} %collective-permute-done.2.ahead.refs_3_) | copy-start | bytes 1572868
  30.8 14.3 %collective-permute-start.3 = (bf16[512,512]{1,0:T(8,128)(2,1)S(1)}, bf16[512,512]{1,0:T(8,128)(2,1)S(1)}, u32[]{:S(2)}, u32[]{:S(2)}) collective-permute-start(bf16[512,512]{1,0:T(8,128)(2,1)S(1)} %get-tuple-element.44.own.cols.refs_4_), channel_id=1, source_target_pairs={{0,2},{1,7},{2,4},{3,1},{4,6},{5,3},{6,0},{7,5},{8,10},{9,15},{10,... | collective-permute-start | bytes 1572872 | tf_op jit(solution)/shard_map/ppermute | solution.py:37
  31.2 18.7 %collective-permute-start.4 = (bf16[512,512]{1,0:T(8,128)(2,1)S(1)}, bf16[512,512]{1,0:T(8,128)(2,1)}, u32[]{:S(2)}, u32[]{:S(2)}) collective-permute-start(bf16[512,512]{1,0:T(8,128)(2,1)S(1)} %get-tuple-element.44.own.cols.refs_4_), channel_id=1, source_target_pairs={{0,6},{1,3},{2,0},{3,5},{4,2},{5,7},{6,4},{7,1},{8,14},{9,11},{10,... | collective-permute-start | bytes 1572872 | tf_op jit(solution)/shard_map/ppermute | solution.py:37
  34.1 18.5 %collective-permute-start.5 = (bf16[512,512]{1,0:T(8,128)(2,1)S(1)}, bf16[512,512]{1,0:T(8,128)(2,1)}, u32[]{:S(2)}, u32[]{:S(2)}) collective-permute-start(bf16[512,512]{1,0:T(8,128)(2,1)S(1)} %collective-permute-done.1.behind.refs_1_), channel_id=1, source_target_pairs={{0,2},{1,7},{2,4},{3,1},{4,6},{5,3},{6,0},{7,5},{8,10},{9,15},{10,... | collective-permute-start | bytes 1572872 | tf_op jit(solution)/shard_map/ppermute | solution.py:37
  45.1 4.8 %copy-start.10 = (bf16[512,512]{1,0:T(8,128)(2,1)}, bf16[512,512]{1,0:T(8,128)(2,1)S(1)}, u32[]{:S(2)}) copy-start(bf16[512,512]{1,0:T(8,128)(2,1)S(1)} %collective-permute-done.3.behind.refs_5_) | copy-start | bytes 1572868
  45.1 15.0 %collective-permute-start.8 = (bf16[512,512]{1,0:T(8,128)(2,1)S(1)}, bf16[512,512]{1,0:T(8,128)(2,1)}, u32[]{:S(2)}, u32[]{:S(2)}) collective-permute-start(bf16[512,512]{1,0:T(8,128)(2,1)S(1)} %collective-permute-done.3.behind.refs_5_), channel_id=1, source_target_pairs={{0,2},{1,7},{2,4},{3,1},{4,6},{5,3},{6,0},{7,5},{8,10},{9,15},{10,... | collective-permute-start | bytes 1572872 | tf_op jit(solution)/shard_map/ppermute | solution.py:37
  49.9 35.5 %copy-start.15 = (s32[3]{0:T(128)}, s32[3]{0:T(128)S(1)}, u32[]{:S(2)}) copy-start(s32[3]{0:T(128)S(1)} %pad_add_fusion.place) | copy-start | bytes 40
  56.4 6.9 %copy-start.11 = (bf16[512,512]{1,0:T(8,128)(2,1)S(1)}, bf16[512,512]{1,0:T(8,128)(2,1)}, u32[]{:S(2)}) copy-start(bf16[512,512]{1,0:T(8,128)(2,1)} %copy-done.10) | copy-start | bytes 1572868
  56.4 16.6 %collective-permute-start.6 = (f16[2,8,72,256]{3,2,1,0:T(8,128)(2,1)S(1)}, f16[2,8,72,256]{3,2,1,0:T(8,128)(2,1)S(1)}, u32[]{:S(2)}, u32[]{:S(2)}) collective-permute-start(f16[2,8,72,256]{3,2,1,0:T(8,128)(2,1)S(1)} %convert_element_type.205), channel_id=1, source_target_pairs={{0,8},{1,25},{2,10},{3,27},{4,12},{5,29},{6,14},{7,31},{8,16},{9,1... | collective-permute-start | bytes 1769480 | tf_op jit(solution)/shard_map/ppermute | solution.py:32
  56.6 16.6 %collective-permute-start.7 = (f16[2,8,72,256]{3,2,1,0:T(8,128)(2,1)S(1)}, f16[2,8,72,256]{3,2,1,0:T(8,128)(2,1)S(1)}, u32[]{:S(2)}, u32[]{:S(2)}) collective-permute-start(f16[2,8,72,256]{3,2,1,0:T(8,128)(2,1)S(1)} %convert_element_type.206), channel_id=1, source_target_pairs={{0,24},{1,9},{2,26},{3,11},{4,28},{5,13},{6,30},{7,15},{8,0},{9,17... | collective-permute-start | bytes 1769480 | tf_op jit(solution)/shard_map/ppermute | solution.py:32
  60.1 14.8 %collective-permute-start.9 = (bf16[512,512]{1,0:T(8,128)(2,1)S(1)}, bf16[512,512]{1,0:T(8,128)(2,1)S(1)}, u32[]{:S(2)}, u32[]{:S(2)}) collective-permute-start(bf16[512,512]{1,0:T(8,128)(2,1)S(1)} %pad_maximum_fusion.4.own.cols.refs_8_), channel_id=1, source_target_pairs={{0,2},{1,7},{2,4},{3,1},{4,6},{5,3},{6,0},{7,5},{8,10},{9,15},{10,... | collective-permute-start | bytes 1572872 | tf_op jit(solution)/shard_map/ppermute | solution.py:37
  60.1 14.8 %collective-permute-start.10 = (bf16[512,512]{1,0:T(8,128)(2,1)S(1)}, bf16[512,512]{1,0:T(8,128)(2,1)S(1)}, u32[]{:S(2)}, u32[]{:S(2)}) collective-permute-start(bf16[512,512]{1,0:T(8,128)(2,1)S(1)} %pad_maximum_fusion.4.own.cols.refs_8_), channel_id=1, source_target_pairs={{0,6},{1,3},{2,0},{3,5},{4,2},{5,7},{6,4},{7,1},{8,14},{9,11},{10,... | collective-permute-start | bytes 1572872 | tf_op jit(solution)/shard_map/ppermute | solution.py:37
  67.3 26.0 %collective-permute-start.12 = (f16[2,8,72,256]{3,2,1,0:T(8,128)(2,1)S(1)}, f16[2,8,72,256]{3,2,1,0:T(8,128)(2,1)S(1)}, u32[]{:S(2)}, u32[]{:S(2)}) collective-permute-start(f16[2,8,72,256]{3,2,1,0:T(8,128)(2,1)S(1)} %convert_element_type.214), channel_id=1, source_target_pairs={{0,8},{1,25},{2,10},{3,27},{4,12},{5,29},{6,14},{7,31},{8,16},{9,1... | collective-permute-start | bytes 1769480 | tf_op jit(solution)/shard_map/ppermute | solution.py:32
  73.0 20.3 %collective-permute-start.13 = (f16[2,8,72,256]{3,2,1,0:T(8,128)(2,1)S(1)}, f16[2,8,72,256]{3,2,1,0:T(8,128)(2,1)S(1)}, u32[]{:S(2)}, u32[]{:S(2)}) collective-permute-start(f16[2,8,72,256]{3,2,1,0:T(8,128)(2,1)S(1)} %convert_element_type.215), channel_id=1, source_target_pairs={{0,24},{1,9},{2,26},{3,11},{4,28},{5,13},{6,30},{7,15},{8,0},{9,17... | collective-permute-start | bytes 1769480 | tf_op jit(solution)/shard_map/ppermute | solution.py:32
  74.9 10.5 %copy-start.12 = (bf16[512,512]{1,0:T(8,128)(2,1)}, bf16[512,512]{1,0:T(8,128)(2,1)S(1)}, u32[]{:S(2)}) copy-start(bf16[512,512]{1,0:T(8,128)(2,1)S(1)} %collective-permute-done.9.behind.refs_9_) | copy-start | bytes 1572868
  74.9 10.5 %copy-start.13 = (bf16[512,512]{1,0:T(8,128)(2,1)}, bf16[512,512]{1,0:T(8,128)(2,1)S(1)}, u32[]{:S(2)}) copy-start(bf16[512,512]{1,0:T(8,128)(2,1)S(1)} %collective-permute-done.10.ahead.refs_11_) | copy-start | bytes 1572868
  74.9 10.5 %collective-permute-start.14 = (bf16[512,512]{1,0:T(8,128)(2,1)S(1)}, bf16[512,512]{1,0:T(8,128)(2,1)S(1)}, u32[]{:S(2)}, u32[]{:S(2)}) collective-permute-start(bf16[512,512]{1,0:T(8,128)(2,1)S(1)} %collective-permute-done.9.behind.refs_9_), channel_id=1, source_target_pairs={{0,2},{1,7},{2,4},{3,1},{4,6},{5,3},{6,0},{7,5},{8,10},{9,15},{10,... | collective-permute-start | bytes 1572872 | tf_op jit(solution)/shard_map/ppermute | solution.py:37
  75.4 19.1 %collective-permute-start.11 = (f16[2,8,72,256]{3,2,1,0:T(8,128)(2,1)S(1)}, f16[2,8,72,256]{3,2,1,0:T(8,128)(2,1)S(1)}, u32[]{:S(2)}, u32[]{:S(2)}) collective-permute-start(f16[2,8,72,256]{3,2,1,0:T(8,128)(2,1)S(1)} %select_convert_fusion.5), channel_id=1, source_target_pairs={{0,8},{1,25},{2,10},{3,27},{4,12},{5,29},{6,14},{7,31},{8,16},{9,1... | collective-permute-start | bytes 1769480 | tf_op jit(solution)/shard_map/ppermute | solution.py:32
  85.4 2.6 %copy-start.14 = (bf16[512,512]{1,0:T(8,128)(2,1)}, bf16[512,512]{1,0:T(8,128)(2,1)S(1)}, u32[]{:S(2)}) copy-start(bf16[512,512]{1,0:T(8,128)(2,1)S(1)} %collective-permute-done.14.beyond.refs_10_) | copy-start | bytes 1572868
  88.1 2.1 %copy-start.4 = (f32[2,8,72,256]{3,2,1,0:T(8,128)}, f32[2,8,72,256]{3,2,1,0:T(8,128)S(1)}, u32[]{:S(2)}) copy-start(f32[2,8,72,256]{3,2,1,0:T(8,128)S(1)} %get-tuple-element.59) | copy-start | bytes 3538948
  88.1 2.1 %copy-start.6 = (f32[2,8,72,256]{3,2,1,0:T(8,128)}, f32[2,8,72,256]{3,2,1,0:T(8,128)S(1)}, u32[]{:S(2)}) copy-start(f32[2,8,72,256]{3,2,1,0:T(8,128)S(1)} %get-tuple-element.63) | copy-start | bytes 3538948
  89.1 16.6 %collective-permute-start.16 = (f16[2,8,72,256]{3,2,1,0:T(8,128)(2,1)}, f16[2,8,72,256]{3,2,1,0:T(8,128)(2,1)S(1)}, u32[]{:S(2)}, u32[]{:S(2)}) collective-permute-start(f16[2,8,72,256]{3,2,1,0:T(8,128)(2,1)} %convert_element_type.234), channel_id=1, source_target_pairs={{0,8},{1,25},{2,10},{3,27},{4,12},{5,29},{6,14},{7,31},{8,16},{9,1... | collective-permute-start | bytes 1769480 | tf_op jit(solution)/shard_map/ppermute | solution.py:32
  90.2 17.2 %collective-permute-start.17 = (f16[2,8,72,256]{3,2,1,0:T(8,128)(2,1)}, f16[2,8,72,256]{3,2,1,0:T(8,128)(2,1)S(1)}, u32[]{:S(2)}, u32[]{:S(2)}) collective-permute-start(f16[2,8,72,256]{3,2,1,0:T(8,128)(2,1)} %convert_element_type.235), channel_id=1, source_target_pairs={{0,24},{1,9},{2,26},{3,11},{4,28},{5,13},{6,30},{7,15},{8,0},{9,17... | collective-permute-start | bytes 1769480 | tf_op jit(solution)/shard_map/ppermute | solution.py:32
  93.3 1.2 copy-start.21
  94.5 24.4 %collective-permute-start.15 = (f16[2,8,72,256]{3,2,1,0:T(8,128)(2,1)}, f16[2,8,72,256]{3,2,1,0:T(8,128)(2,1)}, u32[]{:S(2)}, u32[]{:S(2)}) collective-permute-start(f16[2,8,72,256]{3,2,1,0:T(8,128)(2,1)} %select_convert_fusion.4), channel_id=1, source_target_pairs={{0,8},{1,25},{2,10},{3,27},{4,12},{5,29},{6,14},{7,31},{8,16},{9,1... | collective-permute-start | bytes 1769480 | tf_op jit(solution)/shard_map/ppermute | solution.py:32
  95.9 26.8 %all-to-all-start = ((f16[16,72,256]{2,1,0:T(8,128)(2,1)}), f16[16,72,256]{2,1,0:T(8,128)(2,1)S(1)}, u32[]{:S(2)}, u32[]{:S(2)}) async-start(f16[16,72,256]{2,1,0:T(8,128)(2,1)} %bitcast.17), calls=%async_computation | async-start | bytes 1179648 | tf_op jit(solution)/shard_map/all_to_all | solution.py:306
  105.8 1.6 copy-start.23
  107.4 0.8 copy-start.20
  108.2 9.3 %copy-start.7 = (f32[2,8,72,256]{3,2,1,0:T(8,128)S(1)}, f32[2,8,72,256]{3,2,1,0:T(8,128)}, u32[]{:S(2)}) copy-start(f32[2,8,72,256]{3,2,1,0:T(8,128)} %copy-done.6) | copy-start | bytes 3538948
  108.2 9.3 %copy-start.24 = (f16[2,8,72,256]{3,2,1,0:T(8,128)(2,1)S(1)}, f16[2,8,72,256]{3,2,1,0:T(8,128)(2,1)}, u32[]{:S(2)}) copy-start(f16[2,8,72,256]{3,2,1,0:T(8,128)(2,1)} %copy-done.23) | copy-start | bytes 1769476
  117.6 1.3 copy-start.22
  117.6 2.8 %copy-start.26 = (f32[72,256]{1,0:T(8,128)S(1)}, f32[72,256]{1,0:T(8,128)}, u32[]{:S(2)}) copy-start(f32[72,256]{1,0:T(8,128)} %get-tuple-element.72) | copy-start | bytes 221188
  118.8 16.5 %collective-permute-start.21 = (f16[2,8,72,256]{3,2,1,0:T(8,128)(2,1)}, f16[2,8,72,256]{3,2,1,0:T(8,128)(2,1)}, u32[]{:S(2)}, u32[]{:S(2)}) collective-permute-start(f16[2,8,72,256]{3,2,1,0:T(8,128)(2,1)} %select_convert_fusion.2), channel_id=1, source_target_pairs={{0,8},{1,25},{2,10},{3,27},{4,12},{5,29},{6,14},{7,31},{8,16},{9,1... | collective-permute-start | bytes 1769480 | tf_op jit(solution)/shard_map/ppermute | solution.py:32
  122.7 12.6 %copy-start.5 = (f32[2,8,72,256]{3,2,1,0:T(8,128)S(1)}, f32[2,8,72,256]{3,2,1,0:T(8,128)}, u32[]{:S(2)}) copy-start(f32[2,8,72,256]{3,2,1,0:T(8,128)} %copy-done.4) | copy-start | bytes 3538948
  122.7 0.8 copy-start.18
  123.5 26.5 %all-to-all-start.1 = ((f16[16,72,256]{2,1,0:T(8,128)(2,1)}), f16[16,72,256]{2,1,0:T(8,128)(2,1)S(1)}, u32[]{:S(2)}, u32[]{:S(2)}) async-start(f16[16,72,256]{2,1,0:T(8,128)(2,1)} %bitcast.148), calls=%async_computation.1 | async-start | bytes 1179648 | tf_op jit(solution)/shard_map/all_to_all | solution.py:306
  133.1 37.8 %collective-permute-start.28 = (f32[3,512,256]{2,1,0:T(8,128)}, f32[3,512,256]{2,1,0:T(8,128)S(1)}, u32[]{:S(2)}, u32[]{:S(2)}) collective-permute-start(f32[3,512,256]{2,1,0:T(8,128)} %get-tuple-element.81), channel_id=1, source_target_pairs={{0,1},{1,0},{2,3},{3,2},{4,5},{5,4},{6,7},{7,6},{8,9},{9,8},{10,11... | collective-permute-start | bytes 4718600 | tf_op jit(solution)/shard_map/ppermute | solution.py:58
  150.0 0.8 copy-start.17
  150.8 20.1 %copy-start.3 = (f32[3,512,256]{2,1,0:T(8,128)S(1)}, f32[3,512,256]{2,1,0:T(8,128)}, u32[]{:S(2)}) copy-start(f32[3,512,256]{2,1,0:T(8,128)} %get-tuple-element.80.kept) | copy-start | bytes 4718596
  150.8 20.1 %copy-start.16 = (s32[3]{0:T(128)S(1)}, s32[3]{0:T(128)}, u32[]{:S(2)}) copy-start(s32[3]{0:T(128)} %copy-done.15) | copy-start | bytes 40
  150.9 13.4 %collective-permute-start.24 = (f32[2,256]{1,0:T(2,128)S(1)}, f32[2,256]{1,0:T(2,128)S(1)}, u32[]{:S(2)}, u32[]{:S(2)}) collective-permute-start(f32[2,256]{1,0:T(2,128)S(1)} %bitcast_reduce_fusion), channel_id=1, source_target_pairs={{0,16},{1,17},{2,18},{3,19},{4,20},{5,21},{6,22},{7,23},{8,24},{9,... | collective-permute-start | bytes 6152 | tf_op jit(solution)/shard_map/ppermute | solution.py:32
  156.0 8.3 %collective-permute-start.23 = (f32[2,256]{1,0:T(2,128)S(1)}, f32[2,256]{1,0:T(2,128)S(1)}, u32[]{:S(2)}, u32[]{:S(2)}) collective-permute-start(f32[2,256]{1,0:T(2,128)S(1)} %bitcast_reduce_fusion), channel_id=1, source_target_pairs={{0,24},{1,9},{2,26},{3,11},{4,28},{5,13},{6,30},{7,15},{8,0},{9,17... | collective-permute-start | bytes 6152 | tf_op jit(solution)/shard_map/ppermute | solution.py:32
  156.0 8.3 %collective-permute-start.22 = (f32[2,256]{1,0:T(2,128)S(1)}, f32[2,256]{1,0:T(2,128)S(1)}, u32[]{:S(2)}, u32[]{:S(2)}) collective-permute-start(f32[2,256]{1,0:T(2,128)S(1)} %bitcast_reduce_fusion), channel_id=1, source_target_pairs={{0,8},{1,25},{2,10},{3,27},{4,12},{5,29},{6,14},{7,31},{8,16},{9,1... | collective-permute-start | bytes 6152 | tf_op jit(solution)/shard_map/ppermute | solution.py:32
  158.1 21.8 %all-to-all-start.2 = ((f16[16,72,256]{2,1,0:T(8,128)(2,1)}), f16[16,72,256]{2,1,0:T(8,128)(2,1)}, u32[]{:S(2)}, u32[]{:S(2)}) async-start(f16[16,72,256]{2,1,0:T(8,128)(2,1)} %bitcast.147), calls=%async_computation.2 | async-start | bytes 1179648 | tf_op jit(solution)/shard_map/all_to_all | solution.py:306
  164.4 5.2 %collective-permute-start.27 = (f32[2,256]{1,0:T(2,128)S(1)}, f32[2,256]{1,0:T(2,128)S(1)}, u32[]{:S(2)}, u32[]{:S(2)}) collective-permute-start(f32[2,256]{1,0:T(2,128)S(1)} %add_add_fusion.1), channel_id=1, source_target_pairs={{0,4},{1,5},{2,6},{3,7},{4,0},{5,1},{6,2},{7,3},{8,12},{9,13},{10,... | collective-permute-start | bytes 6152 | tf_op jit(solution)/shard_map/ppermute | solution.py:37
  164.5 5.1 %collective-permute-start.26 = (f32[2,256]{1,0:T(2,128)S(1)}, f32[2,256]{1,0:T(2,128)S(1)}, u32[]{:S(2)}, u32[]{:S(2)}) collective-permute-start(f32[2,256]{1,0:T(2,128)S(1)} %add_add_fusion.1), channel_id=1, source_target_pairs={{0,6},{1,3},{2,0},{3,5},{4,2},{5,7},{6,4},{7,1},{8,14},{9,11},{10,... | collective-permute-start | bytes 6152 | tf_op jit(solution)/shard_map/ppermute | solution.py:37
  165.9 4.8 %collective-permute-start.25 = (f32[2,256]{1,0:T(2,128)S(1)}, f32[2,256]{1,0:T(2,128)S(1)}, u32[]{:S(2)}, u32[]{:S(2)}) collective-permute-start(f32[2,256]{1,0:T(2,128)S(1)} %add_add_fusion.1), channel_id=1, source_target_pairs={{0,2},{1,7},{2,4},{3,1},{4,6},{5,3},{6,0},{7,5},{8,10},{9,15},{10,... | collective-permute-start | bytes 6152 | tf_op jit(solution)/shard_map/ppermute | solution.py:37
  170.9 11.0 %copy-start.25 = (f32[2,1,64,256]{3,2,1,0:T(8,128)S(1)}, f32[2,1,64,256]{3,2,1,0:T(8,128)}, u32[]{:S(2)}) copy-start(f32[2,1,64,256]{3,2,1,0:T(8,128)} %fusion.7) | copy-start | bytes 393220
Sparse Core Ops, SparseCore 0:
  30.9 72.8 all-gather.2

commit v4 on v3

--- a/solution.py
+++ b/solution.py
@@ -337,7 +337,8 @@
     sums = jnp.sum(sums.reshape(experts, NZ, slab), axis=1)
     rows2 = owned(part2, after(got2, rows1))
     terms.append(send_rows(after(rows2, terms[1])))
-    sums = sums + step_x(sums, 1) + step_x(sums, -1) + step_x(sums, 2)
+    sums = sums + step_x(sums, 1)
+    sums = sums + step_x(sums, 2)
     sums = sums + step_y(sums, 1) + step_y(sums, -1) + step_y(sums, 2)
     count = experts * blocks
     sums = jnp.sum(sums[:, :count], axis=0).reshape(experts, blocks), sums[:, count : count + blocks]

time: 191 us -> 189 us (0.990)
  waiting for transfers between devices: 66.9 us -> 63.6 us
    all_to_all x3, waiting for transfers between devices: 16.9 us -> 10.7 us  [send_rows(): return lax.all_to_all(summed, AXES, 0, 0, axis_index_groups=GROUPS_CZ)]
    ppermute x12 -> x11, waiting for transfers between devices: 8.11 us -> 11.8 us  [step_x(): return lax.ppermute(value, AXES, pairs)]
    ppermute x12, starting transfers between devices: 12.1 us -> 14.5 us  [step_y(): return lax.ppermute(value, 'tp', pairs)]
    ppermute x12 -> x11, starting transfers between devices: 14.6 us -> 12.7 us  [step_x(): return lax.ppermute(value, AXES, pairs)]
  transfers between devices with their start and end apart: 33 -> 32, of which waited for: 15 -> 17; matrix products, arithmetic and copies ran while one was open for 13% -> 13% of each run, Pallas kernels for 12% -> 12%
where the time goes in v4:
time: 189 us; the launch traced here: 188 us
  waiting for transfers between devices  63.6 us (34%)
  starting transfers between devices  54 us (29%)
  other arithmetic  28.1 us (15%)
  Pallas kernels  22.1 us (12%)
  between operations  14.7 us (8%)
  local copies, waits for them, and re-layouts  5.3 us (3%)
    ppermute x12, waiting for transfers between devices, step_y(): return lax.ppermute(value, 'tp', pairs)  28.5 us
    all_to_all x3, starting transfers between devices, send_rows(): return lax.all_to_all(summed, AXES, 0, 0, axis_index_groups=GROUPS_CZ)  22 us
    ppermute x12, starting transfers between devices, step_y(): return lax.ppermute(value, 'tp', pairs)  14.5 us
    ppermute x11, starting transfers between devices, step_x(): return lax.ppermute(value, AXES, pairs)  12.7 us
    ppermute x11, waiting for transfers between devices, step_x(): return lax.ppermute(value, AXES, pairs)  11.8 us
    all_to_all x3, waiting for transfers between devices, send_rows(): return lax.all_to_all(summed, AXES, 0, 0, axis_index_groups=GROUPS_CZ)  10.7 us
    ppermute x3, waiting for transfers between devices, shift_x(): return lax.ppermute(value, 'fsdp', pairs)  10.2 us
    pallas_call x3, Pallas kernels, gram_parts(): pl.pallas_call(gram_kernel, grid_spec=pltpu.PrefetchScalarGridSpec(num_sc...  10.1 us
  transfers between devices with their start and end apart: 32, of which 17 were waited for; matrix products, arithmetic and copies ran while one was open for 13% of the time, Pallas kernels for 12%

profile of v4, /device:TPU:32, one launch (start us, length us, event | category | flops | bytes accessed | tf_op | source)
XLA Modules:
  0.0 187.8 jit_solution(2184150253141767885)
XLA Ops:
  7.2 1.5 select_bitcast_fusion
  8.9 2.4 %collective-permute-done = bf16[3,576,256]{2,1,0:T(8,128)(2,1)S(1)} collective-permute-done((bf16[3,576,256]{2,1,0:T(8,128)(2,1)S(1)}, bf16[3,576,256]{2,1,0:T(8,128)(2,1)S(1)}, u32[]{:S(2)}, u32[]{:S(2)}) %collective-permute-start) | collective-permute-done | bytes 884768 | tf_op jit(solution)/shard_map/ppermute | solution.py:58
  11.7 1.7 collective-permute-start.1
  13.4 1.7 collective-permute-start.2
  15.0 2.8 %collective-permute-start.18 = (bf16[3,64,512]{2,1,0:T(8,128)(2,1)S(1)}, bf16[3,64,512]{2,1,0:T(8,128)(2,1)S(1)}, u32[]{:S(2)}, u32[]{:S(2)}) collective-permute-start(bf16[3,64,512]{2,1,0:T(8,128)(2,1)S(1)} %pad_maximum_fusion.6), channel_id=1, source_target_pairs={{0,24},{8,0},{16,8},{24,16},{32,56},{40,32},{48,40},{56,48},{64,88... | collective-permute-start | bytes 589832 | tf_op jit(solution)/shard_map/ppermute | solution.py:42
  17.8 0.8 collective-permute-start.19
  18.6 0.9 collective-permute-start.20
  19.5 6.5 %collective-permute-done.18 = bf16[3,64,512]{2,1,0:T(8,128)(2,1)S(1)} collective-permute-done((bf16[3,64,512]{2,1,0:T(8,128)(2,1)S(1)}, bf16[3,64,512]{2,1,0:T(8,128)(2,1)S(1)}, u32[]{:S(2)}, u32[]{:S(2)}) %collective-permute-start.18) | collective-permute-done | bytes 196640 | tf_op jit(solution)/shard_map/ppermute | solution.py:42
  26.0 1.2 collective-permute-done.19
  27.2 2.5 %collective-permute-done.20 = bf16[3,64,512]{2,1,0:T(8,128)(2,1)S(1)} collective-permute-done((bf16[3,64,512]{2,1,0:T(8,128)(2,1)S(1)}, bf16[3,64,512]{2,1,0:T(8,128)(2,1)S(1)}, u32[]{:S(2)}, u32[]{:S(2)}) %collective-permute-start.20) | collective-permute-done | bytes 196640 | tf_op jit(solution)/shard_map/ppermute | solution.py:42
  29.7 1.1 pad_maximum_fusion.1
  31.2 2.9 %collective-permute-start.4 = (bf16[512,512]{1,0:T(8,128)(2,1)S(1)}, bf16[512,512]{1,0:T(8,128)(2,1)}, u32[]{:S(2)}, u32[]{:S(2)}) collective-permute-start(bf16[512,512]{1,0:T(8,128)(2,1)S(1)} %get-tuple-element.44.own.cols.refs_4_), channel_id=1, source_target_pairs={{0,6},{1,3},{2,0},{3,5},{4,2},{5,7},{6,4},{7,1},{8,14},{9,11},{10,... | collective-permute-start | bytes 1572872 | tf_op jit(solution)/shard_map/ppermute | solution.py:37
  34.1 11.0 %collective-permute-done.3.behind.refs_5_ = bf16[512,512]{1,0:T(8,128)(2,1)S(1)} collective-permute-done((bf16[512,512]{1,0:T(8,128)(2,1)S(1)}, bf16[512,512]{1,0:T(8,128)(2,1)S(1)}, u32[]{:S(2)}, u32[]{:S(2)}) %collective-permute-start.3) | collective-permute-done | bytes 524320 | tf_op jit(solution)/shard_map/ppermute | solution.py:37
  45.1 4.7 %fusion.4.adagrad = f32[2,3]{1,0:T(2,128)} fusion(f32[2,512,3,256]{3,1,2,0:T(8,128)} %param.4, bf16[2,512,3,256]{3,1,2,0:T(8,128)(2,1)} %param.3), kind=kLoop, calls=%fused_computation.6 | loop fusion | flops 5505018 | bytes 4718616 | tf_op jit(solution)/shard_map/reduce_sum | solution.py:286
  49.9 2.7 %collective-permute-done.5.beyond.refs_2_ = bf16[512,512]{1,0:T(8,128)(2,1)} collective-permute-done((bf16[512,512]{1,0:T(8,128)(2,1)S(1)}, bf16[512,512]{1,0:T(8,128)(2,1)}, u32[]{:S(2)}, u32[]{:S(2)}) %collective-permute-start.5) | collective-permute-done | bytes 524320 | tf_op jit(solution)/shard_map/ppermute | solution.py:37
  52.6 3.7 %shard_map.50 = (f32[2,8,72,256]{3,2,1,0:T(8,128)S(1)}, f32[2,8,72,256]{3,2,1,0:T(8,128)S(1)}, f32[2,8,72,256]{3,2,1,0:T(8,128)S(1)}, f32[2,8,72,256]{3,2,1,0:T(8,128)S(1)}) custom-call(s32[3]{0:T(128)S(1)} %pad_add_fusion.place, bf16[512,512]{1,0:T(8,128)(2,1)S(1)} %get-tuple-element.43.own.cols.refs_0_, ...), custom_call_target="tpu_custom_call" | custom-call | flops 1073741824 | bytes 6291456 | tf_op jit(solution)/shard_map/pallas_call | solution.py:126
  56.6 3.5 %collective-permute-start.7 = (f16[2,8,72,256]{3,2,1,0:T(8,128)(2,1)S(1)}, f16[2,8,72,256]{3,2,1,0:T(8,128)(2,1)S(1)}, u32[]{:S(2)}, u32[]{:S(2)}) collective-permute-start(f16[2,8,72,256]{3,2,1,0:T(8,128)(2,1)S(1)} %convert_element_type.206), channel_id=1, source_target_pairs={{0,24},{1,9},{2,26},{3,11},{4,28},{5,13},{6,30},{7,15},{8,0},{9,17... | collective-permute-start | bytes 1769480 | tf_op jit(solution)/shard_map/ppermute | solution.py:32
  60.1 3.2 %collective-permute-start.10 = (bf16[512,512]{1,0:T(8,128)(2,1)S(1)}, bf16[512,512]{1,0:T(8,128)(2,1)S(1)}, u32[]{:S(2)}, u32[]{:S(2)}) collective-permute-start(bf16[512,512]{1,0:T(8,128)(2,1)S(1)} %pad_maximum_fusion.4.own.cols.refs_8_), channel_id=1, source_target_pairs={{0,6},{1,3},{2,0},{3,5},{4,2},{5,7},{6,4},{7,1},{8,14},{9,11},{10,... | collective-permute-start | bytes 1572872 | tf_op jit(solution)/shard_map/ppermute | solution.py:37
  63.4 3.8 %shard_map.51 = (f32[2,8,72,256]{3,2,1,0:T(8,128)S(1)}, f32[2,8,72,256]{3,2,1,0:T(8,128)S(1)}, f32[2,8,72,256]{3,2,1,0:T(8,128)S(1)}, f32[2,8,72,256]{3,2,1,0:T(8,128)S(1)}) custom-call(s32[3]{0:T(128)S(1)} %pad_add_fusion.place, bf16[512,512]{1,0:T(8,128)(2,1)S(1)} %get-tuple-element.44.own.cols.refs_4_, bf16[512,512]{1,0:T(8,128)(2,1)S(1)} %copy-done.11, ...), custom_call_target="tpu_custom_call" | custom-call | flops 1073741824 | bytes 6291456 | tf_op jit(solution)/shard_map/pallas_call | solution.py:126
  67.5 5.5 %collective-permute-done.6 = f16[2,8,72,256]{3,2,1,0:T(8,128)(2,1)S(1)} collective-permute-done((f16[2,8,72,256]{3,2,1,0:T(8,128)(2,1)S(1)}, f16[2,8,72,256]{3,2,1,0:T(8,128)(2,1)S(1)}, u32[]{:S(2)}, u32[]{:S(2)}) %collective-permute-start.6) | collective-permute-done | bytes 589856 | tf_op jit(solution)/shard_map/ppermute | solution.py:32
  73.2 1.7 collective-permute-done.9.behind.refs_9_
  75.6 9.8 %collective-permute-done.14.beyond.refs_10_ = bf16[512,512]{1,0:T(8,128)(2,1)S(1)} collective-permute-done((bf16[512,512]{1,0:T(8,128)(2,1)S(1)}, bf16[512,512]{1,0:T(8,128)(2,1)S(1)}, u32[]{:S(2)}, u32[]{:S(2)}) %collective-permute-start.14) | collective-permute-done | bytes 524320 | tf_op jit(solution)/shard_map/ppermute | solution.py:37
  85.4 2.6 %shard_map.52 = (f32[2,8,72,256]{3,2,1,0:T(8,128)S(1)}, f32[2,8,72,256]{3,2,1,0:T(8,128)S(1)}, f32[2,8,72,256]{3,2,1,0:T(8,128)S(1)}, f32[2,8,72,256]{3,2,1,0:T(8,128)S(1)}) custom-call(s32[3]{0:T(128)S(1)} %pad_add_fusion.place, bf16[512,512]{1,0:T(8,128)(2,1)S(1)} %pad_maximum_fusion.4.own.cols.refs_8_, ...), custom_call_target="tpu_custom_call" | custom-call | flops 1073741824 | bytes 6291456 | tf_op jit(solution)/shard_map/pallas_call | solution.py:126
  88.1 1.1 convert_element_type.234
  89.2 0.9 convert_element_type.235
  90.2 3.1 %collective-permute-start.17 = (f16[2,8,72,256]{3,2,1,0:T(8,128)(2,1)}, f16[2,8,72,256]{3,2,1,0:T(8,128)(2,1)S(1)}, u32[]{:S(2)}, u32[]{:S(2)}) collective-permute-start(f16[2,8,72,256]{3,2,1,0:T(8,128)(2,1)} %convert_element_type.235), channel_id=1, source_target_pairs={{0,24},{1,9},{2,26},{3,11},{4,28},{5,13},{6,30},{7,15},{8,0},{9,17... | collective-permute-start | bytes 1769480 | tf_op jit(solution)/shard_map/ppermute | solution.py:32
  93.4 1.1 select_convert_fusion.4
  94.6 1.3 select_convert_fusion.3
  95.9 8.9 %all-to-all-start = ((f16[16,72,256]{2,1,0:T(8,128)(2,1)}), f16[16,72,256]{2,1,0:T(8,128)(2,1)S(1)}, u32[]{:S(2)}, u32[]{:S(2)}) async-start(f16[16,72,256]{2,1,0:T(8,128)(2,1)} %bitcast.17), calls=%async_computation | async-start | bytes 1179648 | tf_op jit(solution)/shard_map/all_to_all | solution.py:306
  104.8 1.0 collective-permute-done.16
  105.8 1.6 collective-permute-done.17
  107.4 0.8 copy-done.20
  108.2 9.3 %shard_map.53 = (f32[3,512,256]{2,1,0:T(8,128)}, f32[3,512,256]{2,1,0:T(8,128)}, f32[72,256]{1,0:T(8,128)}) custom-call(s32[3]{0:T(128)} %copy-done.15, f32[2,3]{1,0:T(2,128)} %fusion.4.adagrad, bf16[512,512]{1,0:T(8,128)(2,1)} %copy-done.1, bf16[512,512]{1,0:T(8,128)(2,1)} %copy-done.8, bf16[512,512]{1,0:T(8,128)(2,1)} %collective-permute-done.5.beyond.refs_2_, ...), custom_call_target="tpu_custom_call" | custom-call | flops 3221225472 | bytes 15728640 | tf_op jit(solution)/shard_map/pallas_call | solution.py:208
  117.6 1.1 select_convert_fusion.2
  118.9 0.7 convert_multiply_fusion.6
  119.6 0.7 convert_multiply_fusion.5
  120.3 2.3 %select_convert_fusion.1 = f16[2,8,72,256]{3,2,1,0:T(8,128)(2,1)} fusion(f16[2,8,72,256]{3,2,1,0:T(8,128)(2,1)S(1)} %copy-done.22, f16[2,8,72,256]{3,2,1,0:T(8,128)(2,1)} %collective-permute-done.15, f32[2,8,72,256]{3,2,1,0:T(8,128)S(1)} %get-tuple-element.51, f32[2,256]{1,0:T(2,128)S(1)} %bitcast.171, f32[2,256]{1,0:T(2,128)S(1)} %bitcast.172, ...), kind=kLoop, calls=%fused_computation.11 | loop fusion | flops 2949120 | bytes 3031184 | tf_op jit(solution)/shard_map/convert_element_type | solution.py:155
  122.7 0.8 copy-done.18
  123.5 8.8 %all-to-all-start.1 = ((f16[16,72,256]{2,1,0:T(8,128)(2,1)}), f16[16,72,256]{2,1,0:T(8,128)(2,1)S(1)}, u32[]{:S(2)}, u32[]{:S(2)}) async-start(f16[16,72,256]{2,1,0:T(8,128)(2,1)} %bitcast.148), calls=%async_computation.1 | async-start | bytes 1179648 | tf_op jit(solution)/shard_map/all_to_all | solution.py:306
  132.3 0.9 slice.181
  133.4 1.2 multiply_reduce_fusion.2
  134.6 0.7 fusion.7
  135.3 0.7 convert_multiply_fusion.3
  136.0 0.7 convert_multiply_fusion.2
  136.8 2.5 %select_convert_fusion = f16[2,8,72,256]{3,2,1,0:T(8,128)(2,1)} fusion(f16[2,8,72,256]{3,2,1,0:T(8,128)(2,1)} %copy-done.20, f16[2,8,72,256]{3,2,1,0:T(8,128)(2,1)} %collective-permute-done.21, f32[2,8,72,256]{3,2,1,0:T(8,128)S(1)} %copy-done.5, f32[2,256]{1,0:T(2,128)S(1)} %bitcast.155, f32[2,256]{1,0:T(2,128)S(1)} %bitcast.157, f32[2,256]{1,0:T(2,128)S(1)} %bitcast.162, ...), kind=kLoop, calls=%fused_computation.8 | loop fusion | flops 2654208 | bytes 2957384 | tf_op jit(solution)/shard_map/convert_element_type | solution.py:155
  139.3 10.7 %all-to-all-done.1 = f16[16,72,256]{2,1,0:T(8,128)(2,1)S(1)} async-done(((f16[16,72,256]{2,1,0:T(8,128)(2,1)}), f16[16,72,256]{2,1,0:T(8,128)(2,1)S(1)}, u32[]{:S(2)}, u32[]{:S(2)}) %all-to-all-start.1) | async-done | bytes 589856 | tf_op jit(solution)/shard_map/all_to_all | solution.py:306
  150.0 0.8 copy-done.17
  150.8 4.3 %all-to-all-start.2 = ((f16[16,72,256]{2,1,0:T(8,128)(2,1)}), f16[16,72,256]{2,1,0:T(8,128)(2,1)}, u32[]{:S(2)}, u32[]{:S(2)}) async-start(f16[16,72,256]{2,1,0:T(8,128)(2,1)} %bitcast.147), calls=%async_computation.2 | async-start | bytes 1179648 | tf_op jit(solution)/shard_map/all_to_all | solution.py:306
  155.1 0.9 slice_convert_fusion
  156.0 0.9 slice.183
  156.9 1.8 collective-permute-start.22
  158.8 3.4 %collective-permute-done.22 = f32[2,256]{1,0:T(2,128)S(1)} collective-permute-done((f32[2,256]{1,0:T(2,128)S(1)}, f32[2,256]{1,0:T(2,128)S(1)}, u32[]{:S(2)}, u32[]{:S(2)}) %collective-permute-start.22) | collective-permute-done | bytes 2080 | tf_op jit(solution)/shard_map/ppermute | solution.py:32
  162.2 3.5 %collective-permute-start.23 = (f32[2,256]{1,0:T(2,128)S(1)}, f32[2,256]{1,0:T(2,128)S(1)}, u32[]{:S(2)}, u32[]{:S(2)}) collective-permute-start(f32[2,256]{1,0:T(2,128)S(1)} %add.164), channel_id=1, source_target_pairs={{0,16},{1,17},{2,18},{3,19},{4,20},{5,21},{6,22},{7,23},{8,24},{9,... | collective-permute-start | bytes 6152 | tf_op jit(solution)/shard_map/ppermute | solution.py:32
  165.6 1.2 multiply_reduce_fusion.1
  167.2 2.5 %collective-permute-start.26 = (f32[2,256]{1,0:T(2,128)S(1)}, f32[2,256]{1,0:T(2,128)S(1)}, u32[]{:S(2)}, u32[]{:S(2)}) collective-permute-start(f32[2,256]{1,0:T(2,128)S(1)} %add.165), channel_id=1, source_target_pairs={{0,4},{1,5},{2,6},{3,7},{4,0},{5,1},{6,2},{7,3},{8,12},{9,13},{10,... | collective-permute-start | bytes 6152 | tf_op jit(solution)/shard_map/ppermute | solution.py:37
  169.8 0.5 collective-permute-start.25
  170.3 1.5 collective-permute-start.24
  171.8 0.5 collective-permute-done.26
  172.3 1.0 collective-permute-done.25
  173.4 1.8 collective-permute-done.24
  175.4 2.7 %shard_map.54 = f32[2,3,512,256]{3,2,1,0:T(8,128)} custom-call(s32[3]{0:T(128)S(1)} %copy-done.16, f32[2,3]{1,0:T(2,128)S(1)} %fusion.12.scale, f32[3,512,256]{2,1,0:T(8,128)S(1)} %copy-done.3, f32[3,512,256]{2,1,0:T(8,128)S(1)} %collective-permute-done.27.given), custom_call_target="tpu_custom_call" | custom-call | flops 786432 | bytes 6291456 | tf_op jit(solution)/shard_map/pallas_call | solution.py:236
  178.1 0.9 slice.185
  178.9 1.2 multiply_reduce_fusion
  180.2 0.8 pad_maximum_fusion.5
  (141 shorter events, 3.9 us)
Async XLA Ops:
  7.2 100.2 %all-gather.3.cloned.1.call-start = ((), (), s32[]{:S(2)}) async-start(), calls=%async_computation.3 | async-start | bytes 7077888 | tf_op jit(solution)/shard_map/all_gather | solution.py:281
  7.2 1.5 copy-start.19
  8.8 2.5 %collective-permute-start = (bf16[3,576,256]{2,1,0:T(8,128)(2,1)S(1)}, bf16[3,576,256]{2,1,0:T(8,128)(2,1)S(1)}, u32[]{:S(2)}, u32[]{:S(2)}) collective-permute-start(bf16[3,576,256]{2,1,0:T(8,128)(2,1)S(1)} %pad_maximum_fusion), channel_id=1, source_target_pairs={{0,1},{1,0},{2,3},{3,2},{4,5},{5,4},{6,7},{7,6},{8,9},{9,8},{10,11... | collective-permute-start | bytes 2654216 | tf_op jit(solution)/shard_map/ppermute | solution.py:58
  11.5 73.9 %copy-start = (bf16[512,512]{1,0:T(8,128)(2,1)}, bf16[512,512]{1,0:T(8,128)(2,1)S(1)}, u32[]{:S(2)}) copy-start(bf16[512,512]{1,0:T(8,128)(2,1)S(1)} %pad_maximum_fusion.4.own.cols.refs_8_) | copy-start | bytes 1572868
  11.7 40.9 %copy-start.1 = (bf16[512,512]{1,0:T(8,128)(2,1)}, bf16[512,512]{1,0:T(8,128)(2,1)S(1)}, u32[]{:S(2)}) copy-start(bf16[512,512]{1,0:T(8,128)(2,1)S(1)} %get-tuple-element.43.own.cols.refs_0_) | copy-start | bytes 1572868
  11.7 51.6 %copy-start.2 = (bf16[512,512]{1,0:T(8,128)(2,1)}, bf16[512,512]{1,0:T(8,128)(2,1)S(1)}, u32[]{:S(2)}) copy-start(bf16[512,512]{1,0:T(8,128)(2,1)S(1)} %get-tuple-element.44.own.cols.refs_4_) | copy-start | bytes 1572868
  11.7 18.0 %collective-permute-start.1 = (bf16[512,512]{1,0:T(8,128)(2,1)S(1)}, bf16[512,512]{1,0:T(8,128)(2,1)S(1)}, u32[]{:S(2)}, u32[]{:S(2)}) collective-permute-start(bf16[512,512]{1,0:T(8,128)(2,1)S(1)} %get-tuple-element.43.own.cols.refs_0_), channel_id=1, source_target_pairs={{0,2},{1,7},{2,4},{3,1},{4,6},{5,3},{6,0},{7,5},{8,10},{9,15},{10,... | collective-permute-start | bytes 1572872 | tf_op jit(solution)/shard_map/ppermute | solution.py:37
  13.4 16.3 %collective-permute-start.2 = (bf16[512,512]{1,0:T(8,128)(2,1)S(1)}, bf16[512,512]{1,0:T(8,128)(2,1)S(1)}, u32[]{:S(2)}, u32[]{:S(2)}) collective-permute-start(bf16[512,512]{1,0:T(8,128)(2,1)S(1)} %get-tuple-element.43.own.cols.refs_0_), channel_id=1, source_target_pairs={{0,6},{1,3},{2,0},{3,5},{4,2},{5,7},{6,4},{7,1},{8,14},{9,11},{10,... | collective-permute-start | bytes 1572872 | tf_op jit(solution)/shard_map/ppermute | solution.py:37
  15.0 11.0 %collective-permute-start.18 = (bf16[3,64,512]{2,1,0:T(8,128)(2,1)S(1)}, bf16[3,64,512]{2,1,0:T(8,128)(2,1)S(1)}, u32[]{:S(2)}, u32[]{:S(2)}) collective-permute-start(bf16[3,64,512]{2,1,0:T(8,128)(2,1)S(1)} %pad_maximum_fusion.6), channel_id=1, source_target_pairs={{0,24},{8,0},{16,8},{24,16},{32,56},{40,32},{48,40},{56,48},{64,88... | collective-permute-start | bytes 589832 | tf_op jit(solution)/shard_map/ppermute | solution.py:42
  17.8 9.4 %collective-permute-start.19 = (bf16[3,64,512]{2,1,0:T(8,128)(2,1)S(1)}, bf16[3,64,512]{2,1,0:T(8,128)(2,1)S(1)}, u32[]{:S(2)}, u32[]{:S(2)}) collective-permute-start(bf16[3,64,512]{2,1,0:T(8,128)(2,1)S(1)} %pad_maximum_fusion.6), channel_id=1, source_target_pairs={{0,16},{8,24},{16,0},{24,8},{32,48},{40,56},{48,32},{56,40},{64,80... | collective-permute-start | bytes 589832 | tf_op jit(solution)/shard_map/ppermute | solution.py:42
  18.6 11.1 %collective-permute-start.20 = (bf16[3,64,512]{2,1,0:T(8,128)(2,1)S(1)}, bf16[3,64,512]{2,1,0:T(8,128)(2,1)S(1)}, u32[]{:S(2)}, u32[]{:S(2)}) collective-permute-start(bf16[3,64,512]{2,1,0:T(8,128)(2,1)S(1)} %pad_maximum_fusion.6), channel_id=1, source_target_pairs={{0,8},{8,16},{16,24},{24,0},{32,40},{40,48},{48,56},{56,32},{64,72... | collective-permute-start | bytes 589832 | tf_op jit(solution)/shard_map/ppermute | solution.py:42
  29.7 22.9 %copy-start.8 = (bf16[512,512]{1,0:T(8,128)(2,1)}, bf16[512,512]{1,0:T(8,128)(2,1)S(1)}, u32[]{:S(2)}) copy-start(bf16[512,512]{1,0:T(8,128)(2,1)S(1)} %collective-permute-done.1.behind.refs_1_) | copy-start | bytes 1572868
  29.7 22.9 %copy-start.9 = (bf16[512,512]{1,0:T(8,128)(2,1)}, bf16[512,512]{1,0:T(8,128)(2,1)S(1)}, u32[]{:S(2)}) copy-start(bf16[512,512]{1,0:T(8,128)(2,1)S(1)} %collective-permute-done.2.ahead.refs_3_) | copy-start | bytes 1572868
  30.8 14.3 %collective-permute-start.3 = (bf16[512,512]{1,0:T(8,128)(2,1)S(1)}, bf16[512,512]{1,0:T(8,128)(2,1)S(1)}, u32[]{:S(2)}, u32[]{:S(2)}) collective-permute-start(bf16[512,512]{1,0:T(8,128)(2,1)S(1)} %get-tuple-element.44.own.cols.refs_4_), channel_id=1, source_target_pairs={{0,2},{1,7},{2,4},{3,1},{4,6},{5,3},{6,0},{7,5},{8,10},{9,15},{10,... | collective-permute-start | bytes 1572872 | tf_op jit(solution)/shard_map/ppermute | solution.py:37
  31.2 18.7 %collective-permute-start.4 = (bf16[512,512]{1,0:T(8,128)(2,1)S(1)}, bf16[512,512]{1,0:T(8,128)(2,1)}, u32[]{:S(2)}, u32[]{:S(2)}) collective-permute-start(bf16[512,512]{1,0:T(8,128)(2,1)S(1)} %get-tuple-element.44.own.cols.refs_4_), channel_id=1, source_target_pairs={{0,6},{1,3},{2,0},{3,5},{4,2},{5,7},{6,4},{7,1},{8,14},{9,11},{10,... | collective-permute-start | bytes 1572872 | tf_op jit(solution)/shard_map/ppermute | solution.py:37
  34.1 18.5 %collective-permute-start.5 = (bf16[512,512]{1,0:T(8,128)(2,1)S(1)}, bf16[512,512]{1,0:T(8,128)(2,1)}, u32[]{:S(2)}, u32[]{:S(2)}) collective-permute-start(bf16[512,512]{1,0:T(8,128)(2,1)S(1)} %collective-permute-done.1.behind.refs_1_), channel_id=1, source_target_pairs={{0,2},{1,7},{2,4},{3,1},{4,6},{5,3},{6,0},{7,5},{8,10},{9,15},{10,... | collective-permute-start | bytes 1572872 | tf_op jit(solution)/shard_map/ppermute | solution.py:37
  45.1 4.8 %copy-start.10 = (bf16[512,512]{1,0:T(8,128)(2,1)}, bf16[512,512]{1,0:T(8,128)(2,1)S(1)}, u32[]{:S(2)}) copy-start(bf16[512,512]{1,0:T(8,128)(2,1)S(1)} %collective-permute-done.3.behind.refs_5_) | copy-start | bytes 1572868
  45.1 15.0 %collective-permute-start.8 = (bf16[512,512]{1,0:T(8,128)(2,1)S(1)}, bf16[512,512]{1,0:T(8,128)(2,1)}, u32[]{:S(2)}, u32[]{:S(2)}) collective-permute-start(bf16[512,512]{1,0:T(8,128)(2,1)S(1)} %collective-permute-done.3.behind.refs_5_), channel_id=1, source_target_pairs={{0,2},{1,7},{2,4},{3,1},{4,6},{5,3},{6,0},{7,5},{8,10},{9,15},{10,... | collective-permute-start | bytes 1572872 | tf_op jit(solution)/shard_map/ppermute | solution.py:37
  49.9 35.5 %copy-start.15 = (s32[3]{0:T(128)}, s32[3]{0:T(128)S(1)}, u32[]{:S(2)}) copy-start(s32[3]{0:T(128)S(1)} %pad_add_fusion.place) | copy-start | bytes 40
  56.4 6.9 %copy-start.11 = (bf16[512,512]{1,0:T(8,128)(2,1)S(1)}, bf16[512,512]{1,0:T(8,128)(2,1)}, u32[]{:S(2)}) copy-start(bf16[512,512]{1,0:T(8,128)(2,1)} %copy-done.10) | copy-start | bytes 1572868
  56.4 16.6 %collective-permute-start.6 = (f16[2,8,72,256]{3,2,1,0:T(8,128)(2,1)S(1)}, f16[2,8,72,256]{3,2,1,0:T(8,128)(2,1)S(1)}, u32[]{:S(2)}, u32[]{:S(2)}) collective-permute-start(f16[2,8,72,256]{3,2,1,0:T(8,128)(2,1)S(1)} %convert_element_type.205), channel_id=1, source_target_pairs={{0,8},{1,25},{2,10},{3,27},{4,12},{5,29},{6,14},{7,31},{8,16},{9,1... | collective-permute-start | bytes 1769480 | tf_op jit(solution)/shard_map/ppermute | solution.py:32
  56.6 16.6 %collective-permute-start.7 = (f16[2,8,72,256]{3,2,1,0:T(8,128)(2,1)S(1)}, f16[2,8,72,256]{3,2,1,0:T(8,128)(2,1)S(1)}, u32[]{:S(2)}, u32[]{:S(2)}) collective-permute-start(f16[2,8,72,256]{3,2,1,0:T(8,128)(2,1)S(1)} %convert_element_type.206), channel_id=1, source_target_pairs={{0,24},{1,9},{2,26},{3,11},{4,28},{5,13},{6,30},{7,15},{8,0},{9,17... | collective-permute-start | bytes 1769480 | tf_op jit(solution)/shard_map/ppermute | solution.py:32
  60.1 14.8 %collective-permute-start.9 = (bf16[512,512]{1,0:T(8,128)(2,1)S(1)}, bf16[512,512]{1,0:T(8,128)(2,1)S(1)}, u32[]{:S(2)}, u32[]{:S(2)}) collective-permute-start(bf16[512,512]{1,0:T(8,128)(2,1)S(1)} %pad_maximum_fusion.4.own.cols.refs_8_), channel_id=1, source_target_pairs={{0,2},{1,7},{2,4},{3,1},{4,6},{5,3},{6,0},{7,5},{8,10},{9,15},{10,... | collective-permute-start | bytes 1572872 | tf_op jit(solution)/shard_map/ppermute | solution.py:37
  60.1 14.8 %collective-permute-start.10 = (bf16[512,512]{1,0:T(8,128)(2,1)S(1)}, bf16[512,512]{1,0:T(8,128)(2,1)S(1)}, u32[]{:S(2)}, u32[]{:S(2)}) collective-permute-start(bf16[512,512]{1,0:T(8,128)(2,1)S(1)} %pad_maximum_fusion.4.own.cols.refs_8_), channel_id=1, source_target_pairs={{0,6},{1,3},{2,0},{3,5},{4,2},{5,7},{6,4},{7,1},{8,14},{9,11},{10,... | collective-permute-start | bytes 1572872 | tf_op jit(solution)/shard_map/ppermute | solution.py:37
  67.3 26.0 %collective-permute-start.12 = (f16[2,8,72,256]{3,2,1,0:T(8,128)(2,1)S(1)}, f16[2,8,72,256]{3,2,1,0:T(8,128)(2,1)S(1)}, u32[]{:S(2)}, u32[]{:S(2)}) collective-permute-start(f16[2,8,72,256]{3,2,1,0:T(8,128)(2,1)S(1)} %convert_element_type.214), channel_id=1, source_target_pairs={{0,8},{1,25},{2,10},{3,27},{4,12},{5,29},{6,14},{7,31},{8,16},{9,1... | collective-permute-start | bytes 1769480 | tf_op jit(solution)/shard_map/ppermute | solution.py:32
  73.0 20.3 %collective-permute-start.13 = (f16[2,8,72,256]{3,2,1,0:T(8,128)(2,1)S(1)}, f16[2,8,72,256]{3,2,1,0:T(8,128)(2,1)S(1)}, u32[]{:S(2)}, u32[]{:S(2)}) collective-permute-start(f16[2,8,72,256]{3,2,1,0:T(8,128)(2,1)S(1)} %convert_element_type.215), channel_id=1, source_target_pairs={{0,24},{1,9},{2,26},{3,11},{4,28},{5,13},{6,30},{7,15},{8,0},{9,17... | collective-permute-start | bytes 1769480 | tf_op jit(solution)/shard_map/ppermute | solution.py:32
  74.9 10.5 %copy-start.12 = (bf16[512,512]{1,0:T(8,128)(2,1)}, bf16[512,512]{1,0:T(8,128)(2,1)S(1)}, u32[]{:S(2)}) copy-start(bf16[512,512]{1,0:T(8,128)(2,1)S(1)} %collective-permute-done.9.behind.refs_9_) | copy-start | bytes 1572868
  74.9 10.5 %copy-start.13 = (bf16[512,512]{1,0:T(8,128)(2,1)}, bf16[512,512]{1,0:T(8,128)(2,1)S(1)}, u32[]{:S(2)}) copy-start(bf16[512,512]{1,0:T(8,128)(2,1)S(1)} %collective-permute-done.10.ahead.refs_11_) | copy-start | bytes 1572868
  74.9 10.5 %collective-permute-start.14 = (bf16[512,512]{1,0:T(8,128)(2,1)S(1)}, bf16[512,512]{1,0:T(8,128)(2,1)S(1)}, u32[]{:S(2)}, u32[]{:S(2)}) collective-permute-start(bf16[512,512]{1,0:T(8,128)(2,1)S(1)} %collective-permute-done.9.behind.refs_9_), channel_id=1, source_target_pairs={{0,2},{1,7},{2,4},{3,1},{4,6},{5,3},{6,0},{7,5},{8,10},{9,15},{10,... | collective-permute-start | bytes 1572872 | tf_op jit(solution)/shard_map/ppermute | solution.py:37
  75.4 19.1 %collective-permute-start.11 = (f16[2,8,72,256]{3,2,1,0:T(8,128)(2,1)S(1)}, f16[2,8,72,256]{3,2,1,0:T(8,128)(2,1)S(1)}, u32[]{:S(2)}, u32[]{:S(2)}) collective-permute-start(f16[2,8,72,256]{3,2,1,0:T(8,128)(2,1)S(1)} %select_convert_fusion.5), channel_id=1, source_target_pairs={{0,8},{1,25},{2,10},{3,27},{4,12},{5,29},{6,14},{7,31},{8,16},{9,1... | collective-permute-start | bytes 1769480 | tf_op jit(solution)/shard_map/ppermute | solution.py:32
  85.4 2.6 %copy-start.14 = (bf16[512,512]{1,0:T(8,128)(2,1)}, bf16[512,512]{1,0:T(8,128)(2,1)S(1)}, u32[]{:S(2)}) copy-start(bf16[512,512]{1,0:T(8,128)(2,1)S(1)} %collective-permute-done.14.beyond.refs_10_) | copy-start | bytes 1572868
  88.0 2.1 %copy-start.4 = (f32[2,8,72,256]{3,2,1,0:T(8,128)}, f32[2,8,72,256]{3,2,1,0:T(8,128)S(1)}, u32[]{:S(2)}) copy-start(f32[2,8,72,256]{3,2,1,0:T(8,128)S(1)} %get-tuple-element.59) | copy-start | bytes 3538948
  88.1 2.1 %copy-start.6 = (f32[2,8,72,256]{3,2,1,0:T(8,128)}, f32[2,8,72,256]{3,2,1,0:T(8,128)S(1)}, u32[]{:S(2)}) copy-start(f32[2,8,72,256]{3,2,1,0:T(8,128)S(1)} %get-tuple-element.63) | copy-start | bytes 3538948
  89.1 16.7 %collective-permute-start.16 = (f16[2,8,72,256]{3,2,1,0:T(8,128)(2,1)}, f16[2,8,72,256]{3,2,1,0:T(8,128)(2,1)S(1)}, u32[]{:S(2)}, u32[]{:S(2)}) collective-permute-start(f16[2,8,72,256]{3,2,1,0:T(8,128)(2,1)} %convert_element_type.234), channel_id=1, source_target_pairs={{0,8},{1,25},{2,10},{3,27},{4,12},{5,29},{6,14},{7,31},{8,16},{9,1... | collective-permute-start | bytes 1769480 | tf_op jit(solution)/shard_map/ppermute | solution.py:32
  90.2 17.2 %collective-permute-start.17 = (f16[2,8,72,256]{3,2,1,0:T(8,128)(2,1)}, f16[2,8,72,256]{3,2,1,0:T(8,128)(2,1)S(1)}, u32[]{:S(2)}, u32[]{:S(2)}) collective-permute-start(f16[2,8,72,256]{3,2,1,0:T(8,128)(2,1)} %convert_element_type.235), channel_id=1, source_target_pairs={{0,24},{1,9},{2,26},{3,11},{4,28},{5,13},{6,30},{7,15},{8,0},{9,17... | collective-permute-start | bytes 1769480 | tf_op jit(solution)/shard_map/ppermute | solution.py:32
  93.3 1.2 copy-start.21
  94.5 24.3 %collective-permute-start.15 = (f16[2,8,72,256]{3,2,1,0:T(8,128)(2,1)}, f16[2,8,72,256]{3,2,1,0:T(8,128)(2,1)}, u32[]{:S(2)}, u32[]{:S(2)}) collective-permute-start(f16[2,8,72,256]{3,2,1,0:T(8,128)(2,1)} %select_convert_fusion.4), channel_id=1, source_target_pairs={{0,8},{1,25},{2,10},{3,27},{4,12},{5,29},{6,14},{7,31},{8,16},{9,1... | collective-permute-start | bytes 1769480 | tf_op jit(solution)/shard_map/ppermute | solution.py:32
  95.9 26.8 %all-to-all-start = ((f16[16,72,256]{2,1,0:T(8,128)(2,1)}), f16[16,72,256]{2,1,0:T(8,128)(2,1)S(1)}, u32[]{:S(2)}, u32[]{:S(2)}) async-start(f16[16,72,256]{2,1,0:T(8,128)(2,1)} %bitcast.17), calls=%async_computation | async-start | bytes 1179648 | tf_op jit(solution)/shard_map/all_to_all | solution.py:306
  105.8 1.6 copy-start.23
  107.4 0.8 copy-start.20
  108.2 9.3 %copy-start.7 = (f32[2,8,72,256]{3,2,1,0:T(8,128)S(1)}, f32[2,8,72,256]{3,2,1,0:T(8,128)}, u32[]{:S(2)}) copy-start(f32[2,8,72,256]{3,2,1,0:T(8,128)} %copy-done.6) | copy-start | bytes 3538948
  108.2 9.3 %copy-start.24 = (f16[2,8,72,256]{3,2,1,0:T(8,128)(2,1)S(1)}, f16[2,8,72,256]{3,2,1,0:T(8,128)(2,1)}, u32[]{:S(2)}) copy-start(f16[2,8,72,256]{3,2,1,0:T(8,128)(2,1)} %copy-done.23) | copy-start | bytes 1769476
  117.6 1.2 copy-start.22
  117.6 2.7 %copy-start.26 = (f32[72,256]{1,0:T(8,128)S(1)}, f32[72,256]{1,0:T(8,128)}, u32[]{:S(2)}) copy-start(f32[72,256]{1,0:T(8,128)} %get-tuple-element.72) | copy-start | bytes 221188
  118.7 16.5 %collective-permute-start.21 = (f16[2,8,72,256]{3,2,1,0:T(8,128)(2,1)}, f16[2,8,72,256]{3,2,1,0:T(8,128)(2,1)}, u32[]{:S(2)}, u32[]{:S(2)}) collective-permute-start(f16[2,8,72,256]{3,2,1,0:T(8,128)(2,1)} %select_convert_fusion.2), channel_id=1, source_target_pairs={{0,8},{1,25},{2,10},{3,27},{4,12},{5,29},{6,14},{7,31},{8,16},{9,1... | collective-permute-start | bytes 1769480 | tf_op jit(solution)/shard_map/ppermute | solution.py:32
  122.7 12.6 %copy-start.5 = (f32[2,8,72,256]{3,2,1,0:T(8,128)S(1)}, f32[2,8,72,256]{3,2,1,0:T(8,128)}, u32[]{:S(2)}) copy-start(f32[2,8,72,256]{3,2,1,0:T(8,128)} %copy-done.4) | copy-start | bytes 3538948
  122.7 0.8 copy-start.18
  123.5 26.5 %all-to-all-start.1 = ((f16[16,72,256]{2,1,0:T(8,128)(2,1)}), f16[16,72,256]{2,1,0:T(8,128)(2,1)S(1)}, u32[]{:S(2)}, u32[]{:S(2)}) async-start(f16[16,72,256]{2,1,0:T(8,128)(2,1)} %bitcast.148), calls=%async_computation.1 | async-start | bytes 1179648 | tf_op jit(solution)/shard_map/all_to_all | solution.py:306
  133.2 42.2 %collective-permute-start.27 = (f32[3,512,256]{2,1,0:T(8,128)}, f32[3,512,256]{2,1,0:T(8,128)S(1)}, u32[]{:S(2)}, u32[]{:S(2)}) collective-permute-start(f32[3,512,256]{2,1,0:T(8,128)} %get-tuple-element.81), channel_id=1, source_target_pairs={{0,1},{1,0},{2,3},{3,2},{4,5},{5,4},{6,7},{7,6},{8,9},{9,8},{10,11... | collective-permute-start | bytes 4718600 | tf_op jit(solution)/shard_map/ppermute | solution.py:58
  150.0 0.8 copy-start.17
  150.8 24.5 %copy-start.3 = (f32[3,512,256]{2,1,0:T(8,128)S(1)}, f32[3,512,256]{2,1,0:T(8,128)}, u32[]{:S(2)}) copy-start(f32[3,512,256]{2,1,0:T(8,128)} %get-tuple-element.80.kept) | copy-start | bytes 4718596
  150.8 24.5 %copy-start.16 = (s32[3]{0:T(128)S(1)}, s32[3]{0:T(128)}, u32[]{:S(2)}) copy-start(s32[3]{0:T(128)} %copy-done.15) | copy-start | bytes 40
  150.8 27.2 %all-to-all-start.2 = ((f16[16,72,256]{2,1,0:T(8,128)(2,1)}), f16[16,72,256]{2,1,0:T(8,128)(2,1)}, u32[]{:S(2)}, u32[]{:S(2)}) async-start(f16[16,72,256]{2,1,0:T(8,128)(2,1)} %bitcast.147), calls=%async_computation.2 | async-start | bytes 1179648 | tf_op jit(solution)/shard_map/all_to_all | solution.py:306
  156.9 5.2 %collective-permute-start.22 = (f32[2,256]{1,0:T(2,128)S(1)}, f32[2,256]{1,0:T(2,128)S(1)}, u32[]{:S(2)}, u32[]{:S(2)}) collective-permute-start(f32[2,256]{1,0:T(2,128)S(1)} %bitcast_reduce_fusion), channel_id=1, source_target_pairs={{0,8},{1,25},{2,10},{3,27},{4,12},{5,29},{6,14},{7,31},{8,16},{9,1... | collective-permute-start | bytes 6152 | tf_op jit(solution)/shard_map/ppermute | solution.py:32
  162.2 5.1 %collective-permute-start.23 = (f32[2,256]{1,0:T(2,128)S(1)}, f32[2,256]{1,0:T(2,128)S(1)}, u32[]{:S(2)}, u32[]{:S(2)}) collective-permute-start(f32[2,256]{1,0:T(2,128)S(1)} %add.164), channel_id=1, source_target_pairs={{0,16},{1,17},{2,18},{3,19},{4,20},{5,21},{6,22},{7,23},{8,24},{9,... | collective-permute-start | bytes 6152 | tf_op jit(solution)/shard_map/ppermute | solution.py:32
  167.2 5.1 %collective-permute-start.26 = (f32[2,256]{1,0:T(2,128)S(1)}, f32[2,256]{1,0:T(2,128)S(1)}, u32[]{:S(2)}, u32[]{:S(2)}) collective-permute-start(f32[2,256]{1,0:T(2,128)S(1)} %add.165), channel_id=1, source_target_pairs={{0,4},{1,5},{2,6},{3,7},{4,0},{5,1},{6,2},{7,3},{8,12},{9,13},{10,... | collective-permute-start | bytes 6152 | tf_op jit(solution)/shard_map/ppermute | solution.py:37
  169.8 3.6 %collective-permute-start.25 = (f32[2,256]{1,0:T(2,128)S(1)}, f32[2,256]{1,0:T(2,128)S(1)}, u32[]{:S(2)}, u32[]{:S(2)}) collective-permute-start(f32[2,256]{1,0:T(2,128)S(1)} %add.165), channel_id=1, source_target_pairs={{0,6},{1,3},{2,0},{3,5},{4,2},{5,7},{6,4},{7,1},{8,14},{9,11},{10,... | collective-permute-start | bytes 6152 | tf_op jit(solution)/shard_map/ppermute | solution.py:37
  170.3 4.8 %collective-permute-start.24 = (f32[2,256]{1,0:T(2,128)S(1)}, f32[2,256]{1,0:T(2,128)S(1)}, u32[]{:S(2)}, u32[]{:S(2)}) collective-permute-start(f32[2,256]{1,0:T(2,128)S(1)} %add.165), channel_id=1, source_target_pairs={{0,2},{1,7},{2,4},{3,1},{4,6},{5,3},{6,0},{7,5},{8,10},{9,15},{10,... | collective-permute-start | bytes 6152 | tf_op jit(solution)/shard_map/ppermute | solution.py:37
  175.3 4.8 %copy-start.25 = (f32[2,1,64,256]{3,2,1,0:T(8,128)S(1)}, f32[2,1,64,256]{3,2,1,0:T(8,128)}, u32[]{:S(2)}) copy-start(f32[2,1,64,256]{3,2,1,0:T(8,128)} %fusion.7) | copy-start | bytes 393220
Sparse Core Ops, SparseCore 0:
  30.9 72.8 all-gather.2
